TPU v7x, 512 devices: a whole 4x8x8 slice. The times are simulated.
512 devices in a mesh: dp: 16 (over x, y_lo), ctx: 32 (over y_hi, z, core).
Axes of the slice: x: 4, y: 8 (y_hi: 2, y_lo: 4; y = y_hi * 4 + y_lo), z: 8, core: 2. Of those that a mesh axis runs over, the one named last changes fastest.
Arguments:
- query: bfloat16 [16, 4096, 4096], P('dp', 'ctx'), may hold values from -5 to 5
- keys: bfloat16 [16, 4096, 512], P('dp', 'ctx'), may hold values from -5 to 5
- values: bfloat16 [16, 4096, 512], P('dp', 'ctx'), may hold values from -6 to 6
- out_grad: bfloat16 [16, 4096, 4096], P('dp', 'ctx'), may hold values from -16 to 16
- query_lowrank_state: bfloat16 [16, 4096, 8], P('dp', 'ctx'), may hold values from -0.0625 to 0.0625
- value_lowrank_state: bfloat16 [16, 4096, 8], P('dp', 'ctx'), may hold values from -0.0625 to 0.0625
- shift_flags: int32 [4], replicated, may hold values from 0 to 1, as said below
Outputs:
- query_gradient: bfloat16 [16, 4096, 4096], P('dp', 'ctx')
- key_gradient: bfloat16 [16, 4096, 512], P('dp', 'ctx')
- value_gradient: bfloat16 [16, 4096, 512], P('dp', 'ctx')
- query_adapter_gradient: float32 [8, 4096], replicated
- value_adapter_gradient: float32 [8, 512], replicated
Inputs may be any that keep to these rules, and one draw needn't show every extreme that they name: `shift_flags`: exactly half of the 4 entries are 1, the others 0.
All inputs are finite; a program needn't handle non-finite values.
Results may differ from a plain program's by a relative error of at most 0.012.
Values may be sent and summed in bfloat16 or wider, within the bound.
No kernel may reach another device: no remote copies, remote signals or barrier semaphores. Data moves between devices by JAX's collectives and lax.ppermute only.
A program may use at most 64 MiB of HBM per device.

v0:
```python
from functools import partial
import math

import jax
import jax.numpy as jnp
from jax import lax
from jax.sharding import PartitionSpec as P

QUERY_HEADS_HALF = 32
KEY_VALUE_HEADS = 4
HEAD_WIDTH = 128
GROUP_DEV = 8


ADAPTER_SCALE = 2.0


def shifted(array, axis, by):
    count = lax.axis_size(axis)
    return lax.ppermute(array, axis, [(i, (i + by) % count) for i in range(count)])


def from_behind(array, axis, by):
    count = lax.axis_size(axis)
    pairs = [(i, i + by) for i in range(count) if 0 <= i + by < count]
    return lax.ppermute(array, axis, pairs)


def rope_back(gradient, positions):
    half_dim = gradient.shape[-1] // 2
    inv_freq = 10000.0 ** (-(jnp.arange(half_dim, dtype=jnp.float32) * 2.0) / gradient.shape[-1])
    angles = positions.astype(jnp.float32)[:, None] * inv_freq[None, :]
    table_shape = (angles.shape[0],) + (1,) * (gradient.ndim - 2) + (half_dim,)
    cosine = jnp.cos(angles).reshape(table_shape)
    sine_table = jnp.sin(angles).reshape(table_shape)
    front_half = gradient[..., :half_dim]
    back_half = gradient[..., half_dim:]
    return jnp.concatenate(
        [
            front_half * cosine + back_half * sine_table,
            back_half * cosine - front_half * sine_table,
        ],
        axis=-1,
    )


def split_heads(tensor, tok_rows, per_head, head_order):
    shaped = tensor[0].reshape((tok_rows, KEY_VALUE_HEADS) + per_head)
    return jnp.take(shaped, head_order, axis=1)


def keep_state(state_in):
    return state_in


def local(query, keys, values, out_grad, query_lowrank_state, value_lowrank_state, shift_flags):
    tok_rows = query.shape[1]
    per_group = QUERY_HEADS_HALF // KEY_VALUE_HEADS
    half_kv = KEY_VALUE_HEADS // 2
    kv_width = KEY_VALUE_HEADS * HEAD_WIDTH
    score_scale = 1.0 / math.sqrt(HEAD_WIDTH)
    ctx_index = lax.axis_index("ctx")
    ctx_count = lax.axis_size("ctx")
    offset_dev = GROUP_DEV // 2
    head_order = jnp.argsort(shift_flags, stable=True)
    undo_order = jnp.argsort(head_order, stable=True)
    q_heads = jnp.transpose(
        split_heads(query, tok_rows, (per_group, HEAD_WIDTH), head_order), (1, 2, 0, 3)
    )
    d_heads = jnp.transpose(
        split_heads(out_grad, tok_rows, (per_group, HEAD_WIDTH), head_order), (1, 2, 0, 3)
    )
    k_heads = jnp.transpose(split_heads(keys, tok_rows, (HEAD_WIDTH,), head_order), (1, 0, 2))
    v_heads = jnp.transpose(split_heads(values, tok_rows, (HEAD_WIDTH,), head_order), (1, 0, 2))
    local_pos = jnp.arange(tok_rows, dtype=jnp.int32)
    own_pos = ctx_index * tok_rows + local_pos
    own_slot = ctx_index % GROUP_DEV
    moved_heads = shifted(
        (q_heads[half_kv:], d_heads[half_kv:], k_heads[half_kv:], v_heads[half_kv:]),
        "ctx",
        ctx_count - offset_dev,
    )
    q_heads = jnp.concatenate([q_heads[:half_kv], moved_heads[0]], axis=0)
    d_heads = jnp.concatenate([d_heads[:half_kv], moved_heads[1]], axis=0)
    k_heads = jnp.concatenate([k_heads[:half_kv], moved_heads[2]], axis=0)
    v_heads = jnp.concatenate([v_heads[:half_kv], moved_heads[3]], axis=0)
    shift_pos = (ctx_index + offset_dev) % ctx_count * tok_rows + local_pos
    limits = (own_slot, own_slot)
    causal = local_pos[:, None] >= local_pos[None, :]
    q_parts = (q_heads[:half_kv], q_heads[half_kv:])
    d_parts = (d_heads[:half_kv], d_heads[half_kv:])

    def kv_parts(kv_block, head_half):
        return (
            kv_block[0][head_half * half_kv : (head_half + 1) * half_kv],
            kv_block[1][head_half * half_kv : (head_half + 1) * half_kv],
        )

    def scores_of(q_part, key_part, diagonal):
        raw_score = (
            jnp.einsum("cgqd,ckd->cgqk", q_part, key_part, preferred_element_type=jnp.float32)
            * score_scale
        )
        if diagonal:
            raw_score = jnp.where(causal, raw_score, -jnp.inf)
        return raw_score

    def forward_step(softmax_stats, head_half, kv_block, diagonal):
        row_max, row_total, row_weighted = softmax_stats
        key_part, value_part = kv_parts(kv_block, head_half)
        raw_score = scores_of(q_parts[head_half], key_part, diagonal)
        dprob = jnp.einsum(
            "cgqd,ckd->cgqk", d_parts[head_half], value_part, preferred_element_type=jnp.float32
        )
        new_max = jnp.maximum(row_max, jnp.max(raw_score, axis=-1))
        rescale = jnp.exp(row_max - new_max)
        weight = jnp.exp(raw_score - new_max[..., None])
        return (
            new_max,
            row_total * rescale + jnp.sum(weight, axis=-1),
            row_weighted * rescale + jnp.sum(weight * dprob, axis=-1),
        )

    stat_shape = (half_kv, per_group, tok_rows)
    softmax_stats = [
        (
            jnp.full(stat_shape, -jnp.inf, jnp.float32),
            jnp.zeros(stat_shape, jnp.float32),
            jnp.zeros(stat_shape, jnp.float32),
        )
        for head_half in range(2)
    ]
    kv_block = (k_heads, v_heads)
    kept_blocks = [kv_block]
    for hop_index in range(GROUP_DEV):
        if hop_index > 0:
            kv_block = from_behind((kv_block[0], kv_block[1]), "ctx", 1)
            kept_blocks.append(kv_block)
        for head_half in range(2):
            if hop_index == 0:
                softmax_stats[head_half] = forward_step(
                    softmax_stats[head_half], head_half, kv_block, True
                )
            else:
                softmax_stats[head_half] = lax.cond(
                    hop_index <= limits[head_half],
                    partial(forward_step, head_half=head_half, kv_block=kv_block, diagonal=False),
                    keep_state,
                    softmax_stats[head_half],
                )
    log_totals = [
        softmax_stats[head_half][0] + jnp.log(softmax_stats[head_half][1]) for head_half in range(2)
    ]
    deltas = [softmax_stats[head_half][2] / softmax_stats[head_half][1] for head_half in range(2)]

    def backward_step(dq_part, head_half, kv_block, diagonal):
        key_part, value_part = kv_parts(kv_block, head_half)
        raw_score = scores_of(q_parts[head_half], key_part, diagonal)
        prob = jnp.exp(raw_score - log_totals[head_half][..., None])
        dprob = jnp.einsum(
            "cgqd,ckd->cgqk", d_parts[head_half], value_part, preferred_element_type=jnp.float32
        )
        dscore = prob * (dprob - deltas[head_half][..., None])
        prob_low = prob.astype(jnp.bfloat16)
        dscore_low = dscore.astype(jnp.bfloat16)
        dq_next = dq_part + jnp.einsum(
            "cgqk,ckd->cgqd", dscore_low, key_part, preferred_element_type=jnp.float32
        )
        dk_term = jnp.einsum(
            "cgqk,cgqd->ckd", dscore_low, q_parts[head_half], preferred_element_type=jnp.float32
        )
        dv_term = jnp.einsum(
            "cgqk,cgqd->ckd", prob_low, d_parts[head_half], preferred_element_type=jnp.float32
        )
        return (dq_next, dk_term, dv_term)

    def skip_step(dq_part):
        blank_rows = jnp.zeros((half_kv, tok_rows, HEAD_WIDTH), jnp.float32)
        return (dq_part, blank_rows, blank_rows)

    dq_sums = [
        jnp.zeros((half_kv, per_group, tok_rows, HEAD_WIDTH), jnp.float32) for head_half in range(2)
    ]
    kv_block = (k_heads, v_heads)
    carried = None
    for hop_index in range(GROUP_DEV):
        if hop_index > 0:
            kv_block = from_behind((kv_block[0], kv_block[1]), "ctx", 1)
            carried = shifted((carried[0], carried[1]), "ctx", 1)
        dk_terms = []
        dv_terms = []
        for head_half in range(2):
            if hop_index == 0:
                result = backward_step(dq_sums[head_half], head_half, kv_block, True)
            else:
                result = lax.cond(
                    hop_index <= limits[head_half],
                    partial(backward_step, head_half=head_half, kv_block=kv_block, diagonal=False),
                    skip_step,
                    dq_sums[head_half],
                )
            dq_sums[head_half] = result[0]
            dk_terms.append(result[1])
            dv_terms.append(result[2])
        dk_block = jnp.concatenate(dk_terms, axis=0)
        dv_block = jnp.concatenate(dv_terms, axis=0)
        if hop_index == 0:
            carried = (dk_block, dv_block)
        else:
            carried = (carried[0] + dk_block, carried[1] + dv_block)
    owned_sums = (
        shifted(carried[0].astype(jnp.bfloat16), "ctx", ctx_count - (GROUP_DEV - 1)).astype(
            jnp.float32
        ),
        shifted(carried[1].astype(jnp.bfloat16), "ctx", ctx_count - (GROUP_DEV - 1)).astype(
            jnp.float32
        ),
    )
    dk_own = jnp.transpose(owned_sums[0] * score_scale, (1, 0, 2))
    dv_own = jnp.transpose(owned_sums[1], (1, 0, 2))
    positions = (own_pos, shift_pos)
    outputs = []
    for head_half in range(2):
        head_span = slice(head_half * half_kv, (head_half + 1) * half_kv)
        dq_rows = jnp.transpose(dq_sums[head_half], (2, 0, 1, 3)) * score_scale
        gq_part = rope_back(dq_rows, positions[head_half]).astype(jnp.bfloat16)
        gk_part = rope_back(dk_own[:, head_span], positions[head_half]).astype(jnp.bfloat16)
        gv_part = dv_own[:, head_span].astype(jnp.bfloat16)
        outputs.append((gq_part, gk_part, gv_part))
    shifted_out = outputs[1]
    shifted_out = shifted((outputs[1][0], outputs[1][1], outputs[1][2]), "ctx", offset_dev)
    query_grad_rows = jnp.take(
        jnp.concatenate([outputs[0][0], shifted_out[0]], axis=1), undo_order, axis=1
    ).reshape(tok_rows, QUERY_HEADS_HALF * HEAD_WIDTH)
    grad_k = jnp.take(
        jnp.concatenate([outputs[0][1], shifted_out[1]], axis=1), undo_order, axis=1
    ).reshape(tok_rows, kv_width)
    value_grad_rows = jnp.take(
        jnp.concatenate([outputs[0][2], shifted_out[2]], axis=1), undo_order, axis=1
    ).reshape(tok_rows, kv_width)
    query_adapter_term = jnp.dot(
        query_lowrank_state[0].T, query_grad_rows, preferred_element_type=jnp.float32
    )
    value_adapter_term = jnp.dot(
        value_lowrank_state[0].T, value_grad_rows, preferred_element_type=jnp.float32
    )
    query_adapter_sum, value_adapter_sum = lax.psum(
        (query_adapter_term, value_adapter_term), ("dp", "ctx")
    )
    return (
        query_grad_rows[None],
        grad_k[None],
        value_grad_rows[None],
        query_adapter_sum * ADAPTER_SCALE,
        value_adapter_sum * ADAPTER_SCALE,
    )


def solution(mesh):
    placed = (
        P("dp", "ctx", None),
        P("dp", "ctx", None),
        P("dp", "ctx", None),
        P("dp", "ctx", None),
        P("dp", "ctx", None),
        P("dp", "ctx", None),
        P(),
    )
    return jax.shard_map(
        local,
        mesh=mesh,
        in_specs=placed,
        out_specs=(P("dp", "ctx", None), P("dp", "ctx", None), P("dp", "ctx", None), P(), P()),
        check_vma=False,
    )
```

profile of v0, /device:TPU:1, one launch (start us, length us, event | category | flops | bytes accessed | tf_op | source)
XLA Modules:
  0.0 740.6 jit_solution(11481080849213869155)
XLA Ops:
  13.0 16.7 %collective-permute-start.2 = (bf16[2,128,128]{2,1,0:T(8,128)(2,1)}, bf16[2,128,128]{2,1,0:T(8,128)(2,1)}, u32[]{:S(2)}, u32[]{:S(2)}) collective-permute-start(bf16[2,128,128]{2,1,0:T(8,128)(2,1)} %get-tuple-element.1101), channel_id=1, source_target_pairs={{0,28},{1,29},{2,30},{3,31},{4,0},{5,1},{6,2},{7,3},{8,4},{9,5},{1... | collective-permute-start | bytes 196616 | tf_op jit(solution)/shard_map/ppermute | solution.py:20
  45.5 4.2 collective-permute-start.1
  53.5 4.0 collective-permute-start.4
  59.5 4.3 collective-permute-start.6
  65.8 4.4 collective-permute-start.8
  79.9 6.1 collective-permute-start.10
  86.0 4.7 collective-permute-start.11
  91.1 4.6 collective-permute-start.12
  100.7 4.7 collective-permute-start.14
  134.0 9.3 %collective-permute-start.28 = (f32[4,128,128]{2,1,0:T(8,128)}, f32[4,128,128]{2,1,0:T(8,128)}, u32[]{:S(2)}, u32[]{:S(2)}) collective-permute-start(f32[4,128,128]{2,1,0:T(8,128)} %pad_maximum_fusion.3), channel_id=1, source_target_pairs={{0,1},{1,2},{2,3},{3,4},{4,5},{5,6},{6,7},{7,8},{8,9},{9,10},{10,1... | collective-permute-start | bytes 786440 | tf_op jit(solution)/shard_map/ppermute | solution.py:20
  144.3 11.2 %collective-permute-start.19 = (f32[4,128,128]{2,1,0:T(8,128)}, f32[4,128,128]{2,1,0:T(8,128)}, u32[]{:S(2)}, u32[]{:S(2)}) collective-permute-start(f32[4,128,128]{2,1,0:T(8,128)} %pad_maximum_fusion.2), channel_id=1, source_target_pairs={{0,1},{1,2},{2,3},{3,4},{4,5},{5,6},{6,7},{7,8},{8,9},{9,10},{10,1... | collective-permute-start | bytes 786440 | tf_op jit(solution)/shard_map/ppermute | solution.py:20
  156.5 47.5 %collective-permute-start.18 = (bf16[128,2,8,128]{0,3,2,1:T(8,128)(2,1)}, bf16[128,2,8,128]{0,3,2,1:T(8,128)(2,1)}, u32[]{:S(2)}, u32[]{:S(2)}) collective-permute-start(bf16[128,2,8,128]{0,3,2,1:T(8,128)(2,1)} %pad_maximum_fusion.1), channel_id=1, source_target_pairs={{0,4},{1,5},{2,6},{3,7},{4,8},{5,9},{6,10},{7,11},{8,12},{9,13},{1... | collective-permute-start | bytes 1572872 | tf_op jit(solution)/shard_map/ppermute | solution.py:20
  212.7 4.5 collective-permute-start.20
  218.3 6.0 collective-permute-start.29
  227.6 6.7 collective-permute-start.30
  234.6 6.2 collective-permute-start.22
  242.2 5.6 collective-permute-start.31
  264.6 8.4 %collective-permute-done.32 = f32[4,128,128]{2,1,0:T(8,128)S(1)} collective-permute-done((f32[4,128,128]{2,1,0:T(8,128)S(1)}, f32[4,128,128]{2,1,0:T(8,128)S(1)}, u32[]{:S(2)}, u32[]{:S(2)}) %collective-permute-start.32) | collective-permute-done | bytes 262176 | tf_op jit(solution)/shard_map/ppermute | solution.py:20
  279.9 7.1 collective-permute-done.33
  289.2 306.4 %all-reduce.2.cloned.1.call-done = f32[8,4096]{1,0:T(8,128)} async-done(((f32[8,4096]{1,0:T(8,128)}), f32[8,4096]{1,0:T(8,128)}) %all-reduce.2.cloned.1.call-update) | async-done | bytes 131088 | tf_op jit(solution)/shard_map/psum | solution.py:247
  598.2 5.4 collective-permute-start.26
  604.5 5.5 collective-permute-start.35
  614.8 7.3 collective-permute-start.36
  631.4 99.6 %psum.15 = f32[8,512]{1,0:T(8,128)S(1)} all-reduce(f32[8,512]{1,0:T(8,128)S(1)} %convolution_bitcast_fusion.33), channel_id=1, replica_groups=mesh['dp'=16,'ctx'=32] {'dp','ctx'}, use_global_device_ids=true, to_apply=%region_107.110 | all-reduce | flops 4096 | bytes 32768 | tf_op jit(solution)/shard_map/psum | solution.py:247
  (398 shorter events, 144.3 us)
Async XLA Ops:
  7.2 588.5 %all-reduce.2.cloned.1.call-start = ((), (), s32[]{:S(2)}) async-start(), calls=%async_computation | async-start | bytes 262144 | tf_op jit(solution)/shard_map/psum | solution.py:247
  13.0 36.7 %collective-permute-start.2 = (bf16[2,128,128]{2,1,0:T(8,128)(2,1)}, bf16[2,128,128]{2,1,0:T(8,128)(2,1)}, u32[]{:S(2)}, u32[]{:S(2)}) collective-permute-start(bf16[2,128,128]{2,1,0:T(8,128)(2,1)} %get-tuple-element.1101), channel_id=1, source_target_pairs={{0,28},{1,29},{2,30},{3,31},{4,0},{5,1},{6,2},{7,3},{8,4},{9,5},{1... | collective-permute-start | bytes 196616 | tf_op jit(solution)/shard_map/ppermute | solution.py:20
  30.4 15.0 %collective-permute-start = (bf16[2,128,128]{2,1,0:T(8,128)(2,1)}, bf16[2,128,128]{2,1,0:T(8,128)(2,1)S(1)}, u32[]{:S(2)}, u32[]{:S(2)}) collective-permute-start(bf16[2,128,128]{2,1,0:T(8,128)(2,1)} %get-tuple-element.1103), channel_id=1, source_target_pairs={{0,28},{1,29},{2,30},{3,31},{4,0},{5,1},{6,2},{7,3},{8,4},{9,5},{1... | collective-permute-start | bytes 196616 | tf_op jit(solution)/shard_map/ppermute | solution.py:20
  36.7 54.0 %collective-permute-start.16 = (bf16[2,8,128,128]{3,2,1,0:T(8,128)(2,1)}, bf16[2,8,128,128]{3,2,1,0:T(8,128)(2,1)S(1)}, u32[]{:S(2)}, u32[]{:S(2)}) collective-permute-start(bf16[2,8,128,128]{3,2,1,0:T(8,128)(2,1)} %get-tuple-element.1091), channel_id=1, source_target_pairs={{0,28},{1,29},{2,30},{3,31},{4,0},{5,1},{6,2},{7,3},{8,4},{9,5},{1... | collective-permute-start | bytes 1572872 | tf_op jit(solution)/shard_map/ppermute | solution.py:20
  39.6 59.0 %collective-permute-start.17 = (bf16[2,8,128,128]{3,2,1,0:T(8,128)(2,1)}, bf16[2,8,128,128]{3,2,1,0:T(8,128)(2,1)S(1)}, u32[]{:S(2)}, u32[]{:S(2)}) collective-permute-start(bf16[2,8,128,128]{3,2,1,0:T(8,128)(2,1)} %get-tuple-element.1089), channel_id=1, source_target_pairs={{0,28},{1,29},{2,30},{3,31},{4,0},{5,1},{6,2},{7,3},{8,4},{9,5},{1... | collective-permute-start | bytes 1572872 | tf_op jit(solution)/shard_map/ppermute | solution.py:20
  65.8 14.1 %collective-permute-start.8 = (bf16[4,128,128]{2,1,0:T(8,128)(2,1)}, bf16[4,128,128]{2,1,0:T(8,128)(2,1)S(1)}, u32[]{:S(2)}, u32[]{:S(2)}) collective-permute-start(bf16[4,128,128]{2,1,0:T(8,128)(2,1)} %collective-permute-done.6), channel_id=1, source_target_pairs={{0,1},{1,2},{2,3},{3,4},{4,5},{5,6},{6,7},{7,8},{8,9},{9,10},{10,1... | collective-permute-start | bytes 393224 | tf_op jit(solution)/shard_map/ppermute | solution.py:26
  70.2 15.8 %collective-permute-start.9 = (bf16[4,128,128]{2,1,0:T(8,128)(2,1)}, bf16[4,128,128]{2,1,0:T(8,128)(2,1)}, u32[]{:S(2)}, u32[]{:S(2)}) collective-permute-start(bf16[4,128,128]{2,1,0:T(8,128)(2,1)} %collective-permute-done.7), channel_id=1, source_target_pairs={{0,1},{1,2},{2,3},{3,4},{4,5},{5,6},{6,7},{7,8},{8,9},{9,10},{10,1... | collective-permute-start | bytes 393224 | tf_op jit(solution)/shard_map/ppermute | solution.py:26
  79.9 11.2 %collective-permute-start.10 = (bf16[4,128,128]{2,1,0:T(8,128)(2,1)S(1)}, bf16[4,128,128]{2,1,0:T(8,128)(2,1)S(1)}, u32[]{:S(2)}, u32[]{:S(2)}) collective-permute-start(bf16[4,128,128]{2,1,0:T(8,128)(2,1)S(1)} %collective-permute-done.8), channel_id=1, source_target_pairs={{0,1},{1,2},{2,3},{3,4},{4,5},{5,6},{6,7},{7,8},{8,9},{9,10},{10,1... | collective-permute-start | bytes 393224 | tf_op jit(solution)/shard_map/ppermute | solution.py:26
  134.0 83.2 %collective-permute-start.28 = (f32[4,128,128]{2,1,0:T(8,128)}, f32[4,128,128]{2,1,0:T(8,128)}, u32[]{:S(2)}, u32[]{:S(2)}) collective-permute-start(f32[4,128,128]{2,1,0:T(8,128)} %pad_maximum_fusion.3), channel_id=1, source_target_pairs={{0,1},{1,2},{2,3},{3,4},{4,5},{5,6},{6,7},{7,8},{8,9},{9,10},{10,1... | collective-permute-start | bytes 786440 | tf_op jit(solution)/shard_map/ppermute | solution.py:20
  144.3 66.8 %collective-permute-start.19 = (f32[4,128,128]{2,1,0:T(8,128)}, f32[4,128,128]{2,1,0:T(8,128)}, u32[]{:S(2)}, u32[]{:S(2)}) collective-permute-start(f32[4,128,128]{2,1,0:T(8,128)} %pad_maximum_fusion.2), channel_id=1, source_target_pairs={{0,1},{1,2},{2,3},{3,4},{4,5},{5,6},{6,7},{7,8},{8,9},{9,10},{10,1... | collective-permute-start | bytes 786440 | tf_op jit(solution)/shard_map/ppermute | solution.py:20
  156.5 91.2 %collective-permute-start.18 = (bf16[128,2,8,128]{0,3,2,1:T(8,128)(2,1)}, bf16[128,2,8,128]{0,3,2,1:T(8,128)(2,1)}, u32[]{:S(2)}, u32[]{:S(2)}) collective-permute-start(bf16[128,2,8,128]{0,3,2,1:T(8,128)(2,1)} %pad_maximum_fusion.1), channel_id=1, source_target_pairs={{0,4},{1,5},{2,6},{3,7},{4,8},{5,9},{6,10},{7,11},{8,12},{9,13},{1... | collective-permute-start | bytes 1572872 | tf_op jit(solution)/shard_map/ppermute | solution.py:20
  212.7 11.7 %collective-permute-start.20 = (f32[4,128,128]{2,1,0:T(8,128)S(1)}, f32[4,128,128]{2,1,0:T(8,128)S(1)}, u32[]{:S(2)}, u32[]{:S(2)}) collective-permute-start(f32[4,128,128]{2,1,0:T(8,128)S(1)} %maximum_add_fusion), channel_id=1, source_target_pairs={{0,1},{1,2},{2,3},{3,4},{4,5},{5,6},{6,7},{7,8},{8,9},{9,10},{10,1... | collective-permute-start | bytes 786440 | tf_op jit(solution)/shard_map/ppermute | solution.py:20
  227.6 13.8 %collective-permute-start.30 = (f32[4,128,128]{2,1,0:T(8,128)S(1)}, f32[4,128,128]{2,1,0:T(8,128)S(1)}, u32[]{:S(2)}, u32[]{:S(2)}) collective-permute-start(f32[4,128,128]{2,1,0:T(8,128)S(1)} %maximum_add_fusion.8), channel_id=1, source_target_pairs={{0,1},{1,2},{2,3},{3,4},{4,5},{5,6},{6,7},{7,8},{8,9},{9,10},{10,1... | collective-permute-start | bytes 786440 | tf_op jit(solution)/shard_map/ppermute | solution.py:20
  234.6 15.1 %collective-permute-start.22 = (f32[4,128,128]{2,1,0:T(8,128)S(1)}, f32[4,128,128]{2,1,0:T(8,128)S(1)}, u32[]{:S(2)}, u32[]{:S(2)}) collective-permute-start(f32[4,128,128]{2,1,0:T(8,128)S(1)} %maximum_add_fusion.2), channel_id=1, source_target_pairs={{0,1},{1,2},{2,3},{3,4},{4,5},{5,6},{6,7},{7,8},{8,9},{9,10},{10,1... | collective-permute-start | bytes 786440 | tf_op jit(solution)/shard_map/ppermute | solution.py:20
  242.2 14.1 %collective-permute-start.31 = (f32[4,128,128]{2,1,0:T(8,128)}, f32[4,128,128]{2,1,0:T(8,128)}, u32[]{:S(2)}, u32[]{:S(2)}) collective-permute-start(f32[4,128,128]{2,1,0:T(8,128)} %maximum_add_fusion.9), channel_id=1, source_target_pairs={{0,1},{1,2},{2,3},{3,4},{4,5},{5,6},{6,7},{7,8},{8,9},{9,10},{10,1... | collective-permute-start | bytes 786440 | tf_op jit(solution)/shard_map/ppermute | solution.py:20
  249.9 12.7 %collective-permute-start.23 = (f32[4,128,128]{2,1,0:T(8,128)S(1)}, f32[4,128,128]{2,1,0:T(8,128)S(1)}, u32[]{:S(2)}, u32[]{:S(2)}) collective-permute-start(f32[4,128,128]{2,1,0:T(8,128)S(1)} %maximum_add_fusion.3), channel_id=1, source_target_pairs={{0,1},{1,2},{2,3},{3,4},{4,5},{5,6},{6,7},{7,8},{8,9},{9,10},{10,1... | collective-permute-start | bytes 786440 | tf_op jit(solution)/shard_map/ppermute | solution.py:20
  257.3 15.7 %collective-permute-start.32 = (f32[4,128,128]{2,1,0:T(8,128)S(1)}, f32[4,128,128]{2,1,0:T(8,128)S(1)}, u32[]{:S(2)}, u32[]{:S(2)}) collective-permute-start(f32[4,128,128]{2,1,0:T(8,128)S(1)} %maximum_add_fusion.10), channel_id=1, source_target_pairs={{0,1},{1,2},{2,3},{3,4},{4,5},{5,6},{6,7},{7,8},{8,9},{9,10},{10,1... | collective-permute-start | bytes 786440 | tf_op jit(solution)/shard_map/ppermute | solution.py:20
  262.7 15.3 %collective-permute-start.24 = (f32[4,128,128]{2,1,0:T(8,128)S(1)}, f32[4,128,128]{2,1,0:T(8,128)S(1)}, u32[]{:S(2)}, u32[]{:S(2)}) collective-permute-start(f32[4,128,128]{2,1,0:T(8,128)S(1)} %maximum_add_fusion.4), channel_id=1, source_target_pairs={{0,1},{1,2},{2,3},{3,4},{4,5},{5,6},{6,7},{7,8},{8,9},{9,10},{10,1... | collective-permute-start | bytes 786440 | tf_op jit(solution)/shard_map/ppermute | solution.py:20
  273.1 14.0 %collective-permute-start.33 = (f32[4,128,128]{2,1,0:T(8,128)S(1)}, f32[4,128,128]{2,1,0:T(8,128)S(1)}, u32[]{:S(2)}, u32[]{:S(2)}) collective-permute-start(f32[4,128,128]{2,1,0:T(8,128)S(1)} %maximum_add_fusion.11), channel_id=1, source_target_pairs={{0,1},{1,2},{2,3},{3,4},{4,5},{5,6},{6,7},{7,8},{8,9},{9,10},{10,1... | collective-permute-start | bytes 786440 | tf_op jit(solution)/shard_map/ppermute | solution.py:20
  278.0 319.2 %collective-permute-start.25 = (f32[4,128,128]{2,1,0:T(8,128)S(1)}, f32[4,128,128]{2,1,0:T(8,128)S(1)}, u32[]{:S(2)}, u32[]{:S(2)}) collective-permute-start(f32[4,128,128]{2,1,0:T(8,128)S(1)} %maximum_add_fusion.5), channel_id=1, source_target_pairs={{0,1},{1,2},{2,3},{3,4},{4,5},{5,6},{6,7},{7,8},{8,9},{9,10},{10,1... | collective-permute-start | bytes 786440 | tf_op jit(solution)/shard_map/ppermute | solution.py:20
  287.1 316.4 %collective-permute-start.34 = (f32[4,128,128]{2,1,0:T(8,128)S(1)}, f32[4,128,128]{2,1,0:T(8,128)S(1)}, u32[]{:S(2)}, u32[]{:S(2)}) collective-permute-start(f32[4,128,128]{2,1,0:T(8,128)S(1)} %maximum_add_fusion.12), channel_id=1, source_target_pairs={{0,1},{1,2},{2,3},{3,4},{4,5},{5,6},{6,7},{7,8},{8,9},{9,10},{10,1... | collective-permute-start | bytes 786440 | tf_op jit(solution)/shard_map/ppermute | solution.py:20
  598.2 11.9 %collective-permute-start.26 = (bf16[4,128,128]{2,1,0:T(8,128)(2,1)S(1)}, bf16[4,128,128]{2,1,0:T(8,128)(2,1)S(1)}, u32[]{:S(2)}, u32[]{:S(2)}) collective-permute-start(bf16[4,128,128]{2,1,0:T(8,128)(2,1)S(1)} %fusion.250), channel_id=1, source_target_pairs={{0,25},{1,26},{2,27},{3,28},{4,29},{5,30},{6,31},{7,0},{8,1},{9,2}... | collective-permute-start | bytes 393224 | tf_op jit(solution)/shard_map/ppermute | solution.py:20
  610.4 15.6 %collective-permute-start.27 = (bf16[128,2,128]{2,0,1:T(8,128)(2,1)S(1)}, bf16[128,2,128]{2,0,1:T(8,128)(2,1)S(1)}, u32[]{:S(2)}, u32[]{:S(2)}) collective-permute-start(bf16[128,2,128]{2,0,1:T(8,128)(2,1)S(1)} %pad_maximum_fusion.8), channel_id=1, source_target_pairs={{0,4},{1,5},{2,6},{3,7},{4,8},{5,9},{6,10},{7,11},{8,12},{9,13},{1... | collective-permute-start | bytes 196616 | tf_op jit(solution)/shard_map/ppermute | solution.py:20
  614.8 15.6 %collective-permute-start.36 = (bf16[128,2,128]{2,0,1:T(8,128)(2,1)S(1)}, bf16[128,2,128]{2,0,1:T(8,128)(2,1)S(1)}, u32[]{:S(2)}, u32[]{:S(2)}) collective-permute-start(bf16[128,2,128]{2,0,1:T(8,128)(2,1)S(1)} %get-tuple-element.1099), channel_id=1, source_target_pairs={{0,4},{1,5},{2,6},{3,7},{4,8},{5,9},{6,10},{7,11},{8,12},{9,13},{1... | collective-permute-start | bytes 196616 | tf_op jit(solution)/shard_map/ppermute | solution.py:20
  (101 other events, 2194.6 us)
Sparse Core Ops, SparseCore 0:
  276.2 319.4 all-reduce.1
where the time goes:
time: 753 us; the launch traced here: 741 us
  waiting for transfers between devices  339 us (45%)
  starting transfers between devices  207 us (27%)
  blocking collectives  99.6 us (13%)
  local copies, waits for them, and re-layouts  36 us (5%)
  other arithmetic  20.8 us (3%)
  matrix products  20.7 us (3%)
  between operations  16.4 us (2%)
    psum x1, waiting for transfers between devices, local(): lax.psum((query_adapter_term, value_adapter_term), ('dp', 'ctx'))  306 us
    ppermute x23, starting transfers between devices, shifted(): lax.ppermute(array, axis, [(i, (i + by) % count) for i in range(count)])  157 us
    psum x1, blocking collectives, local(): lax.psum((query_adapter_term, value_adapter_term), ('dp', 'ctx'))  99.6 us
    ppermute x14, starting transfers between devices, from_behind(): return lax.ppermute(array, axis, pairs)  50.3 us
    ppermute x23, waiting for transfers between devices, shifted(): lax.ppermute(array, axis, [(i, (i + by) % count) for i in range(count)])  32.3 us
    unnamed x177, local copies, waits for them, and re-layouts  17 us
  transfers between devices with their start and end apart: 38, of which 12 were waited for; matrix products, arithmetic and copies ran while one was open for 5% of the time, Pallas kernels for 0%

commit v1 on v0

v1 whole, which is shorter than its diff:
```python
import math

import jax
import jax.numpy as jnp
from jax import lax
from jax.experimental import pallas as pl
from jax.experimental.pallas import tpu as pltpu
from jax.sharding import PartitionSpec as P

QUERY_HEADS_HALF = 32
KEY_VALUE_HEADS = 4
HEAD_WIDTH = 128
GROUP_DEV = 8
TOK_DEV = 128
HALF_KV = KEY_VALUE_HEADS // 2
PER_GROUP = QUERY_HEADS_HALF // KEY_VALUE_HEADS
RANK = 8
CHIPS = GROUP_DEV // 2
PACK_ROWS = 4 * TOK_DEV + 16
Q_TILES = PER_GROUP // 2
ADAPTER_SCALE = 2.0
SCORE_SCALE = 1.0 / math.sqrt(HEAD_WIDTH)
EXP2_SCALE = SCORE_SCALE * math.log2(math.e)
MASKED = -1e30
NT = (((1,), (1,)), ((), ()))
TN = (((0,), (0,)), ((), ()))
VMEM_LIMIT = 56 * 1024 * 1024


def head_columns(ref, head):
    return ref[:, pl.ds(pl.multiple_of(head * HEAD_WIDTH, HEAD_WIDTH), HEAD_WIDTH)]


def pack_kernel(order_ref, keys_ref, values_ref, low_ref, plain_ref, moved_ref):
    for half, out in enumerate((plain_ref, moved_ref)):
        for sub in range(HALF_KV):
            head = order_ref[half * HALF_KV + sub]
            out[sub * TOK_DEV : (sub + 1) * TOK_DEV, :] = head_columns(keys_ref, head)
            out[(2 + sub) * TOK_DEV : (3 + sub) * TOK_DEV, :] = head_columns(values_ref, head)
        out[4 * TOK_DEV :, :] = low_ref[...]


def pack(order, keys, values, low_rows):
    whole = pl.BlockSpec(memory_space=pltpu.VMEM)
    shape = jax.ShapeDtypeStruct((PACK_ROWS, HEAD_WIDTH), jnp.bfloat16)
    return pl.pallas_call(
        pack_kernel,
        out_shape=(shape, shape),
        in_specs=[pl.BlockSpec(memory_space=pltpu.SMEM), whole, whole, whole],
        out_specs=(whole, whole),
        name="pack_heads",
    )(order, keys, values, low_rows)


def group_rows(x):
    return x.reshape(x.shape[0] // 8, 8, x.shape[1])


def attention_kernel(
    order_ref, count_ref, q_ref, d_ref, *refs
):
    mine = refs[:CHIPS]
    other = refs[CHIPS : 2 * CHIPS]
    cos_ref, sin_ref, low_ref = refs[2 * CHIPS : 2 * CHIPS + 3]
    refs = refs[2 * CHIPS + 3 :]
    refs = refs[len(refs) - 13 :]
    gq_ref, qad_ref, vad_ref, keep_ref, send_ref = refs[:5]
    s_ref, dp_ref, m_ref, l_ref, w_ref, dq_ref, dk_ref, dv_ref = refs[5:]
    sub = pl.program_id(0)
    tile = pl.program_id(1)
    chunks = count_ref[0]
    core = count_ref[1]
    rows = 2 * TOK_DEV
    q = jnp.concatenate([q_ref[:, :HEAD_WIDTH], q_ref[:, HEAD_WIDTH:]], axis=0)
    d = jnp.concatenate([d_ref[:, :HEAD_WIDTH], d_ref[:, HEAD_WIDTH:]], axis=0)
    k_rows = pl.ds(pl.multiple_of(sub * TOK_DEV, TOK_DEV), TOK_DEV)
    v_rows = pl.ds(pl.multiple_of((2 + sub) * TOK_DEV, TOK_DEV), TOK_DEV)

    def chunk(j, which):
        return jnp.concatenate([mine[j][which, :], other[j][which, :]], axis=0)

    def each_chunk(body):
        for j in range(CHIPS):
            if j == 0:
                body(j)
            else:
                pl.when(j < chunks)(lambda j=j: body(j))

    m_ref[...] = jnp.full_like(m_ref, MASKED)
    l_ref[...] = jnp.zeros_like(l_ref)
    w_ref[...] = jnp.zeros_like(w_ref)

    def scores(j):
        s = lax.dot_general(chunk(j, k_rows), q, NT, preferred_element_type=jnp.float32)
        if j == 0:
            key = lax.broadcasted_iota(jnp.int32, (rows, rows), 0)
            row = lax.broadcasted_iota(jnp.int32, (rows, rows), 1) % TOK_DEV
            limit = jnp.where(core == 1, rows, 0)
            allowed = (key <= row) | ((key >= TOK_DEV) & (key < limit))
            s = jnp.where(allowed, s, MASKED)
        s_ref[j] = s
        m_ref[...] = jnp.maximum(m_ref[...], jnp.max(group_rows(s), axis=0))
        dp_ref[j] = lax.dot_general(chunk(j, v_rows), d, NT, preferred_element_type=jnp.float32)

    each_chunk(scores)
    top = jnp.max(m_ref[...], axis=0, keepdims=True) * EXP2_SCALE

    def weights(j):
        p = jnp.exp2(s_ref[j] * EXP2_SCALE - top)
        s_ref[j] = p
        l_ref[...] += jnp.sum(group_rows(p), axis=0)
        w_ref[...] += jnp.sum(group_rows(p * dp_ref[j]), axis=0)

    each_chunk(weights)
    inverse = 1.0 / jnp.sum(l_ref[...], axis=0, keepdims=True)
    delta = jnp.sum(w_ref[...], axis=0, keepdims=True) * inverse

    def gradients(j):
        p = s_ref[j] * inverse
        ds = (p * (dp_ref[j] - delta)).astype(jnp.bfloat16)
        dv = jnp.dot(p.astype(jnp.bfloat16), d, preferred_element_type=jnp.float32)
        dk = jnp.dot(ds, q, preferred_element_type=jnp.float32)
        dq = lax.dot_general(ds, chunk(j, k_rows), TN, preferred_element_type=jnp.float32)
        if j == 0:
            dq_ref[...] = dq
        else:
            dq_ref[...] += dq

        @pl.when(tile == 0)
        def _():
            dk_ref[j] = dk
            dv_ref[j] = dv

        @pl.when(tile > 0)
        def _():
            dk_ref[j] += dk
            dv_ref[j] += dv

    each_chunk(gradients)
    dq = dq_ref[...] * SCORE_SCALE
    for h in range(2):
        x = dq[h * TOK_DEV : (h + 1) * TOK_DEV, :]
        turned = x * cos_ref[...] + pltpu.roll(x, HEAD_WIDTH // 2, 1) * sin_ref[...]
        low = turned.astype(jnp.bfloat16)
        gq_ref[:, h * HEAD_WIDTH : (h + 1) * HEAD_WIDTH] = low
        qad_ref[h] = (
            jnp.dot(low_ref[...], low, preferred_element_type=jnp.float32)[:RANK] * ADAPTER_SCALE
        )

    @pl.when(tile == Q_TILES - 1)
    def _():
        for j in range(CHIPS):

            @pl.when(j >= chunks)
            def _():
                dk_ref[j] = jnp.zeros(dk_ref.shape[1:], jnp.float32)
                dv_ref[j] = jnp.zeros(dv_ref.shape[1:], jnp.float32)

            keep_ref[j, k_rows, :] = dk_ref[j, :TOK_DEV]
            keep_ref[j, v_rows, :] = dv_ref[j, :TOK_DEV]
            send_ref[j, k_rows, :] = dk_ref[j, TOK_DEV:].astype(jnp.bfloat16)
            send_ref[j, v_rows, :] = dv_ref[j, TOK_DEV:].astype(jnp.bfloat16)
        vad_ref[0] = jnp.zeros(vad_ref.shape[1:], jnp.float32)
        for j in range(CHIPS):

            @pl.when(j < chunks)
            def _():
                term = jnp.zeros((16, HEAD_WIDTH), jnp.float32)
                for c, side in enumerate((mine, other)):
                    grad = dv_ref[j, c * TOK_DEV : (c + 1) * TOK_DEV].astype(jnp.bfloat16)
                    term += jnp.dot(
                        side[j][4 * TOK_DEV :, :], grad, preferred_element_type=jnp.float32
                    )
                vad_ref[0] += term[:RANK] * ADAPTER_SCALE


def attention(order, counts, query, out_grad, mine, other, cosine, sine, low_rows, before):
    tok = TOK_DEV
    pair = 2 * HEAD_WIDTH

    def whole(shape):
        return pl.BlockSpec(shape, lambda s, t, o, c: (0,) * len(shape))

    columns = pl.BlockSpec((tok, pair), lambda s, t, o, c: (0, o[s] * Q_TILES + t))
    in_specs = [columns, columns]
    in_specs += [whole((PACK_ROWS, HEAD_WIDTH))] * (2 * CHIPS)
    in_specs += [whole((tok, HEAD_WIDTH))] * 2 + [whole((16, HEAD_WIDTH))]
    operands = [query, out_grad, *mine, *other, cosine, sine, low_rows]
    aliases = {}
    if before is not None:
        for out, array in enumerate(before):
            aliases[2 + len(operands)] = out
            operands.append(array)
            in_specs.append(pl.BlockSpec(memory_space=pl.ANY))
    work = 8 * 2.5 * 10 * 2 * 256 * 256 * 128
    return pl.pallas_call(
        attention_kernel,
        grid_spec=pltpu.PrefetchScalarGridSpec(
            num_scalar_prefetch=2,
            grid=(HALF_KV, Q_TILES),
            in_specs=in_specs,
            out_specs=[
                columns,
                pl.BlockSpec((2, RANK, HEAD_WIDTH), lambda s, t, o, c: (o[s] * Q_TILES + t, 0, 0)),
                pl.BlockSpec((1, RANK, HEAD_WIDTH), lambda s, t, o, c: (s, 0, 0)),
                whole((CHIPS, 4 * tok, HEAD_WIDTH)),
                whole((CHIPS, 4 * tok, HEAD_WIDTH)),
            ],
            scratch_shapes=[
                pltpu.VMEM((CHIPS, 2 * tok, 2 * tok), jnp.float32),
                pltpu.VMEM((CHIPS, 2 * tok, 2 * tok), jnp.float32),
                pltpu.VMEM((8, 2 * tok), jnp.float32),
                pltpu.VMEM((8, 2 * tok), jnp.float32),
                pltpu.VMEM((8, 2 * tok), jnp.float32),
                pltpu.VMEM((2 * tok, HEAD_WIDTH), jnp.float32),
                pltpu.VMEM((CHIPS, 2 * tok, HEAD_WIDTH), jnp.float32),
                pltpu.VMEM((CHIPS, 2 * tok, HEAD_WIDTH), jnp.float32),
            ],
        ),
        out_shape=[
            jax.ShapeDtypeStruct((tok, QUERY_HEADS_HALF * HEAD_WIDTH), jnp.bfloat16),
            jax.ShapeDtypeStruct((QUERY_HEADS_HALF, RANK, HEAD_WIDTH), jnp.float32),
            jax.ShapeDtypeStruct((HALF_KV, RANK, HEAD_WIDTH), jnp.float32),
            jax.ShapeDtypeStruct((CHIPS, 4 * tok, HEAD_WIDTH), jnp.float32),
            jax.ShapeDtypeStruct((CHIPS, 4 * tok, HEAD_WIDTH), jnp.bfloat16),
        ],
        input_output_aliases=aliases,
        compiler_params=pltpu.CompilerParams(
            dimension_semantics=("arbitrary", "arbitrary"), vmem_limit_bytes=VMEM_LIMIT
        ),
        cost_estimate=pl.CostEstimate(
            flops=int(work), bytes_accessed=8 << 20, transcendentals=8 * 3 * 65536
        ),
        name="attention_plain" if before is None else "attention_moved",
    )(order, counts, *operands)


def finish_kernel(order_ref, cos_ref, sin_ref, *refs):
    gk_ref, gv_ref = refs[-2:]
    per_half = len(refs[:-2]) // 2
    for half in range(2):
        keep_ref, pair_ref, *arrived = refs[half * per_half : (half + 1) * per_half]
        total = keep_ref[0] + pair_ref[0].astype(jnp.float32)
        for part in arrived:
            total += part[...].astype(jnp.float32)
        for sub in range(HALF_KV):
            head = order_ref[half * HALF_KV + sub]
            columns = pl.ds(pl.multiple_of(head * HEAD_WIDTH, HEAD_WIDTH), HEAD_WIDTH)
            dk = total[sub * TOK_DEV : (sub + 1) * TOK_DEV] * SCORE_SCALE
            turned = dk * cos_ref[...] + pltpu.roll(dk, HEAD_WIDTH // 2, 1) * sin_ref[...]
            gk_ref[:, columns] = turned.astype(jnp.bfloat16)
            gv_ref[:, columns] = total[(2 + sub) * TOK_DEV : (3 + sub) * TOK_DEV].astype(
                jnp.bfloat16
            )


def finish(order, cosine, sine, halves):
    operands = []
    for keep, from_pair, arrived in halves:
        operands += [keep, from_pair, *arrived]
    whole = pl.BlockSpec(memory_space=pltpu.VMEM)
    shape = jax.ShapeDtypeStruct((TOK_DEV, KEY_VALUE_HEADS * HEAD_WIDTH), jnp.bfloat16)
    return pl.pallas_call(
        finish_kernel,
        out_shape=(shape, shape),
        in_specs=[pl.BlockSpec(memory_space=pltpu.SMEM)] + [whole] * (2 + len(operands)),
        out_specs=(whole, whole),
        compiler_params=pltpu.CompilerParams(vmem_limit_bytes=VMEM_LIMIT),
        name="finish_keys_values",
    )(order, cosine, sine, *operands)


def local(query, keys, values, out_grad, query_lowrank_state, value_lowrank_state, shift_flags):
    ctx_index = lax.axis_index("ctx")
    ctx_count = lax.axis_size("ctx")
    dp_count = lax.axis_size("dp")
    half_group = GROUP_DEV // 2
    core = ctx_index % 2
    pair = [(i, i ^ 1) for i in range(ctx_count)]
    chip_slots = (
        (ctx_index % GROUP_DEV) // 2,
        ((ctx_index + half_group) % GROUP_DEV) // 2,
    )

    def forward(distance, half):
        offset = half * half_group
        return [
            (i, (i + 2 * distance) % ctx_count)
            for i in range(ctx_count)
            if ((i + offset) % GROUP_DEV) // 2 + distance < CHIPS
        ]

    def backward(distance, half):
        return [(b, a) for a, b in forward(distance, half)]

    flags = shift_flags
    plain_rank = jnp.cumsum(1 - flags) - 1
    moved_rank = HALF_KV + jnp.cumsum(flags) - 1
    place = jnp.where(flags == 1, moved_rank, plain_rank)
    order = jnp.sum(
        jnp.where(
            place[None, :] == jnp.arange(KEY_VALUE_HEADS)[:, None],
            jnp.arange(KEY_VALUE_HEADS)[None, :],
            0,
        ),
        axis=1,
    ).astype(jnp.int32)

    def low_rows(state):
        return jnp.pad(state[0].T, ((0, 16 - RANK), (0, 0)))

    query_low = low_rows(query_lowrank_state)
    value_low = low_rows(value_lowrank_state)
    half_dim = HEAD_WIDTH // 2
    positions = ctx_index * TOK_DEV + jnp.arange(TOK_DEV, dtype=jnp.int32)
    inv_freq = 10000.0 ** (-(jnp.arange(half_dim, dtype=jnp.float32) * 2.0) / HEAD_WIDTH)
    angles = positions.astype(jnp.float32)[:, None] * inv_freq[None, :]
    cos_half, sin_half = jnp.cos(angles), jnp.sin(angles)
    cosine = jnp.concatenate([cos_half, cos_half], axis=1)
    sine = jnp.concatenate([sin_half, -sin_half], axis=1)

    packed = pack(order, keys[0], values[0], value_low)
    mine = [[packed[0]], [packed[1]]]
    other = [[], []]
    for half in range(2):
        for distance in range(1, CHIPS):
            mine[half].append(lax.ppermute(packed[half], "ctx", forward(distance, half)))
    both = lax.ppermute(jnp.stack([part for half in mine for part in half]), "ctx", pair)
    for half in range(2):
        other[half] = [both[half * CHIPS + j] for j in range(CHIPS)]

    results = []
    before = None
    for half in range(2):
        counts = jnp.stack([chip_slots[half] + 1, core]).astype(jnp.int32)
        result = attention(
            order[half * HALF_KV : (half + 1) * HALF_KV],
            counts,
            query[0],
            out_grad[0],
            mine[half],
            other[half],
            cosine,
            sine,
            query_low,
            before,
        )
        before = (result[0], result[1])
        results.append(result)
    gq, query_terms = before
    value_terms = jnp.concatenate([results[0][2], results[1][2]], axis=0)

    from_pair = lax.ppermute(jnp.concatenate([results[0][4], results[1][4]]), "ctx", pair)
    halves = []
    for half in range(2):
        keep = results[half][3]
        got = from_pair[half * CHIPS : (half + 1) * CHIPS]
        arrived = []
        for distance in range(1, CHIPS):
            part = (keep[distance] + got[distance].astype(jnp.float32)).astype(jnp.bfloat16)
            arrived.append(lax.ppermute(part, "ctx", backward(distance, half)))
        halves.append((keep[:1], got[:1], arrived))
    gk, gv = finish(order, cosine, sine, halves)

    value_rows = value_terms.reshape(ctx_count, 1, HEAD_WIDTH)
    terms = jnp.concatenate([query_terms, value_rows], axis=1)
    terms = jnp.sum(lax.all_to_all(terms, "ctx", 0, 0), axis=0)
    terms = jnp.sum(
        lax.all_to_all(jnp.broadcast_to(terms[None], (dp_count,) + terms.shape), "dp", 0, 0), axis=0
    )
    terms = lax.all_to_all(jnp.broadcast_to(terms[None], (ctx_count,) + terms.shape), "ctx", 0, 0)
    query_adapter = jnp.transpose(terms[:, :RANK], (1, 0, 2)).reshape(RANK, -1)
    value_heads = terms[:, RANK].reshape(KEY_VALUE_HEADS, RANK, HEAD_WIDTH)
    value_adapter = jnp.transpose(jnp.take(value_heads, place, axis=0), (1, 0, 2)).reshape(RANK, -1)
    return gq[None], gk[None], gv[None], query_adapter, value_adapter


def solution(mesh):
    rows = P("dp", "ctx", None)
    return jax.shard_map(
        local,
        mesh=mesh,
        in_specs=(rows,) * 6 + (P(),),
        out_specs=(rows, rows, rows, P(), P()),
        check_vma=False,
    )
```

time: 753 us -> 183 us (0.24)
  the two profiles are of different devices: /device:TPU:1 before, /device:TPU:40 now
where the time goes in v1:
time: 183 us; the launch traced here: 182 us
  starting transfers between devices  48.8 us (27%)
  waiting for transfers between devices  45 us (25%)
  Pallas kernels  34.8 us (19%)
  blocking collectives  33.9 us (19%)
  other arithmetic  10 us (5%)
  local copies, waits for them, and re-layouts  7.98 us (4%)
    all_to_all x1, blocking collectives, local(): terms = jnp.sum(lax.all_to_all(terms, 'ctx', 0, 0), axis=0)  33.9 us
    pallas_call x2, Pallas kernels, attention(): pl.pallas_call(attention_kernel, grid_spec=pltpu.PrefetchScalarGridSpec(n...  30.7 us
    ppermute x6, starting transfers between devices, local(): lax.ppermute(packed[half], 'ctx', forward(distance, half))  15.7 us
    ppermute x6, waiting for transfers between devices, local(): lax.ppermute(packed[half], 'ctx', forward(distance, half))  14.7 us
    ppermute x6, starting transfers between devices, local(): arrived.append(lax.ppermute(part, 'ctx', backward(distance, half)))  14.3 us
    ppermute x6, waiting for transfers between devices, local(): arrived.append(lax.ppermute(part, 'ctx', backward(distance, half)))  13.1 us
    all_to_all x1, waiting for transfers between devices, local(): lax.all_to_all(jnp.broadcast_to(terms[None], (ctx_count,) + terms.shape),...  12.1 us
    all_to_all x1, starting transfers between devices, local(): lax.all_to_all(jnp.broadcast_to(terms[None], (ctx_count,) + terms.shape),...  7.46 us
  transfers between devices with their start and end apart: 16, of which 9 were waited for; matrix products, arithmetic and copies ran while one was open for 4% of the time, Pallas kernels for 0%

profile of v1, /device:TPU:40, one launch (start us, length us, event | category | flops | bytes accessed | tf_op | source)
XLA Modules:
  0.0 181.6 jit_solution(3123689514493878108)
XLA Ops:
  4.9 1.7 pack_heads.1
  6.6 4.4 %collective-permute-start.3 = (bf16[528,128]{1,0:T(8,128)(2,1)}, bf16[528,128]{1,0:T(8,128)(2,1)S(1)}, u32[]{:S(2)}, u32[]{:S(2)}) collective-permute-start(bf16[528,128]{1,0:T(8,128)(2,1)} %get-tuple-element.20.refs_0_), channel_id=1, source_target_pairs={{0,2},{1,3},{2,4},{3,5},{4,6},{5,7},{8,10},{9,11},{10,12},{11,13},... | collective-permute-start | bytes 405512 | tf_op jit(solution)/shard_map/ppermute | solution.py:327
  11.0 6.1 %collective-permute-start.4 = (bf16[528,128]{1,0:T(8,128)(2,1)}, bf16[528,128]{1,0:T(8,128)(2,1)S(1)}, u32[]{:S(2)}, u32[]{:S(2)}) collective-permute-start(bf16[528,128]{1,0:T(8,128)(2,1)} %get-tuple-element.20.refs_0_), channel_id=1, source_target_pairs={{0,4},{1,5},{2,6},{3,7},{8,12},{9,13},{10,14},{11,15},{16,20},{17,... | collective-permute-start | bytes 405512 | tf_op jit(solution)/shard_map/ppermute | solution.py:327
  17.1 1.3 collective-permute-start.5
  18.4 1.9 %collective-permute-start = (bf16[528,128]{1,0:T(8,128)(2,1)}, bf16[528,128]{1,0:T(8,128)(2,1)S(1)}, u32[]{:S(2)}, u32[]{:S(2)}) collective-permute-start(bf16[528,128]{1,0:T(8,128)(2,1)} %get-tuple-element.19.refs_0_), channel_id=1, source_target_pairs={{0,2},{1,3},{4,6},{5,7},{6,8},{7,9},{8,10},{9,11},{12,14},{13,15},... | collective-permute-start | bytes 405512 | tf_op jit(solution)/shard_map/ppermute | solution.py:327
  20.3 1.3 collective-permute-start.1
  24.4 11.5 %collective-permute-done.refs_1_ = bf16[528,128]{1,0:T(8,128)(2,1)S(1)} collective-permute-done((bf16[528,128]{1,0:T(8,128)(2,1)}, bf16[528,128]{1,0:T(8,128)(2,1)S(1)}, u32[]{:S(2)}, u32[]{:S(2)}) %collective-permute-start) | collective-permute-done | bytes 135200 | tf_op jit(solution)/shard_map/ppermute | solution.py:327
  35.9 2.3 %collective-permute-done.1.refs_2_ = bf16[528,128]{1,0:T(8,128)(2,1)S(1)} collective-permute-done((bf16[528,128]{1,0:T(8,128)(2,1)}, bf16[528,128]{1,0:T(8,128)(2,1)S(1)}, u32[]{:S(2)}, u32[]{:S(2)}) %collective-permute-start.1) | collective-permute-done | bytes 135200 | tf_op jit(solution)/shard_map/ppermute | solution.py:327
  38.2 1.9 %collective-permute-start.6 = (bf16[8,528,128]{2,1,0:T(8,128)(2,1)S(1)}, bf16[8,528,128]{2,1,0:T(8,128)(2,1)S(1)}, u32[]{:S(2)}, u32[]{:S(2)}) collective-permute-start(bf16[8,528,128]{2,1,0:T(8,128)(2,1)S(1)} %bitcast_dynamic-update-slice_fusion), channel_id=1, source_target_pairs={{0,1},{1,0},{2,3},{3,2},{4,5},{5,4},{6,7},{7,6},{8,9},{9,8},{10,11... | collective-permute-start | bytes 3244040 | tf_op jit(solution)/shard_map/ppermute | solution.py:328
  44.3 10.8 %attention_plain.1 = (bf16[128,4096]{1,0:T(8,128)(2,1)}, f32[32,8,128]{2,1,0:T(8,128)}, f32[2,8,128]{2,1,0:T(8,128)}, f32[4,512,128]{2,1,0:T(8,128)}, bf16[4,512,128]{2,1,0:T(8,128)(2,1)}) custom-call(s32[2]{0:T(128)} %get-tuple-element.59.order_ref, s32[2]{0:T(128)} %pad_add_fusion.1.count_ref, bf16[128,4096]{1,0:T(8,128)(2,1)} %bitcast.88, ...), custom_call_target="tpu_custom_call" | custom-call | flops 3355443200 | bytes 8388608 | tf_op jit(solution)/shard_map/attention_plain/pallas_call | solution.py:196
  55.0 20.0 %attention_moved.1 = (bf16[128,4096]{1,0:T(8,128)(2,1)}, f32[32,8,128]{2,1,0:T(8,128)}, f32[2,8,128]{2,1,0:T(8,128)}, f32[4,512,128]{2,1,0:T(8,128)}, bf16[4,512,128]{2,1,0:T(8,128)(2,1)}) custom-call(s32[2]{0:T(128)} %get-tuple-element.60.order_ref, s32[2]{0:T(128)} %get-tuple-element.63.count_ref, ...), custom_call_target="tpu_custom_call", output_to_operand_aliasing={{0}: (15, {}), {1}: (16, {})} | custom-call | flops 3355443200 | bytes 8388608 | tf_op jit(solution)/shard_map/attention_moved/pallas_call | solution.py:196
  76.8 33.9 %all_to_all.15 = f32[32,9,128]{2,1,0:T(8,128)S(1)} all-to-all(f32[32,9,128]{2,1,0:T(8,128)S(1)} %pad_maximum_fusion.1), channel_id=1, replica_groups=mesh['dp'=16,'ctx'=32] {'ctx'}, dimensions={0} | all-to-all | bytes 294912 | tf_op jit(solution)/shard_map/all_to_all | solution.py:367
  111.3 7.5 %all-to-all-start.1 = ((f32[16,9,128]{2,1,0:T(8,128)}), f32[16,9,128]{2,1,0:T(8,128)S(1)}, u32[]{:S(2)}, u32[]{:S(2)}) async-start(f32[16,9,128]{2,1,0:T(8,128)} %broadcast_in_dim.55), calls=%async_computation.1 | async-start | bytes 262144 | tf_op jit(solution)/shard_map/all_to_all | solution.py:369
  118.9 2.1 %collective-permute-start.7 = (bf16[8,512,128]{2,1,0:T(8,128)(2,1)S(1)}, bf16[8,512,128]{2,1,0:T(8,128)(2,1)S(1)}, u32[]{:S(2)}, u32[]{:S(2)}) collective-permute-start(bf16[8,512,128]{2,1,0:T(8,128)(2,1)S(1)} %pad_maximum_fusion), channel_id=1, source_target_pairs={{0,1},{1,0},{2,3},{3,2},{4,5},{5,4},{6,7},{7,6},{8,9},{9,8},{10,11... | collective-permute-start | bytes 3145736 | tf_op jit(solution)/shard_map/ppermute | solution.py:353
  121.0 5.1 %all-to-all-done.1 = f32[16,9,128]{2,1,0:T(8,128)S(1)} async-done(((f32[16,9,128]{2,1,0:T(8,128)}), f32[16,9,128]{2,1,0:T(8,128)S(1)}, u32[]{:S(2)}, u32[]{:S(2)}) %all-to-all-start.1) | async-done | bytes 73760 | tf_op jit(solution)/shard_map/all_to_all | solution.py:369
  126.8 7.5 %all-to-all-start.2 = ((f32[32,9,128]{2,1,0:T(8,128)}), f32[32,9,128]{2,1,0:T(8,128)S(1)}, u32[]{:S(2)}, u32[]{:S(2)}) async-start(f32[32,9,128]{2,1,0:T(8,128)} %broadcast_in_dim.56), calls=%async_computation.2 | async-start | bytes 524288 | tf_op jit(solution)/shard_map/all_to_all | solution.py:371
  134.3 12.1 %all-to-all-done.2 = f32[32,9,128]{2,1,0:T(8,128)S(1)} async-done(((f32[32,9,128]{2,1,0:T(8,128)}), f32[32,9,128]{2,1,0:T(8,128)S(1)}, u32[]{:S(2)}, u32[]{:S(2)}) %all-to-all-start.2) | async-done | bytes 147488 | tf_op jit(solution)/shard_map/all_to_all | solution.py:371
  147.7 2.1 %fusion.5 = (bf16[512,128]{1,0:T(8,128)(2,1)S(1)}, bf16[512,128]{1,0:T(8,128)(2,1)S(1)}, bf16[512,128]{1,0:T(8,128)(2,1)S(1)}, bf16[512,128]{1,0:T(8,128)(2,1)S(...) fusion(f32[4,512,128]{2,1,0:T(8,128)} %get-tuple-element.27, ...), kind=kLoop, calls=%fused_computation.30 | loop fusion | flops 1179648 | bytes 4194304 | tf_op jit(solution)/shard_map/convert_element_type | solution.py:360
  151.8 8.4 %collective-permute-start.11 = (bf16[512,128]{1,0:T(8,128)(2,1)S(1)}, bf16[512,128]{1,0:T(8,128)(2,1)S(1)}, u32[]{:S(2)}, u32[]{:S(2)}) collective-permute-start(bf16[512,128]{1,0:T(8,128)(2,1)S(1)} %get-tuple-element.37), channel_id=1, source_target_pairs={{2,0},{3,1},{6,4},{7,5},{8,6},{9,7},{10,8},{11,9},{14,12},{15,13},... | collective-permute-start | bytes 393224 | tf_op jit(solution)/shard_map/ppermute | solution.py:361
  160.2 1.3 collective-permute-start.12
  166.2 2.6 %collective-permute-done.12.refs_8_ = bf16[512,128]{1,0:T(8,128)(2,1)S(1)} collective-permute-done((bf16[512,128]{1,0:T(8,128)(2,1)S(1)}, bf16[512,128]{1,0:T(8,128)(2,1)S(1)}, u32[]{:S(2)}, u32[]{:S(2)}) %collective-permute-start.12) | collective-permute-done | bytes 131104 | tf_op jit(solution)/shard_map/ppermute | solution.py:361
  168.9 1.5 collective-permute-done.8.refs_2_
  170.3 8.3 %collective-permute-done.9.refs_3_ = bf16[512,128]{1,0:T(8,128)(2,1)S(1)} collective-permute-done((bf16[512,128]{1,0:T(8,128)(2,1)S(1)}, bf16[512,128]{1,0:T(8,128)(2,1)S(1)}, u32[]{:S(2)}, u32[]{:S(2)}) %collective-permute-start.9) | collective-permute-done | bytes 131104 | tf_op jit(solution)/shard_map/ppermute | solution.py:361
  179.3 2.3 %finish_keys_values.1 = (bf16[128,512]{1,0:T(8,128)(2,1)}, bf16[128,512]{1,0:T(8,128)(2,1)}) custom-call(s32[4]{0:T(128)} %select_reduce_fusion.order_ref, f32[128,128]{1,0:T(8,128)} %get-tuple-element.61.refs_8_.cos_ref, f32[128,128]{1,0:T(8,128)} %get-tuple-element.62.refs_9_.sin_ref, f32[1,512,128]{2,1,0:T(8,128)} %get-tuple-element.52.refs_0_, ...), custom_call_target="tpu_custom_call" | custom-call | tf_op jit(solution)/shard_map/finish_keys_values/pallas_call | solution.py:263
  (88 shorter events, 22.8 us)
Async XLA Ops:
  6.6 16.0 %collective-permute-start.3 = (bf16[528,128]{1,0:T(8,128)(2,1)}, bf16[528,128]{1,0:T(8,128)(2,1)S(1)}, u32[]{:S(2)}, u32[]{:S(2)}) collective-permute-start(bf16[528,128]{1,0:T(8,128)(2,1)} %get-tuple-element.20.refs_0_), channel_id=1, source_target_pairs={{0,2},{1,3},{2,4},{3,5},{4,6},{5,7},{8,10},{9,11},{10,12},{11,13},... | collective-permute-start | bytes 405512 | tf_op jit(solution)/shard_map/ppermute | solution.py:327
  11.0 12.3 %collective-permute-start.4 = (bf16[528,128]{1,0:T(8,128)(2,1)}, bf16[528,128]{1,0:T(8,128)(2,1)S(1)}, u32[]{:S(2)}, u32[]{:S(2)}) collective-permute-start(bf16[528,128]{1,0:T(8,128)(2,1)} %get-tuple-element.20.refs_0_), channel_id=1, source_target_pairs={{0,4},{1,5},{2,6},{3,7},{8,12},{9,13},{10,14},{11,15},{16,20},{17,... | collective-permute-start | bytes 405512 | tf_op jit(solution)/shard_map/ppermute | solution.py:327
  17.1 7.2 %collective-permute-start.5 = (bf16[528,128]{1,0:T(8,128)(2,1)}, bf16[528,128]{1,0:T(8,128)(2,1)S(1)}, u32[]{:S(2)}, u32[]{:S(2)}) collective-permute-start(bf16[528,128]{1,0:T(8,128)(2,1)} %get-tuple-element.20.refs_0_), channel_id=1, source_target_pairs={{0,6},{1,7},{8,14},{9,15},{16,22},{17,23},{24,30},{25,31},{32,38},... | collective-permute-start | bytes 405512 | tf_op jit(solution)/shard_map/ppermute | solution.py:327
  18.4 21.8 %copy-start.18 = (bf16[1,128,8]{1,2,0:T(8,128)(2,1)S(1)}, bf16[1,128,8]{1,2,0:T(8,128)(2,1)}, u32[]{:S(2)}) copy-start(bf16[1,128,8]{1,2,0:T(8,128)(2,1)} %param.11) | copy-start | bytes 6148
  18.4 17.4 %collective-permute-start = (bf16[528,128]{1,0:T(8,128)(2,1)}, bf16[528,128]{1,0:T(8,128)(2,1)S(1)}, u32[]{:S(2)}, u32[]{:S(2)}) collective-permute-start(bf16[528,128]{1,0:T(8,128)(2,1)} %get-tuple-element.19.refs_0_), channel_id=1, source_target_pairs={{0,2},{1,3},{4,6},{5,7},{6,8},{7,9},{8,10},{9,11},{12,14},{13,15},... | collective-permute-start | bytes 405512 | tf_op jit(solution)/shard_map/ppermute | solution.py:327
  20.3 17.8 %collective-permute-start.1 = (bf16[528,128]{1,0:T(8,128)(2,1)}, bf16[528,128]{1,0:T(8,128)(2,1)S(1)}, u32[]{:S(2)}, u32[]{:S(2)}) collective-permute-start(bf16[528,128]{1,0:T(8,128)(2,1)} %get-tuple-element.19.refs_0_), channel_id=1, source_target_pairs={{4,8},{5,9},{6,10},{7,11},{12,16},{13,17},{14,18},{15,19},{20,24},... | collective-permute-start | bytes 405512 | tf_op jit(solution)/shard_map/ppermute | solution.py:327
  22.6 15.6 %collective-permute-start.2 = (bf16[528,128]{1,0:T(8,128)(2,1)}, bf16[528,128]{1,0:T(8,128)(2,1)S(1)}, u32[]{:S(2)}, u32[]{:S(2)}) collective-permute-start(bf16[528,128]{1,0:T(8,128)(2,1)} %get-tuple-element.19.refs_0_), channel_id=1, source_target_pairs={{4,10},{5,11},{12,18},{13,19},{20,26},{21,27},{28,2},{29,3},{36,42... | collective-permute-start | bytes 405512 | tf_op jit(solution)/shard_map/ppermute | solution.py:327
  23.3 19.3 %copy-start.7 = (bf16[528,128]{1,0:T(8,128)(2,1)}, bf16[528,128]{1,0:T(8,128)(2,1)S(1)}, u32[]{:S(2)}) copy-start(bf16[528,128]{1,0:T(8,128)(2,1)S(1)} %collective-permute-done.4.refs_2_) | copy-start | bytes 405508
  23.3 19.2 %copy-start.16 = (s32[4]{0:T(128)S(1)}, s32[4]{0:T(128)}, u32[]{:S(2)}) copy-start(s32[4]{0:T(128)} %select_reduce_fusion.order_ref) | copy-start | bytes 52
  24.3 19.9 %copy-start.9 = (bf16[528,128]{1,0:T(8,128)(2,1)}, bf16[528,128]{1,0:T(8,128)(2,1)S(1)}, u32[]{:S(2)}) copy-start(bf16[528,128]{1,0:T(8,128)(2,1)S(1)} %collective-permute-done.5.refs_3_) | copy-start | bytes 405508
  38.2 5.0 %collective-permute-start.6 = (bf16[8,528,128]{2,1,0:T(8,128)(2,1)S(1)}, bf16[8,528,128]{2,1,0:T(8,128)(2,1)S(1)}, u32[]{:S(2)}, u32[]{:S(2)}) collective-permute-start(bf16[8,528,128]{2,1,0:T(8,128)(2,1)S(1)} %bitcast_dynamic-update-slice_fusion), channel_id=1, source_target_pairs={{0,1},{1,0},{2,3},{3,2},{4,5},{5,4},{6,7},{7,6},{8,9},{9,8},{10,11... | collective-permute-start | bytes 3244040 | tf_op jit(solution)/shard_map/ppermute | solution.py:328
  55.0 20.0 %copy-start.17 = (f32[2,8,128]{2,1,0:T(8,128)S(1)}, f32[2,8,128]{2,1,0:T(8,128)}, u32[]{:S(2)}) copy-start(f32[2,8,128]{2,1,0:T(8,128)} %get-tuple-element.31) | copy-start | bytes 24580
  75.0 43.8 %copy-start.1 = (bf16[4,512,128]{2,1,0:T(8,128)(2,1)S(1)}, bf16[4,512,128]{2,1,0:T(8,128)(2,1)}, u32[]{:S(2)}) copy-start(bf16[4,512,128]{2,1,0:T(8,128)(2,1)} %get-tuple-element.25) | copy-start | bytes 1572868
  75.0 43.8 %copy-start.2 = (bf16[4,512,128]{2,1,0:T(8,128)(2,1)S(1)}, bf16[4,512,128]{2,1,0:T(8,128)(2,1)}, u32[]{:S(2)}) copy-start(bf16[4,512,128]{2,1,0:T(8,128)(2,1)} %get-tuple-element.26) | copy-start | bytes 1572868
  111.3 14.7 %all-to-all-start.1 = ((f32[16,9,128]{2,1,0:T(8,128)}), f32[16,9,128]{2,1,0:T(8,128)S(1)}, u32[]{:S(2)}, u32[]{:S(2)}) async-start(f32[16,9,128]{2,1,0:T(8,128)} %broadcast_in_dim.55), calls=%async_computation.1 | async-start | bytes 262144 | tf_op jit(solution)/shard_map/all_to_all | solution.py:369
  118.9 28.8 %copy-start = (f32[4,512,128]{2,1,0:T(8,128)S(1)}, f32[4,512,128]{2,1,0:T(8,128)}, u32[]{:S(2)}) copy-start(f32[4,512,128]{2,1,0:T(8,128)} %get-tuple-element.24) | copy-start | bytes 3145732
  118.9 28.7 %collective-permute-start.7 = (bf16[8,512,128]{2,1,0:T(8,128)(2,1)S(1)}, bf16[8,512,128]{2,1,0:T(8,128)(2,1)S(1)}, u32[]{:S(2)}, u32[]{:S(2)}) collective-permute-start(bf16[8,512,128]{2,1,0:T(8,128)(2,1)S(1)} %pad_maximum_fusion), channel_id=1, source_target_pairs={{0,1},{1,0},{2,3},{3,2},{4,5},{5,4},{6,7},{7,6},{8,9},{9,8},{10,11... | collective-permute-start | bytes 3145736 | tf_op jit(solution)/shard_map/ppermute | solution.py:353
  126.8 19.6 %all-to-all-start.2 = ((f32[32,9,128]{2,1,0:T(8,128)}), f32[32,9,128]{2,1,0:T(8,128)S(1)}, u32[]{:S(2)}, u32[]{:S(2)}) async-start(f32[32,9,128]{2,1,0:T(8,128)} %broadcast_in_dim.56), calls=%async_computation.2 | async-start | bytes 524288 | tf_op jit(solution)/shard_map/all_to_all | solution.py:371
  149.8 13.7 %collective-permute-start.10 = (bf16[512,128]{1,0:T(8,128)(2,1)S(1)}, bf16[512,128]{1,0:T(8,128)(2,1)S(1)}, u32[]{:S(2)}, u32[]{:S(2)}) collective-permute-start(bf16[512,128]{1,0:T(8,128)(2,1)S(1)} %get-tuple-element.51), channel_id=1, source_target_pairs={{6,0},{7,1},{14,8},{15,9},{22,16},{23,17},{30,24},{31,25},{38,32},... | collective-permute-start | bytes 393224 | tf_op jit(solution)/shard_map/ppermute | solution.py:361
  151.8 14.5 %collective-permute-start.11 = (bf16[512,128]{1,0:T(8,128)(2,1)S(1)}, bf16[512,128]{1,0:T(8,128)(2,1)S(1)}, u32[]{:S(2)}, u32[]{:S(2)}) collective-permute-start(bf16[512,128]{1,0:T(8,128)(2,1)S(1)} %get-tuple-element.37), channel_id=1, source_target_pairs={{2,0},{3,1},{6,4},{7,5},{8,6},{9,7},{10,8},{11,9},{14,12},{15,13},... | collective-permute-start | bytes 393224 | tf_op jit(solution)/shard_map/ppermute | solution.py:361
  160.2 8.6 %collective-permute-start.12 = (bf16[512,128]{1,0:T(8,128)(2,1)S(1)}, bf16[512,128]{1,0:T(8,128)(2,1)S(1)}, u32[]{:S(2)}, u32[]{:S(2)}) collective-permute-start(bf16[512,128]{1,0:T(8,128)(2,1)S(1)} %get-tuple-element.36), channel_id=1, source_target_pairs={{8,4},{9,5},{10,6},{11,7},{16,12},{17,13},{18,14},{19,15},{24,20},... | collective-permute-start | bytes 393224 | tf_op jit(solution)/shard_map/ppermute | solution.py:361
  161.5 7.3 %collective-permute-start.13 = (bf16[512,128]{1,0:T(8,128)(2,1)S(1)}, bf16[512,128]{1,0:T(8,128)(2,1)S(1)}, u32[]{:S(2)}, u32[]{:S(2)}) collective-permute-start(bf16[512,128]{1,0:T(8,128)(2,1)S(1)} %get-tuple-element.35), channel_id=1, source_target_pairs={{10,4},{11,5},{18,12},{19,13},{26,20},{27,21},{2,28},{3,29},{42,36... | collective-permute-start | bytes 393224 | tf_op jit(solution)/shard_map/ppermute | solution.py:361
  162.2 8.1 %collective-permute-start.8 = (bf16[512,128]{1,0:T(8,128)(2,1)S(1)}, bf16[512,128]{1,0:T(8,128)(2,1)S(1)}, u32[]{:S(2)}, u32[]{:S(2)}) collective-permute-start(bf16[512,128]{1,0:T(8,128)(2,1)S(1)} %get-tuple-element.49), channel_id=1, source_target_pairs={{2,0},{3,1},{4,2},{5,3},{6,4},{7,5},{10,8},{11,9},{12,10},{13,11},... | collective-permute-start | bytes 393224 | tf_op jit(solution)/shard_map/ppermute | solution.py:361
  163.5 15.1 %collective-permute-start.9 = (bf16[512,128]{1,0:T(8,128)(2,1)S(1)}, bf16[512,128]{1,0:T(8,128)(2,1)S(1)}, u32[]{:S(2)}, u32[]{:S(2)}) collective-permute-start(bf16[512,128]{1,0:T(8,128)(2,1)S(1)} %get-tuple-element.50), channel_id=1, source_target_pairs={{4,0},{5,1},{6,2},{7,3},{12,8},{13,9},{14,10},{15,11},{20,16},{21,... | collective-permute-start | bytes 393224 | tf_op jit(solution)/shard_map/ppermute | solution.py:361
  (11 other events, 113.6 us)

commit v2 on v1

v2 whole, which is shorter than its diff:
```python
import math

import jax
import jax.numpy as jnp
from jax import lax
from jax.experimental import pallas as pl
from jax.experimental.pallas import tpu as pltpu
from jax.sharding import Mesh, PartitionSpec as P

QUERY_HEADS_HALF = 32
KEY_VALUE_HEADS = 4
HEAD_WIDTH = 128
GROUP_DEV = 8
TOK_DEV = 128
HALF_KV = KEY_VALUE_HEADS // 2
PER_GROUP = QUERY_HEADS_HALF // KEY_VALUE_HEADS
RANK = 8
CHIPS = GROUP_DEV // 2
PACK_ROWS = 4 * TOK_DEV + 16
PEERS = 16
TERM_ROWS = 32
TERM_BLOCK = PEERS // KEY_VALUE_HEADS
ADAPTER_SCALE = 2.0
SCORE_SCALE = 1.0 / math.sqrt(HEAD_WIDTH)
EXP2_SCALE = SCORE_SCALE * math.log2(math.e)
MASKED = -1e30
NT = (((1,), (1,)), ((), ()))
TN = (((0,), (0,)), ((), ()))
VMEM_LIMIT = 56 * 1024 * 1024
SEQ_AXES = ("yh", "zc")
SUM_AXES = ("dp", "yh")


def head_of(flags, half, sub):
    hit = [flags[head] == half for head in range(KEY_VALUE_HEADS)]
    low = jnp.where(hit[0], 0, jnp.where(hit[1], 1, 2))
    high = jnp.where(hit[3], 3, jnp.where(hit[2], 2, 1))
    return jnp.where(sub == 0, low, high)


def columns_of(head):
    return pl.ds(pl.multiple_of(head * HEAD_WIDTH, HEAD_WIDTH), HEAD_WIDTH)


def pack_kernel(flags_ref, keys_ref, values_ref, low_ref, plain_ref, moved_ref):
    eye = (
        lax.broadcasted_iota(jnp.int32, (TOK_DEV, TOK_DEV), 0)
        == lax.broadcasted_iota(jnp.int32, (TOK_DEV, TOK_DEV), 1)
    ).astype(jnp.bfloat16)
    low = lax.dot_general(low_ref[...], eye, TN, preferred_element_type=jnp.float32)
    low = jnp.concatenate([low, jnp.zeros_like(low)], axis=0).astype(jnp.bfloat16)
    for half, out in enumerate((plain_ref, moved_ref)):
        for sub in range(HALF_KV):
            columns = columns_of(head_of(flags_ref, half, sub))
            out[sub * TOK_DEV : (sub + 1) * TOK_DEV, :] = keys_ref[:, columns]
            out[(2 + sub) * TOK_DEV : (3 + sub) * TOK_DEV, :] = values_ref[:, columns]
        out[4 * TOK_DEV :, :] = low


def pack(flags, keys, values, low):
    whole = pl.BlockSpec(memory_space=pltpu.VMEM)
    shape = jax.ShapeDtypeStruct((PACK_ROWS, HEAD_WIDTH), jnp.bfloat16)
    return pl.pallas_call(
        pack_kernel,
        out_shape=(shape, shape),
        in_specs=[pl.BlockSpec(memory_space=pltpu.SMEM), whole, whole, whole],
        out_specs=(whole, whole),
        name="pack_heads",
    )(flags, keys, values, low)


def attention_kernel(flags_ref, table_ref, q_ref, d_ref, mine_ref, other_ref, *refs):
    cos_ref, sin_ref, low_ref = refs[:3]
    refs = refs[len(refs) - 9 :]
    gq_ref, term_ref, keep_ref, send_ref = refs[:4]
    k_all, v_all, low_all, dk_ref, dv_ref = refs[4:]
    sub = pl.program_id(0)
    chunks = table_ref[0]
    core = table_ref[1]
    rows = 2 * TOK_DEV
    wide = PER_GROUP * TOK_DEV
    k_rows = pl.ds(pl.multiple_of(sub * TOK_DEV, TOK_DEV), TOK_DEV)
    v_rows = pl.ds(pl.multiple_of((2 + sub) * TOK_DEV, TOK_DEV), TOK_DEV)

    def branch(n):
        for j in range(n):
            place = table_ref[2 + j]
            for c, side in enumerate((mine_ref, other_ref)):
                span = slice(j * rows + c * TOK_DEV, j * rows + (c + 1) * TOK_DEV)
                k_all[span, :] = side[place, k_rows, :]
                v_all[span, :] = side[place, v_rows, :]
                low_all[:, span] = side[place, 4 * TOK_DEV :, :]
        width = n * rows
        key = lax.broadcasted_iota(jnp.int32, (rows, wide), 0)
        row = lax.broadcasted_iota(jnp.int32, (rows, wide), 1) % TOK_DEV
        limit = jnp.where(core == 1, rows, 0)
        allowed = (key <= row) | ((key >= TOK_DEV) & (key < limit))

        def stacked(ref):
            return jnp.concatenate(
                [ref[:, h * HEAD_WIDTH : (h + 1) * HEAD_WIDTH] for h in range(PER_GROUP)], axis=0
            )

        q = stacked(q_ref)
        d = stacked(d_ref)
        k = k_all[:width, :]
        s = lax.dot_general(k, q, NT, preferred_element_type=jnp.float32)
        near = jnp.where(allowed, s[:rows], MASKED)
        s = near if n == 1 else jnp.concatenate([near, s[rows:]], axis=0)
        dp = lax.dot_general(v_all[:width, :], d, NT, preferred_element_type=jnp.float32)
        top = jnp.max(s, axis=0, keepdims=True) * EXP2_SCALE
        p = jnp.exp2(s * EXP2_SCALE - top)
        inverse = 1.0 / jnp.sum(p, axis=0, keepdims=True)
        delta = jnp.sum(p * dp, axis=0, keepdims=True) * inverse
        p = p * inverse
        ds = (p * (dp - delta)).astype(jnp.bfloat16)
        dv_ref[:width, :] = jnp.dot(p.astype(jnp.bfloat16), d, preferred_element_type=jnp.float32)
        dk_ref[:width, :] = jnp.dot(ds, q, preferred_element_type=jnp.float32)
        dq = lax.dot_general(ds, k, TN, preferred_element_type=jnp.float32) * SCORE_SCALE
        low_rank = low_ref[...]
        parts = []
        for h in range(PER_GROUP):
            x = dq[h * TOK_DEV : (h + 1) * TOK_DEV, :]
            turned = x * cos_ref[...] + pltpu.roll(x, HEAD_WIDTH // 2, 1) * sin_ref[...]
            low = turned.astype(jnp.bfloat16)
            gq_ref[:, h * HEAD_WIDTH : (h + 1) * HEAD_WIDTH] = low
            parts.append(
                lax.dot_general(low_rank, low, TN, preferred_element_type=jnp.float32)
                * ADAPTER_SCALE
            )
        value_part = (
            jnp.dot(
                low_all[:, :width],
                dv_ref[:width, :].astype(jnp.bfloat16),
                preferred_element_type=jnp.float32,
            )
            * ADAPTER_SCALE
        )
        pair_rows = 2 * RANK // PER_GROUP
        blank = jnp.zeros((2 * RANK - pair_rows, HEAD_WIDTH), jnp.float32)
        for i in range(TERM_BLOCK):
            block = jnp.concatenate(parts[2 * i : 2 * i + 2], axis=0)
            term_ref[i, : 2 * RANK, :] = block.astype(jnp.bfloat16)
            block = jnp.concatenate([value_part[i * pair_rows : (i + 1) * pair_rows], blank], axis=0)
            term_ref[i, 2 * RANK :, :] = block.astype(jnp.bfloat16)
        for j in range(CHIPS):
            place = table_ref[2 + j]
            if j < n:
                span = slice(j * rows, j * rows + TOK_DEV)
                past = slice(j * rows + TOK_DEV, (j + 1) * rows)
                keep_ref[place, k_rows, :] = dk_ref[span, :]
                keep_ref[place, v_rows, :] = dv_ref[span, :]
                send_ref[place, k_rows, :] = dk_ref[past, :].astype(jnp.bfloat16)
                send_ref[place, v_rows, :] = dv_ref[past, :].astype(jnp.bfloat16)
            else:
                keep_ref[place, k_rows, :] = jnp.zeros((TOK_DEV, HEAD_WIDTH), jnp.float32)
                keep_ref[place, v_rows, :] = jnp.zeros((TOK_DEV, HEAD_WIDTH), jnp.float32)
                send_ref[place, k_rows, :] = jnp.zeros((TOK_DEV, HEAD_WIDTH), jnp.bfloat16)
                send_ref[place, v_rows, :] = jnp.zeros((TOK_DEV, HEAD_WIDTH), jnp.bfloat16)

    for n in range(1, CHIPS + 1):
        pl.when(chunks == n)(lambda n=n: branch(n))


def attention(half, flags, table, query, out_grad, mine, other, cosine, sine, low, before):
    tok = TOK_DEV
    wide = PER_GROUP * HEAD_WIDTH
    keys = CHIPS * 2 * tok

    def whole(shape):
        return pl.BlockSpec(shape, lambda s, f, t: (0,) * len(shape))

    columns = pl.BlockSpec((tok, wide), lambda s, f, t: (0, head_of(f, half, s)))
    terms = pl.BlockSpec(
        (TERM_BLOCK, TERM_ROWS, HEAD_WIDTH), lambda s, f, t: (head_of(f, half, s), 0, 0)
    )
    stack = whole((CHIPS, PACK_ROWS, HEAD_WIDTH))
    grads = whole((CHIPS, 4 * tok, HEAD_WIDTH))
    table_spec = whole((tok, HEAD_WIDTH))
    in_specs = [columns, columns, stack, stack, table_spec, table_spec, whole((tok, RANK))]
    operands = [query, out_grad, mine, other, cosine, sine, low]
    aliases = {}
    if before is not None:
        for out, array in enumerate(before):
            aliases[2 + len(operands)] = out
            operands.append(array)
            in_specs.append(pl.BlockSpec(memory_space=pl.ANY))
    return pl.pallas_call(
        attention_kernel,
        grid_spec=pltpu.PrefetchScalarGridSpec(
            num_scalar_prefetch=2,
            grid=(HALF_KV,),
            in_specs=in_specs,
            out_specs=[columns, terms, grads, grads],
            scratch_shapes=[
                pltpu.VMEM((keys, HEAD_WIDTH), jnp.bfloat16),
                pltpu.VMEM((keys, HEAD_WIDTH), jnp.bfloat16),
                pltpu.VMEM((16, keys), jnp.bfloat16),
                pltpu.VMEM((keys, HEAD_WIDTH), jnp.float32),
                pltpu.VMEM((keys, HEAD_WIDTH), jnp.float32),
            ],
        ),
        out_shape=[
            jax.ShapeDtypeStruct((tok, QUERY_HEADS_HALF * HEAD_WIDTH), jnp.bfloat16),
            jax.ShapeDtypeStruct((PEERS, TERM_ROWS, HEAD_WIDTH), jnp.bfloat16),
            jax.ShapeDtypeStruct((CHIPS, 4 * tok, HEAD_WIDTH), jnp.float32),
            jax.ShapeDtypeStruct((CHIPS, 4 * tok, HEAD_WIDTH), jnp.bfloat16),
        ],
        input_output_aliases=aliases,
        compiler_params=pltpu.CompilerParams(
            dimension_semantics=("arbitrary",), vmem_limit_bytes=VMEM_LIMIT
        ),
        cost_estimate=pl.CostEstimate(
            flops=10 * HALF_KV * wide * keys * HEAD_WIDTH,
            bytes_accessed=6 << 20,
            transcendentals=HALF_KV * wide * keys,
        ),
        name="attention_plain" if half == 0 else "attention_moved",
    )(flags, table, *operands)


def finish_kernel(flags_ref, cos_ref, sin_ref, *refs):
    gk_ref, gv_ref = refs[-2:]
    start = 0
    for half, count in ((0, 1 + CHIPS), (1, 4)):
        keep_ref, pair_ref, *arrived = refs[start : start + count]
        start += count
        total = keep_ref[0] + pair_ref[0].astype(jnp.float32)
        for part in arrived:
            total += part[...].astype(jnp.float32)
        for sub in range(HALF_KV):
            columns = columns_of(head_of(flags_ref, half, sub))
            dk = total[sub * TOK_DEV : (sub + 1) * TOK_DEV] * SCORE_SCALE
            turned = dk * cos_ref[...] + pltpu.roll(dk, HEAD_WIDTH // 2, 1) * sin_ref[...]
            gk_ref[:, columns] = turned.astype(jnp.bfloat16)
            dv = total[(2 + sub) * TOK_DEV : (3 + sub) * TOK_DEV]
            gv_ref[:, columns] = dv.astype(jnp.bfloat16)


def finish(flags, cosine, sine, halves):
    tok = TOK_DEV

    def whole(shape):
        return pl.BlockSpec(shape, lambda i, f: (0,) * len(shape))

    first = whole((1, 4 * tok, HEAD_WIDTH))
    part = whole((4 * tok, HEAD_WIDTH))
    operands, in_specs = [cosine, sine], [whole((tok, HEAD_WIDTH))] * 2
    for keep, from_pair, arrived in halves:
        operands += [keep, from_pair, *arrived]
        in_specs += [first, first] + [part] * len(arrived)
    shape = jax.ShapeDtypeStruct((tok, KEY_VALUE_HEADS * HEAD_WIDTH), jnp.bfloat16)
    return pl.pallas_call(
        finish_kernel,
        grid_spec=pltpu.PrefetchScalarGridSpec(
            num_scalar_prefetch=1,
            grid=(1,),
            in_specs=in_specs,
            out_specs=[whole(shape.shape)] * 2,
        ),
        out_shape=[shape, shape],
        compiler_params=pltpu.CompilerParams(vmem_limit_bytes=VMEM_LIMIT),
        name="finish_keys_values",
    )(flags, *operands)


def exchange(array, axes):
    return lax.all_to_all(array, axes, 0, 0)


def to_all(array, axes):
    count = lax.axis_size(axes)
    return exchange(jnp.broadcast_to(array[None], (count,) + array.shape), axes)


def add_up(array):
    return jnp.sum(array.astype(jnp.float32), axis=0).astype(jnp.bfloat16)


def local(query, keys, values, out_grad, query_lowrank_state, value_lowrank_state, shift_flags):
    ctx_index = lax.axis_index(SEQ_AXES)
    ctx_count = lax.axis_size(SEQ_AXES)
    half_group = GROUP_DEV // 2
    core = ctx_index % 2
    slots = [((ctx_index + half * half_group) % GROUP_DEV) // 2 for half in range(2)]

    def send(array, pairs):
        return lax.ppermute(array, SEQ_AXES, pairs)

    def hop(distance, half, from_slots):
        return [
            (i, (i + 2 * distance) % ctx_count)
            for i in range(ctx_count)
            if ((i + half * half_group) % GROUP_DEV) // 2 in from_slots
        ]

    def back(pairs):
        return [(b, a) for a, b in pairs]

    pair = [(i, i ^ 1) for i in range(ctx_count)]
    plain_hops = [hop(n, 0, range(CHIPS - n)) for n in range(1, CHIPS)]
    side = hop(1, 1, (0, 2))
    cross = hop(2, 1, (0, 1))
    swap = hop(1, 1, (2,)) + hop(-1, 1, (3,))

    half_dim = HEAD_WIDTH // 2
    positions = ctx_index * TOK_DEV + jnp.arange(TOK_DEV, dtype=jnp.int32)
    inv_freq = 10000.0 ** (-(jnp.arange(half_dim, dtype=jnp.float32) * 2.0) / HEAD_WIDTH)
    angles = positions.astype(jnp.float32)[:, None] * inv_freq[None, :]
    cos_half, sin_half = jnp.cos(angles), jnp.sin(angles)
    cosine = jnp.concatenate([cos_half, cos_half], axis=1)
    sine = jnp.concatenate([sin_half, -sin_half], axis=1)
    late = (slots[1] == 2).astype(jnp.int32)
    plain_table = jnp.stack([slots[0] + 1, core] + [0, 1, 2, 3]).astype(jnp.int32)
    moved_table = jnp.stack(
        [slots[1] + 1, core, 0, 1 + late, 2 + late, 3 - 2 * late]
    ).astype(jnp.int32)

    plain, moved = pack(shift_flags, keys[0], values[0], value_lowrank_state[0])
    moved_cross = send(moved, cross)
    moved_side = send(moved, side)
    plain_got = [send(plain, pairs) for pairs in plain_hops]
    plain_got, cosine, sine, plain_table, moved_table = lax.optimization_barrier(
        (plain_got, cosine, sine, plain_table, moved_table)
    )
    plain_mine = jnp.stack([plain, *plain_got])
    plain_other = send(plain_mine, pair)
    low = query_lowrank_state[0]
    gq, terms, plain_keep, plain_send = attention(
        0, shift_flags, plain_table, query[0], out_grad[0], plain_mine, plain_other,
        cosine, sine, low, None,
    )
    moved_swap = send(moved_cross, swap)
    moved_mine = jnp.stack([moved, moved_side, moved_cross, moved_swap])
    moved_other = send(moved_mine, pair)
    plain_from = send(plain_send, pair)
    moved_other, plain_from = lax.optimization_barrier((moved_other, plain_from))
    plain_back = []
    for n in range(1, CHIPS):
        part = (plain_keep[n] + plain_from[n].astype(jnp.float32)).astype(jnp.bfloat16)
        plain_back.append(send(part, back(plain_hops[n - 1])))
    gq, terms, moved_keep, moved_send = attention(
        1, shift_flags, moved_table, query[0], out_grad[0], moved_mine, moved_other,
        cosine, sine, low, (gq, terms),
    )

    moved_from = send(moved_send, pair)
    terms = exchange(terms, "zc")
    terms, moved_from, plain_back = lax.optimization_barrier((terms, moved_from, plain_back))
    terms = add_up(terms)

    def partial(n):
        return moved_keep[n] + moved_from[n].astype(jnp.float32)

    side_back = send(partial(1).astype(jnp.bfloat16), back(side))
    swap_back = send(partial(3).astype(jnp.bfloat16), swap)
    terms = to_all(terms, SUM_AXES)
    terms, side_back, swap_back = lax.optimization_barrier((terms, side_back, swap_back))
    terms = add_up(terms)
    cross_part = (partial(2) + swap_back.astype(jnp.float32)).astype(jnp.bfloat16)
    cross_back = send(cross_part, back(cross))
    terms = to_all(terms, "zc")
    gk, gv = finish(
        shift_flags, cosine, sine,
        [(plain_keep, plain_from, plain_back), (moved_keep, moved_from, [side_back, cross_back])],
    )

    query_terms = terms[:, : 2 * RANK].reshape(QUERY_HEADS_HALF, RANK, HEAD_WIDTH)
    pair_rows = 2 * RANK // PER_GROUP
    value_terms = terms[:, 2 * RANK : 2 * RANK + pair_rows].reshape(
        KEY_VALUE_HEADS, RANK, HEAD_WIDTH
    )

    def wide(heads):
        return jnp.transpose(heads, (1, 0, 2)).reshape(RANK, -1).astype(jnp.float32)

    return gq[None], gk[None], gv[None], wide(query_terms), wide(value_terms)


def solution(mesh):
    dp, ctx = mesh.shape["dp"], mesh.shape["ctx"]
    split = Mesh(mesh.devices.reshape(dp, ctx // PEERS, PEERS), ("dp", "yh", "zc"))
    rows = P("dp", SEQ_AXES, None)
    return jax.shard_map(
        local,
        mesh=split,
        in_specs=(rows,) * 6 + (P(),),
        out_specs=(rows, rows, rows, P(), P()),
        check_vma=False,
    )
```

time: 183 us -> 151 us (0.83)
  the two profiles are of different devices: /device:TPU:40 before, /device:TPU:1 now
where the time goes in v2:
time: 151 us; the launch traced here: 150 us
  starting transfers between devices  73.2 us (48%)
  waiting for transfers between devices  45.5 us (30%)
  Pallas kernels  21.4 us (14%)
  local copies, waits for them, and re-layouts  6.41 us (4%)
  other arithmetic  2.77 us (2%)
    ppermute x16, starting transfers between devices, send(): return lax.ppermute(array, SEQ_AXES, pairs)  51.1 us
    ppermute x16, waiting for transfers between devices, send(): return lax.ppermute(array, SEQ_AXES, pairs)  44.7 us
    all_to_all x3, starting transfers between devices, exchange(): return lax.all_to_all(array, axes, 0, 0)  22.1 us
    pallas_call x2, Pallas kernels, attention(): pl.pallas_call(attention_kernel, grid_spec=pltpu.PrefetchScalarGridSpec(n...  16.7 us
    unnamed x34, local copies, waits for them, and re-layouts  3.62 us
  transfers between devices with their start and end apart: 19, of which 10 were waited for; matrix products, arithmetic and copies ran while one was open for 2% of the time, Pallas kernels for 6%

profile of v2, /device:TPU:1, one launch (start us, length us, event | category | flops | bytes accessed | tf_op | source)
XLA Modules:
  0.0 150.3 jit_solution(10465196482502075145)
XLA Ops:
  2.0 1.8 %pack_heads.1 = (bf16[528,128]{1,0:T(8,128)(2,1)}, bf16[528,128]{1,0:T(8,128)(2,1)}) custom-call(s32[4]{0:T(128)} %flags_ref.7, bf16[128,512]{1,0:T(8,128)(2,1)} %bitcast.61, bf16[128,512]{1,0:T(8,128)(2,1)} %bitcast.62, bf16[128,8]{1,0:T(8,128)(2,1)} %bitcast.60), custom_call_target="tpu_custom_call" | custom-call | tf_op jit(solution)/shard_map/pack_heads/pallas_call | solution.py:63
  3.9 4.8 %collective-permute-start = (bf16[528,128]{1,0:T(8,128)(2,1)}, bf16[528,128]{1,0:T(8,128)(2,1)S(1)}, u32[]{:S(2)}, u32[]{:S(2)}) collective-permute-start(bf16[528,128]{1,0:T(8,128)(2,1)} %get-tuple-element.34), channel_id=1, source_target_pairs={{0,2},{1,3},{2,4},{3,5},{4,6},{5,7},{8,10},{9,11},{10,12},{11,13},... | collective-permute-start | bytes 405512 | tf_op jit(solution)/shard_map/ppermute | solution.py:288
  8.7 5.8 %collective-permute-start.1 = (bf16[528,128]{1,0:T(8,128)(2,1)}, bf16[528,128]{1,0:T(8,128)(2,1)S(1)}, u32[]{:S(2)}, u32[]{:S(2)}) collective-permute-start(bf16[528,128]{1,0:T(8,128)(2,1)} %get-tuple-element.34), channel_id=1, source_target_pairs={{0,4},{1,5},{2,6},{3,7},{8,12},{9,13},{10,14},{11,15},{16,20},{17,... | collective-permute-start | bytes 405512 | tf_op jit(solution)/shard_map/ppermute | solution.py:288
  19.8 3.7 %collective-permute-start.7 = (bf16[4,528,128]{2,1,0:T(8,128)(2,1)S(1)}, bf16[4,528,128]{2,1,0:T(8,128)(2,1)S(1)}, u32[]{:S(2)}, u32[]{:S(2)}) collective-permute-start(bf16[4,528,128]{2,1,0:T(8,128)(2,1)S(1)} %pad_maximum_fusion.1.mine_ref), channel_id=1, source_target_pairs={{0,1},{1,0},{2,3},{3,2},{4,5},{5,4},{6,7},{7,6},{8,9},{9,8},{10,11... | collective-permute-start | bytes 1622024 | tf_op jit(solution)/shard_map/ppermute | solution.py:288
  24.9 4.2 %collective-permute-start.3 = (bf16[528,128]{1,0:T(8,128)(2,1)S(1)}, bf16[528,128]{1,0:T(8,128)(2,1)S(1)}, u32[]{:S(2)}, u32[]{:S(2)}) collective-permute-start(bf16[528,128]{1,0:T(8,128)(2,1)S(1)} %copy-done.6), channel_id=1, source_target_pairs={{0,2},{1,3},{4,6},{5,7},{8,10},{9,11},{12,14},{13,15},{16,18},{17,... | collective-permute-start | bytes 405512 | tf_op jit(solution)/shard_map/ppermute | solution.py:288
  29.1 13.9 %collective-permute-done.4 = bf16[528,128]{1,0:T(8,128)(2,1)S(1)} collective-permute-done((bf16[528,128]{1,0:T(8,128)(2,1)S(1)}, bf16[528,128]{1,0:T(8,128)(2,1)S(1)}, u32[]{:S(2)}, u32[]{:S(2)}) %collective-permute-start.4) | collective-permute-done | bytes 135200 | tf_op jit(solution)/shard_map/ppermute | solution.py:288
  42.9 6.1 %collective-permute-start.5 = (bf16[528,128]{1,0:T(8,128)(2,1)S(1)}, bf16[528,128]{1,0:T(8,128)(2,1)S(1)}, u32[]{:S(2)}, u32[]{:S(2)}) collective-permute-start(bf16[528,128]{1,0:T(8,128)(2,1)S(1)} %collective-permute-done.4), channel_id=1, source_target_pairs={{0,2},{1,3},{8,10},{9,11},{16,18},{17,19},{24,26},{25,27},{2,0},{3... | collective-permute-start | bytes 405512 | tf_op jit(solution)/shard_map/ppermute | solution.py:288
  49.8 2.8 %collective-permute-done.5 = bf16[528,128]{1,0:T(8,128)(2,1)S(1)} collective-permute-done((bf16[528,128]{1,0:T(8,128)(2,1)S(1)}, bf16[528,128]{1,0:T(8,128)(2,1)S(1)}, u32[]{:S(2)}, u32[]{:S(2)}) %collective-permute-start.5) | collective-permute-done | bytes 135200 | tf_op jit(solution)/shard_map/ppermute | solution.py:288
  52.6 2.9 %collective-permute-start.6 = (bf16[4,528,128]{2,1,0:T(8,128)(2,1)S(1)}, bf16[4,528,128]{2,1,0:T(8,128)(2,1)S(1)}, u32[]{:S(2)}, u32[]{:S(2)}) collective-permute-start(bf16[4,528,128]{2,1,0:T(8,128)(2,1)S(1)} %pad_maximum_fusion.mine_ref), channel_id=1, source_target_pairs={{0,1},{1,0},{2,3},{3,2},{4,5},{5,4},{6,7},{7,6},{8,9},{9,8},{10,11... | collective-permute-start | bytes 1622024 | tf_op jit(solution)/shard_map/ppermute | solution.py:288
  56.4 6.4 %attention_plain.1 = (bf16[128,4096]{1,0:T(8,128)(2,1)}, bf16[16,32,128]{2,1,0:T(8,128)(2,1)}, f32[4,512,128]{2,1,0:T(8,128)}, bf16[4,512,128]{2,1,0:T(8,128)(2,1)}) custom-call(s32[4]{0:T(128)} %flags_ref.7, s32[6]{0:T(128)} %stack.57.table_ref, bf16[128,4096]{1,0:T(8,128)(2,1)} %bitcast.66, bf16[128,4096]{1,0:T(8,128)(2,1)} %bitcast.68, ...), custom_call_target="tpu_custom_call" | custom-call | flops 2684354560 | bytes 6291456 | tf_op jit(solution)/shard_map/attention_plain/pallas_call | solution.py:188
  62.8 2.1 %collective-permute-start.8 = (bf16[4,512,128]{2,1,0:T(8,128)(2,1)}, bf16[4,512,128]{2,1,0:T(8,128)(2,1)S(1)}, u32[]{:S(2)}, u32[]{:S(2)}) collective-permute-start(bf16[4,512,128]{2,1,0:T(8,128)(2,1)} %get-tuple-element.43), channel_id=1, source_target_pairs={{0,1},{1,0},{2,3},{3,2},{4,5},{5,4},{6,7},{7,6},{8,9},{9,8},{10,11... | collective-permute-start | bytes 1572872 | tf_op jit(solution)/shard_map/ppermute | solution.py:288
  64.9 1.9 %collective-permute-done.8.refs_1_ = bf16[4,512,128]{2,1,0:T(8,128)(2,1)S(1)} collective-permute-done((bf16[4,512,128]{2,1,0:T(8,128)(2,1)}, bf16[4,512,128]{2,1,0:T(8,128)(2,1)S(1)}, u32[]{:S(2)}, u32[]{:S(2)}) %collective-permute-start.8) | collective-permute-done | bytes 524320 | tf_op jit(solution)/shard_map/ppermute | solution.py:288
  66.8 10.3 %attention_moved.1 = (bf16[128,4096]{1,0:T(8,128)(2,1)}, bf16[16,32,128]{2,1,0:T(8,128)(2,1)}, f32[4,512,128]{2,1,0:T(8,128)}, bf16[4,512,128]{2,1,0:T(8,128)(2,1)}) custom-call(s32[4]{0:T(128)} %flags_ref.7, s32[6]{0:T(128)} %stack.62.table_ref, bf16[128,4096]{1,0:T(8,128)(2,1)} %bitcast.67, ...), custom_call_target="tpu_custom_call", output_to_operand_aliasing={{0}: (9, {}), {1}: (10, {})} | custom-call | flops 2684354560 | bytes 6291456 | tf_op jit(solution)/shard_map/attention_moved/pallas_call | solution.py:188
  77.1 2.1 %collective-permute-start.9 = (bf16[4,512,128]{2,1,0:T(8,128)(2,1)}, bf16[4,512,128]{2,1,0:T(8,128)(2,1)S(1)}, u32[]{:S(2)}, u32[]{:S(2)}) collective-permute-start(bf16[4,512,128]{2,1,0:T(8,128)(2,1)} %get-tuple-element.51), channel_id=1, source_target_pairs={{0,1},{1,0},{2,3},{3,2},{4,5},{5,4},{6,7},{7,6},{8,9},{9,8},{10,11... | collective-permute-start | bytes 1572872 | tf_op jit(solution)/shard_map/ppermute | solution.py:288
  79.1 6.8 %all-to-all-start = ((bf16[16,32,128]{2,1,0:T(8,128)(2,1)}), bf16[16,32,128]{2,1,0:T(8,128)(2,1)S(1)}, u32[]{:S(2)}, u32[]{:S(2)}) async-start(bf16[16,32,128]{2,1,0:T(8,128)(2,1)} %get-tuple-element.50), calls=%async_computation | async-start | bytes 262144 | tf_op jit(solution)/shard_map/all_to_all | solution.py:268
  90.0 4.2 %collective-permute-done.10.refs_2_ = bf16[512,128]{1,0:T(8,128)(2,1)S(1)} collective-permute-done((bf16[512,128]{1,0:T(8,128)(2,1)S(1)}, bf16[512,128]{1,0:T(8,128)(2,1)S(1)}, u32[]{:S(2)}, u32[]{:S(2)}) %collective-permute-start.10) | collective-permute-done | bytes 131104 | tf_op jit(solution)/shard_map/ppermute | solution.py:288
  94.2 8.9 %collective-permute-done.11.refs_3_ = bf16[512,128]{1,0:T(8,128)(2,1)S(1)} collective-permute-done((bf16[512,128]{1,0:T(8,128)(2,1)S(1)}, bf16[512,128]{1,0:T(8,128)(2,1)S(1)}, u32[]{:S(2)}, u32[]{:S(2)}) %collective-permute-start.11) | collective-permute-done | bytes 131104 | tf_op jit(solution)/shard_map/ppermute | solution.py:288
  104.0 6.4 %all-to-all-start.1 = ((bf16[32,32,128]{2,1,0:T(8,128)(2,1)}), bf16[32,32,128]{2,1,0:T(8,128)(2,1)S(1)}, u32[]{:S(2)}, u32[]{:S(2)}) async-start(bf16[32,32,128]{2,1,0:T(8,128)(2,1)} %broadcast_in_dim.11), calls=%async_computation.1 | async-start | bytes 524288 | tf_op jit(solution)/shard_map/all_to_all | solution.py:268
  111.8 4.0 %collective-permute-start.14 = (bf16[512,128]{1,0:T(8,128)(2,1)S(1)}, bf16[512,128]{1,0:T(8,128)(2,1)S(1)}, u32[]{:S(2)}, u32[]{:S(2)}) collective-permute-start(bf16[512,128]{1,0:T(8,128)(2,1)S(1)} %get-tuple-element.63), channel_id=1, source_target_pairs={{0,2},{1,3},{8,10},{9,11},{16,18},{17,19},{24,26},{25,27},{2,0},{3... | collective-permute-start | bytes 393224 | tf_op jit(solution)/shard_map/ppermute | solution.py:288
  116.5 3.3 %collective-permute-done.14 = bf16[512,128]{1,0:T(8,128)(2,1)S(1)} collective-permute-done((bf16[512,128]{1,0:T(8,128)(2,1)S(1)}, bf16[512,128]{1,0:T(8,128)(2,1)S(1)}, u32[]{:S(2)}, u32[]{:S(2)}) %collective-permute-start.14) | collective-permute-done | bytes 131104 | tf_op jit(solution)/shard_map/ppermute | solution.py:288
  121.3 9.0 %all-to-all-start.2 = ((bf16[16,32,128]{2,1,0:T(8,128)(2,1)}), bf16[16,32,128]{2,1,0:T(8,128)(2,1)S(1)}, u32[]{:S(2)}, u32[]{:S(2)}) async-start(bf16[16,32,128]{2,1,0:T(8,128)(2,1)} %broadcast_in_dim.27), calls=%async_computation.2 | async-start | bytes 262144 | tf_op jit(solution)/shard_map/all_to_all | solution.py:268
  130.3 7.5 %collective-permute-start.15 = (bf16[512,128]{1,0:T(8,128)(2,1)S(1)}, bf16[512,128]{1,0:T(8,128)(2,1)S(1)}, u32[]{:S(2)}, u32[]{:S(2)}) collective-permute-start(bf16[512,128]{1,0:T(8,128)(2,1)S(1)} %fusion), channel_id=1, source_target_pairs={{8,4},{9,5},{10,6},{11,7},{16,12},{17,13},{18,14},{19,15},{24,20},... | collective-permute-start | bytes 393224 | tf_op jit(solution)/shard_map/ppermute | solution.py:288
  137.8 7.6 %collective-permute-done.15.refs_8_ = bf16[512,128]{1,0:T(8,128)(2,1)S(1)} collective-permute-done((bf16[512,128]{1,0:T(8,128)(2,1)S(1)}, bf16[512,128]{1,0:T(8,128)(2,1)S(1)}, u32[]{:S(2)}, u32[]{:S(2)}) %collective-permute-start.15) | collective-permute-done | bytes 131104 | tf_op jit(solution)/shard_map/ppermute | solution.py:288
  146.1 2.9 %finish_keys_values.1 = (bf16[128,512]{1,0:T(8,128)(2,1)}, bf16[128,512]{1,0:T(8,128)(2,1)}) custom-call(s32[4]{0:T(128)} %flags_ref.7, f32[128,128]{1,0:T(8,128)} %get-tuple-element.41.refs_0_.cos_ref, f32[128,128]{1,0:T(8,128)} %get-tuple-element.42.refs_1_.sin_ref, f32[4,512,128]{2,1,0:T(8,128)} %get-tuple-element.48.refs_0_, ...), custom_call_target="tpu_custom_call" | custom-call | tf_op jit(solution)/shard_map/finish_keys_values/pallas_call | solution.py:253
  (71 shorter events, 20.0 us)
Async XLA Ops:
  3.9 14.4 %collective-permute-start = (bf16[528,128]{1,0:T(8,128)(2,1)}, bf16[528,128]{1,0:T(8,128)(2,1)S(1)}, u32[]{:S(2)}, u32[]{:S(2)}) collective-permute-start(bf16[528,128]{1,0:T(8,128)(2,1)} %get-tuple-element.34), channel_id=1, source_target_pairs={{0,2},{1,3},{2,4},{3,5},{4,6},{5,7},{8,10},{9,11},{10,12},{11,13},... | collective-permute-start | bytes 405512 | tf_op jit(solution)/shard_map/ppermute | solution.py:288
  8.7 9.6 %collective-permute-start.1 = (bf16[528,128]{1,0:T(8,128)(2,1)}, bf16[528,128]{1,0:T(8,128)(2,1)S(1)}, u32[]{:S(2)}, u32[]{:S(2)}) collective-permute-start(bf16[528,128]{1,0:T(8,128)(2,1)} %get-tuple-element.34), channel_id=1, source_target_pairs={{0,4},{1,5},{2,6},{3,7},{8,12},{9,13},{10,14},{11,15},{16,20},{17,... | collective-permute-start | bytes 405512 | tf_op jit(solution)/shard_map/ppermute | solution.py:288
  14.5 5.2 %collective-permute-start.2 = (bf16[528,128]{1,0:T(8,128)(2,1)}, bf16[528,128]{1,0:T(8,128)(2,1)S(1)}, u32[]{:S(2)}, u32[]{:S(2)}) collective-permute-start(bf16[528,128]{1,0:T(8,128)(2,1)} %get-tuple-element.34), channel_id=1, source_target_pairs={{0,6},{1,7},{8,14},{9,15},{16,22},{17,23},{24,30},{25,31},{32,38},... | collective-permute-start | bytes 405512 | tf_op jit(solution)/shard_map/ppermute | solution.py:288
  19.7 29.3 %copy-start.13 = (bf16[1,128,8]{1,2,0:T(8,128)(2,1)S(1)}, bf16[1,128,8]{1,2,0:T(8,128)(2,1)}, u32[]{:S(2)}) copy-start(bf16[1,128,8]{1,2,0:T(8,128)(2,1)} %param.11) | copy-start | bytes 6148
  19.8 32.8 %copy-start.4 = (bf16[4,528,128]{2,1,0:T(8,128)(2,1)}, bf16[4,528,128]{2,1,0:T(8,128)(2,1)S(1)}, u32[]{:S(2)}) copy-start(bf16[4,528,128]{2,1,0:T(8,128)(2,1)S(1)} %pad_maximum_fusion.1.mine_ref) | copy-start | bytes 1622020
  19.8 35.7 %collective-permute-start.7 = (bf16[4,528,128]{2,1,0:T(8,128)(2,1)S(1)}, bf16[4,528,128]{2,1,0:T(8,128)(2,1)S(1)}, u32[]{:S(2)}, u32[]{:S(2)}) collective-permute-start(bf16[4,528,128]{2,1,0:T(8,128)(2,1)S(1)} %pad_maximum_fusion.1.mine_ref), channel_id=1, source_target_pairs={{0,1},{1,0},{2,3},{3,2},{4,5},{5,4},{6,7},{7,6},{8,9},{9,8},{10,11... | collective-permute-start | bytes 1622024 | tf_op jit(solution)/shard_map/ppermute | solution.py:288
  23.6 19.4 %collective-permute-start.4 = (bf16[528,128]{1,0:T(8,128)(2,1)S(1)}, bf16[528,128]{1,0:T(8,128)(2,1)S(1)}, u32[]{:S(2)}, u32[]{:S(2)}) collective-permute-start(bf16[528,128]{1,0:T(8,128)(2,1)S(1)} %copy-done.6), channel_id=1, source_target_pairs={{4,8},{5,9},{6,10},{7,11},{12,16},{13,17},{14,18},{15,19},{20,24},... | collective-permute-start | bytes 405512 | tf_op jit(solution)/shard_map/ppermute | solution.py:288
  24.9 24.9 %collective-permute-start.3 = (bf16[528,128]{1,0:T(8,128)(2,1)S(1)}, bf16[528,128]{1,0:T(8,128)(2,1)S(1)}, u32[]{:S(2)}, u32[]{:S(2)}) collective-permute-start(bf16[528,128]{1,0:T(8,128)(2,1)S(1)} %copy-done.6), channel_id=1, source_target_pairs={{0,2},{1,3},{4,6},{5,7},{8,10},{9,11},{12,14},{13,15},{16,18},{17,... | collective-permute-start | bytes 405512 | tf_op jit(solution)/shard_map/ppermute | solution.py:288
  42.9 9.6 %collective-permute-start.5 = (bf16[528,128]{1,0:T(8,128)(2,1)S(1)}, bf16[528,128]{1,0:T(8,128)(2,1)S(1)}, u32[]{:S(2)}, u32[]{:S(2)}) collective-permute-start(bf16[528,128]{1,0:T(8,128)(2,1)S(1)} %collective-permute-done.4), channel_id=1, source_target_pairs={{0,2},{1,3},{8,10},{9,11},{16,18},{17,19},{24,26},{25,27},{2,0},{3... | collective-permute-start | bytes 405512 | tf_op jit(solution)/shard_map/ppermute | solution.py:288
  52.6 12.2 %collective-permute-start.6 = (bf16[4,528,128]{2,1,0:T(8,128)(2,1)S(1)}, bf16[4,528,128]{2,1,0:T(8,128)(2,1)S(1)}, u32[]{:S(2)}, u32[]{:S(2)}) collective-permute-start(bf16[4,528,128]{2,1,0:T(8,128)(2,1)S(1)} %pad_maximum_fusion.mine_ref), channel_id=1, source_target_pairs={{0,1},{1,0},{2,3},{3,2},{4,5},{5,4},{6,7},{7,6},{8,9},{9,8},{10,11... | collective-permute-start | bytes 1622024 | tf_op jit(solution)/shard_map/ppermute | solution.py:288
  62.8 4.0 %collective-permute-start.8 = (bf16[4,512,128]{2,1,0:T(8,128)(2,1)}, bf16[4,512,128]{2,1,0:T(8,128)(2,1)S(1)}, u32[]{:S(2)}, u32[]{:S(2)}) collective-permute-start(bf16[4,512,128]{2,1,0:T(8,128)(2,1)} %get-tuple-element.43), channel_id=1, source_target_pairs={{0,1},{1,0},{2,3},{3,2},{4,5},{5,4},{6,7},{7,6},{8,9},{9,8},{10,11... | collective-permute-start | bytes 1572872 | tf_op jit(solution)/shard_map/ppermute | solution.py:288
  66.8 19.1 %copy-start = (f32[4,512,128]{2,1,0:T(8,128)S(1)}, f32[4,512,128]{2,1,0:T(8,128)}, u32[]{:S(2)}) copy-start(f32[4,512,128]{2,1,0:T(8,128)} %get-tuple-element.48.refs_0_) | copy-start | bytes 3145732
  77.1 26.1 %collective-permute-start.9 = (bf16[4,512,128]{2,1,0:T(8,128)(2,1)}, bf16[4,512,128]{2,1,0:T(8,128)(2,1)S(1)}, u32[]{:S(2)}, u32[]{:S(2)}) collective-permute-start(bf16[4,512,128]{2,1,0:T(8,128)(2,1)} %get-tuple-element.51), channel_id=1, source_target_pairs={{0,1},{1,0},{2,3},{3,2},{4,5},{5,4},{6,7},{7,6},{8,9},{9,8},{10,11... | collective-permute-start | bytes 1572872 | tf_op jit(solution)/shard_map/ppermute | solution.py:288
  79.1 24.0 %all-to-all-start = ((bf16[16,32,128]{2,1,0:T(8,128)(2,1)}), bf16[16,32,128]{2,1,0:T(8,128)(2,1)S(1)}, u32[]{:S(2)}, u32[]{:S(2)}) async-start(bf16[16,32,128]{2,1,0:T(8,128)(2,1)} %get-tuple-element.50), calls=%async_computation | async-start | bytes 262144 | tf_op jit(solution)/shard_map/all_to_all | solution.py:268
  85.9 24.5 %copy-start.1 = (f32[4,512,128]{2,1,0:T(8,128)S(1)}, f32[4,512,128]{2,1,0:T(8,128)}, u32[]{:S(2)}) copy-start(f32[4,512,128]{2,1,0:T(8,128)} %get-tuple-element.55.refs_5_) | copy-start | bytes 3145732
  86.0 8.2 %collective-permute-start.10 = (bf16[512,128]{1,0:T(8,128)(2,1)S(1)}, bf16[512,128]{1,0:T(8,128)(2,1)S(1)}, u32[]{:S(2)}, u32[]{:S(2)}) collective-permute-start(bf16[512,128]{1,0:T(8,128)(2,1)S(1)} %get-tuple-element.67), channel_id=1, source_target_pairs={{2,0},{3,1},{4,2},{5,3},{6,4},{7,5},{10,8},{11,9},{12,10},{13,11},... | collective-permute-start | bytes 393224 | tf_op jit(solution)/shard_map/ppermute | solution.py:288
  87.5 15.7 %collective-permute-start.11 = (bf16[512,128]{1,0:T(8,128)(2,1)S(1)}, bf16[512,128]{1,0:T(8,128)(2,1)S(1)}, u32[]{:S(2)}, u32[]{:S(2)}) collective-permute-start(bf16[512,128]{1,0:T(8,128)(2,1)S(1)} %get-tuple-element.66), channel_id=1, source_target_pairs={{4,0},{5,1},{6,2},{7,3},{12,8},{13,9},{14,10},{15,11},{20,16},{21,... | collective-permute-start | bytes 393224 | tf_op jit(solution)/shard_map/ppermute | solution.py:288
  88.8 14.4 %collective-permute-start.12 = (bf16[512,128]{1,0:T(8,128)(2,1)S(1)}, bf16[512,128]{1,0:T(8,128)(2,1)S(1)}, u32[]{:S(2)}, u32[]{:S(2)}) collective-permute-start(bf16[512,128]{1,0:T(8,128)(2,1)S(1)} %get-tuple-element.65), channel_id=1, source_target_pairs={{6,0},{7,1},{14,8},{15,9},{22,16},{23,17},{30,24},{31,25},{38,32},... | collective-permute-start | bytes 393224 | tf_op jit(solution)/shard_map/ppermute | solution.py:288
  103.2 27.1 %copy-start.3 = (bf16[4,512,128]{2,1,0:T(8,128)(2,1)}, bf16[4,512,128]{2,1,0:T(8,128)(2,1)S(1)}, u32[]{:S(2)}) copy-start(bf16[4,512,128]{2,1,0:T(8,128)(2,1)S(1)} %collective-permute-done.9.refs_6_) | copy-start | bytes 1572868
  104.0 16.5 %all-to-all-start.1 = ((bf16[32,32,128]{2,1,0:T(8,128)(2,1)}), bf16[32,32,128]{2,1,0:T(8,128)(2,1)S(1)}, u32[]{:S(2)}, u32[]{:S(2)}) async-start(bf16[32,32,128]{2,1,0:T(8,128)(2,1)} %broadcast_in_dim.11), calls=%async_computation.1 | async-start | bytes 524288 | tf_op jit(solution)/shard_map/all_to_all | solution.py:268
  110.5 6.0 %collective-permute-start.13 = (bf16[512,128]{1,0:T(8,128)(2,1)S(1)}, bf16[512,128]{1,0:T(8,128)(2,1)S(1)}, u32[]{:S(2)}, u32[]{:S(2)}) collective-permute-start(bf16[512,128]{1,0:T(8,128)(2,1)S(1)} %get-tuple-element.64), channel_id=1, source_target_pairs={{2,0},{3,1},{6,4},{7,5},{10,8},{11,9},{14,12},{15,13},{18,16},{19,... | collective-permute-start | bytes 393224 | tf_op jit(solution)/shard_map/ppermute | solution.py:288
  111.8 8.0 %collective-permute-start.14 = (bf16[512,128]{1,0:T(8,128)(2,1)S(1)}, bf16[512,128]{1,0:T(8,128)(2,1)S(1)}, u32[]{:S(2)}, u32[]{:S(2)}) collective-permute-start(bf16[512,128]{1,0:T(8,128)(2,1)S(1)} %get-tuple-element.63), channel_id=1, source_target_pairs={{0,2},{1,3},{8,10},{9,11},{16,18},{17,19},{24,26},{25,27},{2,0},{3... | collective-permute-start | bytes 393224 | tf_op jit(solution)/shard_map/ppermute | solution.py:288
  121.3 27.8 %all-to-all-start.2 = ((bf16[16,32,128]{2,1,0:T(8,128)(2,1)}), bf16[16,32,128]{2,1,0:T(8,128)(2,1)S(1)}, u32[]{:S(2)}, u32[]{:S(2)}) async-start(bf16[16,32,128]{2,1,0:T(8,128)(2,1)} %broadcast_in_dim.27), calls=%async_computation.2 | async-start | bytes 262144 | tf_op jit(solution)/shard_map/all_to_all | solution.py:268
  130.3 15.1 %collective-permute-start.15 = (bf16[512,128]{1,0:T(8,128)(2,1)S(1)}, bf16[512,128]{1,0:T(8,128)(2,1)S(1)}, u32[]{:S(2)}, u32[]{:S(2)}) collective-permute-start(bf16[512,128]{1,0:T(8,128)(2,1)S(1)} %fusion), channel_id=1, source_target_pairs={{8,4},{9,5},{10,6},{11,7},{16,12},{17,13},{18,14},{19,15},{24,20},... | collective-permute-start | bytes 393224 | tf_op jit(solution)/shard_map/ppermute | solution.py:288
  (11 other events, 54.4 us)

commit v3 on v2

v3 whole, which is shorter than its diff:
```python
from functools import partial
import math

import jax
import jax.numpy as jnp
from jax import lax
from jax.experimental import pallas as pl
from jax.experimental.pallas import tpu as pltpu
from jax.sharding import Mesh, PartitionSpec as P

QUERY_HEADS_HALF = 32
KEY_VALUE_HEADS = 4
HEAD_WIDTH = 128
GROUP_DEV = 8
TOK_DEV = 128
HALF_KV = KEY_VALUE_HEADS // 2
PER_GROUP = QUERY_HEADS_HALF // KEY_VALUE_HEADS
RANK = 8
PACK_ROWS = 4 * TOK_DEV + 16
PEERS = 16
TERM_ROWS = 32
TERM_BLOCK = PEERS // KEY_VALUE_HEADS
ADAPTER_SCALE = 2.0
SCORE_SCALE = 1.0 / math.sqrt(HEAD_WIDTH)
EXP2_SCALE = SCORE_SCALE * math.log2(math.e)
MASKED = -1e30
NT = (((1,), (1,)), ((), ()))
TN = (((0,), (0,)), ((), ()))
VMEM_LIMIT = 56 * 1024 * 1024
SEQ_AXES = ("yh", "zc")
SUM_AXES = ("dp", "yh")


def head_of(flags, half, sub):
    hit = [flags[head] == half for head in range(KEY_VALUE_HEADS)]
    low = jnp.where(hit[0], 0, jnp.where(hit[1], 1, 2))
    high = jnp.where(hit[3], 3, jnp.where(hit[2], 2, 1))
    return jnp.where(sub == 0, low, high)


def columns_of(head):
    return pl.ds(pl.multiple_of(head * HEAD_WIDTH, HEAD_WIDTH), HEAD_WIDTH)


def pack_kernel(flags_ref, table_ref, keys_ref, values_ref, low_ref, both_ref, light_ref):
    low = low_ref[...].astype(jnp.float32)
    low = jnp.concatenate([low, jnp.zeros_like(low)], axis=0).astype(jnp.bfloat16)
    for place in range(2):
        half = table_ref[2 + place]
        for sub in range(HALF_KV):
            columns = columns_of(head_of(flags_ref, half, sub))
            for kind, ref in enumerate((keys_ref, values_ref)):
                rows = slice((2 * kind + sub) * TOK_DEV, (2 * kind + sub + 1) * TOK_DEV)
                both_ref[place, rows, :] = ref[:, columns]
                if place == 0:
                    light_ref[rows, :] = ref[:, columns]
        both_ref[place, 4 * TOK_DEV :, :] = low
    light_ref[4 * TOK_DEV :, :] = low


def pack(flags, table, keys, values, low):
    whole = pl.BlockSpec(memory_space=pltpu.VMEM)
    scalars = pl.BlockSpec(memory_space=pltpu.SMEM)
    return pl.pallas_call(
        pack_kernel,
        out_shape=(
            jax.ShapeDtypeStruct((2, PACK_ROWS, HEAD_WIDTH), jnp.bfloat16),
            jax.ShapeDtypeStruct((PACK_ROWS, HEAD_WIDTH), jnp.bfloat16),
        ),
        in_specs=[scalars, scalars, whole, whole, whole],
        out_specs=(whole, whole),
        name="pack_heads",
    )(flags, table, keys, values, low)


def attention_kernel(heavy, flags_ref, table_ref, q_ref, d_ref, *refs):
    chunks = 4 if heavy else 2
    mine, other = refs[:chunks], refs[chunks : 2 * chunks]
    cos_ref, sin_ref, low_ref = refs[2 * chunks : 2 * chunks + 3]
    outs = refs[len(refs) - (11 if heavy else 9) : len(refs) - 5]
    gq_ref, term_ref, keep_ref, send_ref, *swap_refs = outs
    k_all, v_all, low_all, dk_ref, dv_ref = refs[len(refs) - 5 :]
    sub = pl.program_id(0)
    odd, core = table_ref[0], table_ref[1]
    rows = 2 * TOK_DEV
    wide = PER_GROUP * TOK_DEV
    k_rows = pl.ds(pl.multiple_of(sub * TOK_DEV, TOK_DEV), TOK_DEV)
    v_rows = pl.ds(pl.multiple_of((2 + sub) * TOK_DEV, TOK_DEV), TOK_DEV)

    def branch(n):
        for j in range(n):
            for c, side in enumerate((mine[j], other[j])):
                span = slice(j * rows + c * TOK_DEV, j * rows + (c + 1) * TOK_DEV)
                k_all[span, :] = side[0, k_rows, :]
                v_all[span, :] = side[0, v_rows, :]
                low_all[:, span] = side[0, 4 * TOK_DEV :, :]
        width = n * rows
        key = lax.broadcasted_iota(jnp.int32, (rows, wide), 0)
        row = lax.broadcasted_iota(jnp.int32, (rows, wide), 1) % TOK_DEV
        limit = jnp.where(core == 1, rows, 0)
        allowed = (key <= row) | ((key >= TOK_DEV) & (key < limit))

        def stacked(ref):
            return jnp.concatenate(
                [ref[:, h * HEAD_WIDTH : (h + 1) * HEAD_WIDTH] for h in range(PER_GROUP)], axis=0
            )

        q = stacked(q_ref)
        d = stacked(d_ref)
        k = k_all[:width, :]
        s = lax.dot_general(k, q, NT, preferred_element_type=jnp.float32)
        near = jnp.where(allowed, s[:rows], MASKED)
        s = near if n == 1 else jnp.concatenate([near, s[rows:]], axis=0)
        dp = lax.dot_general(v_all[:width, :], d, NT, preferred_element_type=jnp.float32)
        top = jnp.max(s, axis=0, keepdims=True) * EXP2_SCALE
        p = jnp.exp2(s * EXP2_SCALE - top)
        inverse = 1.0 / jnp.sum(p, axis=0, keepdims=True)
        delta = jnp.sum(p * dp, axis=0, keepdims=True) * inverse
        p = p * inverse
        ds = (p * (dp - delta)).astype(jnp.bfloat16)
        dv_ref[:width, :] = jnp.dot(p.astype(jnp.bfloat16), d, preferred_element_type=jnp.float32)
        dk_ref[:width, :] = jnp.dot(ds, q, preferred_element_type=jnp.float32)
        dq = lax.dot_general(ds, k, TN, preferred_element_type=jnp.float32) * SCORE_SCALE
        low_rank = low_ref[...]
        parts = []
        for h in range(PER_GROUP):
            x = dq[h * TOK_DEV : (h + 1) * TOK_DEV, :]
            turned = x * cos_ref[...] + pltpu.roll(x, HEAD_WIDTH // 2, 1) * sin_ref[...]
            low = turned.astype(jnp.bfloat16)
            gq_ref[:, h * HEAD_WIDTH : (h + 1) * HEAD_WIDTH] = low
            parts.append(
                jnp.dot(low_rank, low, preferred_element_type=jnp.float32) * ADAPTER_SCALE
            )
        value_part = (
            jnp.dot(
                low_all[:, :width],
                dv_ref[:width, :].astype(jnp.bfloat16),
                preferred_element_type=jnp.float32,
            )
            * ADAPTER_SCALE
        )
        pair_rows = 2 * RANK // PER_GROUP
        blank = jnp.zeros((2 * RANK - pair_rows, HEAD_WIDTH), jnp.float32)
        for i in range(TERM_BLOCK):
            block = jnp.concatenate(parts[2 * i : 2 * i + 2], axis=0)
            term_ref[i, : 2 * RANK, :] = block.astype(jnp.bfloat16)
            block = jnp.concatenate([value_part[i * pair_rows : (i + 1) * pair_rows], blank], axis=0)
            term_ref[i, 2 * RANK :, :] = block.astype(jnp.bfloat16)

        def store(ref, j, span):
            for grad_ref, to_rows in ((dk_ref, k_rows), (dv_ref, v_rows)):
                if j < n:
                    grad = grad_ref[j * rows + span * TOK_DEV : j * rows + (span + 1) * TOK_DEV, :]
                else:
                    grad = jnp.zeros((TOK_DEV, HEAD_WIDTH), jnp.float32)
                ref[to_rows, :] = grad.astype(ref.dtype)

        kept = (0, 1, 3) if heavy else (0, 1)
        for to, j in enumerate(kept):
            store(keep_ref.at[to], j, 0)
            store(send_ref.at[to], j, 1)
        for span, ref in enumerate(swap_refs):
            store(ref, 2, span)

    base = 3 if heavy else 1
    for more in range(2):
        pl.when(odd == more)(lambda n=base + more: branch(n))


def attention(heavy, flags, table, query, out_grad, mine, other, cosine, sine, low, before):
    tok = TOK_DEV
    wide = PER_GROUP * HEAD_WIDTH
    chunks = len(mine)
    keys = chunks * 2 * tok
    kept = chunks - 1 if heavy else chunks
    place = 1 if heavy else 0

    def whole(shape):
        return pl.BlockSpec(shape, lambda s, f, t: (0,) * len(shape))

    def head(f, t, s):
        return head_of(f, t[2 + place], s)

    columns = pl.BlockSpec((tok, wide), lambda s, f, t: (0, head(f, t, s)))
    terms = pl.BlockSpec((TERM_BLOCK, TERM_ROWS, HEAD_WIDTH), lambda s, f, t: (head(f, t, s), 0, 0))
    table_spec = whole((tok, HEAD_WIDTH))
    in_specs = [columns, columns]
    for array in (*mine, *other):
        at = place if array.shape[0] == 2 else 0
        in_specs.append(
            pl.BlockSpec((1, PACK_ROWS, HEAD_WIDTH), lambda s, f, t, at=at: (at, 0, 0))
        )
    in_specs += [table_spec, table_spec, whole((RANK, tok))]
    operands = [query, out_grad, *mine, *other, cosine, sine, low]
    aliases = {}
    if before is not None:
        for out, array in enumerate(before):
            aliases[2 + len(operands)] = out
            operands.append(array)
            in_specs.append(pl.BlockSpec(memory_space=pl.ANY))
    out_shape = [
        jax.ShapeDtypeStruct((tok, QUERY_HEADS_HALF * HEAD_WIDTH), jnp.bfloat16),
        jax.ShapeDtypeStruct((PEERS, TERM_ROWS, HEAD_WIDTH), jnp.bfloat16),
        jax.ShapeDtypeStruct((kept, 4 * tok, HEAD_WIDTH), jnp.float32),
        jax.ShapeDtypeStruct((kept, 4 * tok, HEAD_WIDTH), jnp.bfloat16),
    ]
    if heavy:
        out_shape += [jax.ShapeDtypeStruct((4 * tok, HEAD_WIDTH), jnp.bfloat16)] * 2
    return pl.pallas_call(
        partial(attention_kernel, heavy),
        grid_spec=pltpu.PrefetchScalarGridSpec(
            num_scalar_prefetch=2,
            grid=(HALF_KV,),
            in_specs=in_specs,
            out_specs=[columns, terms] + [whole(o.shape) for o in out_shape[2:]],
            scratch_shapes=[
                pltpu.VMEM((keys, HEAD_WIDTH), jnp.bfloat16),
                pltpu.VMEM((keys, HEAD_WIDTH), jnp.bfloat16),
                pltpu.VMEM((16, keys), jnp.bfloat16),
                pltpu.VMEM((keys, HEAD_WIDTH), jnp.float32),
                pltpu.VMEM((keys, HEAD_WIDTH), jnp.float32),
            ],
        ),
        out_shape=out_shape,
        input_output_aliases=aliases,
        compiler_params=pltpu.CompilerParams(
            dimension_semantics=("arbitrary",), vmem_limit_bytes=VMEM_LIMIT
        ),
        cost_estimate=pl.CostEstimate(
            flops=10 * HALF_KV * wide * keys * HEAD_WIDTH,
            bytes_accessed=6 << 20,
            transcendentals=HALF_KV * wide * keys,
        ),
        name="attention_heavy" if heavy else "attention_light",
    )(flags, table, *operands)


def finish_kernel(flags_ref, table_ref, cos_ref, sin_ref, *refs):
    light_keep, light_from, heavy_keep, heavy_from, side_ref, cross_ref, gk_ref, gv_ref = refs
    for place, (keep_ref, from_ref) in enumerate(
        ((light_keep, light_from), (heavy_keep, heavy_from))
    ):
        total = keep_ref[0] + from_ref[0].astype(jnp.float32) + side_ref[place].astype(jnp.float32)
        if place == 0:
            total += cross_ref[...].astype(jnp.float32)
        for sub in range(HALF_KV):
            columns = columns_of(head_of(flags_ref, table_ref[2 + place], sub))
            dk = total[sub * TOK_DEV : (sub + 1) * TOK_DEV] * SCORE_SCALE
            turned = dk * cos_ref[...] + pltpu.roll(dk, HEAD_WIDTH // 2, 1) * sin_ref[...]
            gk_ref[:, columns] = turned.astype(jnp.bfloat16)
            dv = total[(2 + sub) * TOK_DEV : (3 + sub) * TOK_DEV]
            gv_ref[:, columns] = dv.astype(jnp.bfloat16)


def finish(flags, table, cosine, sine, kept, side_back, cross_back):
    tok = TOK_DEV

    def whole(shape):
        return pl.BlockSpec(shape, lambda i, f, t: (0,) * len(shape))

    first = whole((1, 4 * tok, HEAD_WIDTH))
    shape = jax.ShapeDtypeStruct((tok, KEY_VALUE_HEADS * HEAD_WIDTH), jnp.bfloat16)
    return pl.pallas_call(
        finish_kernel,
        grid_spec=pltpu.PrefetchScalarGridSpec(
            num_scalar_prefetch=2,
            grid=(1,),
            in_specs=[whole((tok, HEAD_WIDTH))] * 2
            + [first] * 4
            + [whole(side_back.shape), whole(cross_back.shape)],
            out_specs=[whole(shape.shape)] * 2,
        ),
        out_shape=[shape, shape],
        compiler_params=pltpu.CompilerParams(vmem_limit_bytes=VMEM_LIMIT),
        name="finish_keys_values",
    )(flags, table, cosine, sine, *kept, side_back, cross_back)


def exchange(array, axes):
    return lax.all_to_all(array, axes, 0, 0)


def to_all(array, axes):
    count = lax.axis_size(axes)
    return exchange(jnp.broadcast_to(array[None], (count,) + array.shape), axes)


def add_up(array):
    return jnp.sum(array.astype(jnp.float32), axis=0).astype(jnp.bfloat16)


def local(query, keys, values, out_grad, query_lowrank_state, value_lowrank_state, shift_flags):
    ctx_index = lax.axis_index(SEQ_AXES)
    ctx_count = lax.axis_size(SEQ_AXES)

    def send(array, to):
        pairs = [(i, to(i) % ctx_count) for i in range(ctx_count) if to(i) is not None]
        return lax.ppermute(array, SEQ_AXES, pairs)

    def flip(mask):
        return lambda i: i ^ mask

    def to_odd(i):
        return i + 2 if i // 2 % 2 == 0 else None

    def to_even(i):
        return i - 2 if i // 2 % 2 == 1 else None

    chip = ctx_index // 2
    light_half = chip // 2 % 2
    table = jnp.stack([chip % 2, ctx_index % 2, light_half, 1 - light_half]).astype(jnp.int32)

    both, light = pack(shift_flags, table, keys[0], values[0], value_lowrank_state[0].T)
    crossed = send(light, lambda i: i + GROUP_DEV // 2)
    sided = send(both, to_odd)
    both_other = send(both, flip(1))
    sided_other = send(sided, flip(1))
    half_dim = HEAD_WIDTH // 2
    positions = ctx_index * TOK_DEV + jnp.arange(TOK_DEV, dtype=jnp.int32)
    inv_freq = 10000.0 ** (-(jnp.arange(half_dim, dtype=jnp.float32) * 2.0) / HEAD_WIDTH)
    angles = positions.astype(jnp.float32)[:, None] * inv_freq[None, :]
    cos_half, sin_half = jnp.cos(angles), jnp.sin(angles)
    cosine = jnp.concatenate([cos_half, cos_half], axis=1)
    sine = jnp.concatenate([sin_half, -sin_half], axis=1)
    low = query_lowrank_state[0].T
    crossed, sided_other, both_other, cosine, sine, low = lax.optimization_barrier(
        (crossed, sided_other, both_other, cosine, sine, low)
    )
    crossed_other, swapped, swapped_other = (send(crossed, flip(mask)) for mask in (1, 2, 3))
    gq, terms, light_keep, light_send = attention(
        False, shift_flags, table, query[0], out_grad[0], [both, sided], [both_other, sided_other],
        cosine, sine, low, None,
    )
    gq, terms, heavy_keep, heavy_send, swap_keep, swap_send = attention(
        True, shift_flags, table, query[0], out_grad[0],
        [both, crossed[None], swapped[None], sided],
        [both_other, crossed_other[None], swapped_other[None], sided_other],
        cosine, sine, low, (gq, terms),
    )

    light_from = send(light_send, flip(1))
    heavy_from = send(heavy_send, flip(1))
    swap_from = send(swap_keep, flip(2))
    swap_far = send(swap_send, flip(3))
    terms = exchange(terms, "zc")
    terms, light_from, heavy_from, swap_from, swap_far = lax.optimization_barrier(
        (terms, light_from, heavy_from, swap_from, swap_far)
    )

    def wide(array):
        return array.astype(jnp.float32)

    cross_part = heavy_keep[1] + wide(heavy_from[1]) + wide(swap_from) + wide(swap_far)
    side_part = jnp.stack([light_keep[1] + wide(light_from[1]), heavy_keep[2] + wide(heavy_from[2])])
    cross_back = send(cross_part.astype(jnp.bfloat16), lambda i: i - GROUP_DEV // 2)
    side_back = send(side_part.astype(jnp.bfloat16), to_even)
    terms = to_all(add_up(terms), SUM_AXES)
    terms, cross_back, side_back = lax.optimization_barrier((terms, cross_back, side_back))
    gk, gv = finish(
        shift_flags, table, cosine, sine, [light_keep, light_from, heavy_keep, heavy_from],
        side_back, cross_back,
    )
    terms = to_all(add_up(terms), "zc")
    query_terms = terms[:, : 2 * RANK].reshape(QUERY_HEADS_HALF, RANK, HEAD_WIDTH)
    pair_rows = 2 * RANK // PER_GROUP
    value_terms = terms[:, 2 * RANK : 2 * RANK + pair_rows].reshape(
        KEY_VALUE_HEADS, RANK, HEAD_WIDTH
    )

    def rank_rows(heads):
        return wide(jnp.transpose(heads, (1, 0, 2)).reshape(RANK, -1))

    return gq[None], gk[None], gv[None], rank_rows(query_terms), rank_rows(value_terms)


def solution(mesh):
    dp, ctx = mesh.shape["dp"], mesh.shape["ctx"]
    split = Mesh(mesh.devices.reshape(dp, ctx // PEERS, PEERS), ("dp", "yh", "zc"))
    rows = P("dp", SEQ_AXES, None)
    return jax.shard_map(
        local,
        mesh=split,
        in_specs=(rows,) * 6 + (P(),),
        out_specs=(rows, rows, rows, P(), P()),
        check_vma=False,
    )
```

time: 151 us -> 126 us (0.83); the launches traced: 150 us -> 123 us
  waiting for transfers between devices: 45.5 us -> 25.5 us
  local copies, waits for them, and re-layouts: 6.41 us -> 2.85 us
  starting transfers between devices: 73.2 us -> 70 us
    ppermute x16 -> x13, waiting for transfers between devices: 44.7 us -> 19.2 us  [send(): return lax.ppermute(array, SEQ_AXES, pairs)]
    ppermute x16 -> x13, starting transfers between devices: 51.1 us -> 44.5 us  [send(): return lax.ppermute(array, SEQ_AXES, pairs)]
    all_to_all x3, waiting for transfers between devices: 0.75 us -> 6.32 us  [exchange(): return lax.all_to_all(array, axes, 0, 0)]
    all_to_all x3, starting transfers between devices: 22.1 us -> 25.5 us  [exchange(): return lax.all_to_all(array, axes, 0, 0)]
    unnamed x34 -> x32, local copies, waits for them, and re-layouts: 3.62 us -> 1.35 us
  transfers between devices with their start and end apart: 19 -> 16, of which waited for: 10 -> 5; matrix products, arithmetic and copies ran while one was open for 2% -> 1% of each run, Pallas kernels for 6% -> 7%
where the time goes in v3:
time: 126 us; the launch traced here: 123 us
  starting transfers between devices  70 us (56%)
  waiting for transfers between devices  25.5 us (20%)
  Pallas kernels  20.7 us (16%)
  other arithmetic  3.19 us (3%)
  local copies, waits for them, and re-layouts  2.85 us (2%)
    ppermute x13, starting transfers between devices, send(): return lax.ppermute(array, SEQ_AXES, pairs)  44.5 us
    all_to_all x3, starting transfers between devices, exchange(): return lax.all_to_all(array, axes, 0, 0)  25.5 us
    ppermute x13, waiting for transfers between devices, send(): return lax.ppermute(array, SEQ_AXES, pairs)  19.2 us
    pallas_call x2, Pallas kernels, attention(): pl.pallas_call(partial(attention_kernel, heavy), grid_spec=pltpu.Prefetch...  16.1 us
    all_to_all x3, waiting for transfers between devices, exchange(): return lax.all_to_all(array, axes, 0, 0)  6.32 us
    pallas_call x1, Pallas kernels, finish(): pl.pallas_call(finish_kernel, grid_spec=pltpu.PrefetchScalarGridSpec(num_...  2.85 us
  transfers between devices with their start and end apart: 16, of which 5 were waited for; matrix products, arithmetic and copies ran while one was open for 1% of the time, Pallas kernels for 7%

profile of v3, /device:TPU:1, one launch (start us, length us, event | category | flops | bytes accessed | tf_op | source)
XLA Modules:
  0.0 123.3 jit_solution(6068207685013159016)
XLA Ops:
  1.3 1.8 %pack_heads.1 = (bf16[2,528,128]{2,1,0:T(8,128)(2,1)}, bf16[528,128]{1,0:T(8,128)(2,1)}) custom-call(s32[4]{0:T(128)} %flags_ref.7, s32[4]{0:T(128)} %pad_add_fusion.table_ref, bf16[128,512]{1,0:T(8,128)(2,1)} %bitcast.42, bf16[128,512]{1,0:T(8,128)(2,1)} %bitcast.43, bf16[8,128]{1,0:T(8,128)(2,1)} %bitcast.45), custom_call_target="tpu_custom_call" | custom-call | tf_op jit(solution)/shard_map/pack_heads/pallas_call | solution.py:64
  3.1 4.8 %collective-permute-start.1 = (bf16[2,528,128]{2,1,0:T(8,128)(2,1)}, bf16[2,528,128]{2,1,0:T(8,128)(2,1)S(1)}, u32[]{:S(2)}, u32[]{:S(2)}) collective-permute-start(bf16[2,528,128]{2,1,0:T(8,128)(2,1)} %get-tuple-element.33.refs_0_), channel_id=1, source_target_pairs={{0,2},{1,3},{4,6},{5,7},{8,10},{9,11},{12,14},{13,15},{16,18},{17,... | collective-permute-start | bytes 811016 | tf_op jit(solution)/shard_map/ppermute | solution.py:298
  7.9 5.3 %collective-permute-start.3 = (bf16[2,528,128]{2,1,0:T(8,128)(2,1)}, bf16[2,528,128]{2,1,0:T(8,128)(2,1)S(1)}, u32[]{:S(2)}, u32[]{:S(2)}) collective-permute-start(bf16[2,528,128]{2,1,0:T(8,128)(2,1)} %get-tuple-element.33.refs_0_), channel_id=1, source_target_pairs={{0,1},{1,0},{2,3},{3,2},{4,5},{5,4},{6,7},{7,6},{8,9},{9,8},{10,11... | collective-permute-start | bytes 811016 | tf_op jit(solution)/shard_map/ppermute | solution.py:298
  13.2 3.4 %collective-permute-start = (bf16[528,128]{1,0:T(8,128)(2,1)}, bf16[528,128]{1,0:T(8,128)(2,1)S(1)}, u32[]{:S(2)}, u32[]{:S(2)}) collective-permute-start(bf16[528,128]{1,0:T(8,128)(2,1)} %get-tuple-element.34), channel_id=1, source_target_pairs={{0,4},{1,5},{2,6},{3,7},{4,8},{5,9},{6,10},{7,11},{8,12},{9,13},{1... | collective-permute-start | bytes 405512 | tf_op jit(solution)/shard_map/ppermute | solution.py:298
  16.7 2.2 %collective-permute-start.2 = (bf16[2,528,128]{2,1,0:T(8,128)(2,1)S(1)}, bf16[2,528,128]{2,1,0:T(8,128)(2,1)S(1)}, u32[]{:S(2)}, u32[]{:S(2)}) collective-permute-start(bf16[2,528,128]{2,1,0:T(8,128)(2,1)S(1)} %collective-permute-done.1.refs_1_.refs_3_), channel_id=1, source_target_pairs={{0,1},{1,0},{2,3},{3,2},{4,5},{5,4},{6,7},{7,6},{8,9},{9,8},{10,11... | collective-permute-start | bytes 811016 | tf_op jit(solution)/shard_map/ppermute | solution.py:298
  19.9 11.4 %collective-permute-done = bf16[528,128]{1,0:T(8,128)(2,1)S(1)} collective-permute-done((bf16[528,128]{1,0:T(8,128)(2,1)}, bf16[528,128]{1,0:T(8,128)(2,1)S(1)}, u32[]{:S(2)}, u32[]{:S(2)}) %collective-permute-start) | collective-permute-done | bytes 135200 | tf_op jit(solution)/shard_map/ppermute | solution.py:298
  31.4 1.9 %collective-permute-start.6 = (bf16[528,128]{1,0:T(8,128)(2,1)S(1)}, bf16[528,128]{1,0:T(8,128)(2,1)S(1)}, u32[]{:S(2)}, u32[]{:S(2)}) collective-permute-start(bf16[528,128]{1,0:T(8,128)(2,1)S(1)} %collective-permute-done), channel_id=1, source_target_pairs={{0,3},{1,2},{2,1},{3,0},{4,7},{5,6},{6,5},{7,4},{8,11},{9,10},{10,... | collective-permute-start | bytes 405512 | tf_op jit(solution)/shard_map/ppermute | solution.py:298
  33.3 2.6 %collective-permute-start.5 = (bf16[528,128]{1,0:T(8,128)(2,1)S(1)}, bf16[528,128]{1,0:T(8,128)(2,1)S(1)}, u32[]{:S(2)}, u32[]{:S(2)}) collective-permute-start(bf16[528,128]{1,0:T(8,128)(2,1)S(1)} %collective-permute-done), channel_id=1, source_target_pairs={{0,1},{1,0},{2,3},{3,2},{4,5},{5,4},{6,7},{7,6},{8,9},{9,8},{10,11... | collective-permute-start | bytes 405512 | tf_op jit(solution)/shard_map/ppermute | solution.py:298
  35.9 3.3 %collective-permute-start.4 = (bf16[528,128]{1,0:T(8,128)(2,1)S(1)}, bf16[528,128]{1,0:T(8,128)(2,1)S(1)}, u32[]{:S(2)}, u32[]{:S(2)}) collective-permute-start(bf16[528,128]{1,0:T(8,128)(2,1)S(1)} %collective-permute-done), channel_id=1, source_target_pairs={{0,2},{1,3},{2,0},{3,1},{4,6},{5,7},{6,4},{7,5},{8,10},{9,11},{10,... | collective-permute-start | bytes 405512 | tf_op jit(solution)/shard_map/ppermute | solution.py:298
  39.2 5.9 %attention_light.1 = (bf16[128,4096]{1,0:T(8,128)(2,1)}, bf16[16,32,128]{2,1,0:T(8,128)(2,1)}, f32[2,512,128]{2,1,0:T(8,128)}, bf16[2,512,128]{2,1,0:T(8,128)(2,1)}) custom-call(s32[4]{0:T(128)} %flags_ref.7, s32[4]{0:T(128)} %pad_add_fusion.table_ref, bf16[128,4096]{1,0:T(8,128)(2,1)} %bitcast.46, bf16[128,4096]{1,0:T(8,128)(2,1)} %bitcast.48, ...), custom_call_target="tpu_custom_call" | custom-call | flops 1342177280 | bytes 6291456 | tf_op jit(solution)/shard_map/attention_light/pallas_call | solution.py:209
  45.9 10.2 %attention_heavy.1 = (bf16[128,4096]{1,0:T(8,128)(2,1)}, bf16[16,32,128]{2,1,0:T(8,128)(2,1)}, f32[3,512,128]{2,1,0:T(8,128)}, bf16[3,512,128]{2,1,0:T(8,128)(2,...) custom-call(s32[4]{0:T(128)} %flags_ref.7, ...), custom_call_target="tpu_custom_call", output_to_operand_aliasing={{0}: (15, {}), {1}: (16, {})} | custom-call | flops 2684354560 | bytes 6291456 | tf_op jit(solution)/shard_map/attention_heavy/pallas_call | solution.py:209
  56.1 2.7 %collective-permute-start.8 = (bf16[3,512,128]{2,1,0:T(8,128)(2,1)}, bf16[3,512,128]{2,1,0:T(8,128)(2,1)S(1)}, u32[]{:S(2)}, u32[]{:S(2)}) collective-permute-start(bf16[3,512,128]{2,1,0:T(8,128)(2,1)} %get-tuple-element.47), channel_id=1, source_target_pairs={{0,1},{1,0},{2,3},{3,2},{4,5},{5,4},{6,7},{7,6},{8,9},{9,8},{10,11... | collective-permute-start | bytes 1179656 | tf_op jit(solution)/shard_map/ppermute | solution.py:298
  58.9 2.1 %collective-permute-start.7 = (bf16[2,512,128]{2,1,0:T(8,128)(2,1)S(1)}, bf16[2,512,128]{2,1,0:T(8,128)(2,1)S(1)}, u32[]{:S(2)}, u32[]{:S(2)}) collective-permute-start(bf16[2,512,128]{2,1,0:T(8,128)(2,1)S(1)} %copy-done.9), channel_id=1, source_target_pairs={{0,1},{1,0},{2,3},{3,2},{4,5},{5,4},{6,7},{7,6},{8,9},{9,8},{10,11... | collective-permute-start | bytes 786440 | tf_op jit(solution)/shard_map/ppermute | solution.py:298
  60.9 5.4 %all-to-all-start = ((bf16[16,32,128]{2,1,0:T(8,128)(2,1)}), bf16[16,32,128]{2,1,0:T(8,128)(2,1)S(1)}, u32[]{:S(2)}, u32[]{:S(2)}) async-start(bf16[16,32,128]{2,1,0:T(8,128)(2,1)} %get-tuple-element.45), calls=%async_computation | async-start | bytes 262144 | tf_op jit(solution)/shard_map/all_to_all | solution.py:280
  66.4 3.5 %collective-permute-start.9 = (bf16[512,128]{1,0:T(8,128)(2,1)S(1)}, bf16[512,128]{1,0:T(8,128)(2,1)S(1)}, u32[]{:S(2)}, u32[]{:S(2)}) collective-permute-start(bf16[512,128]{1,0:T(8,128)(2,1)S(1)} %copy-done.15), channel_id=1, source_target_pairs={{0,2},{1,3},{2,0},{3,1},{4,6},{5,7},{6,4},{7,5},{8,10},{9,11},{10,... | collective-permute-start | bytes 393224 | tf_op jit(solution)/shard_map/ppermute | solution.py:298
  69.9 2.2 %collective-permute-start.10 = (bf16[512,128]{1,0:T(8,128)(2,1)S(1)}, bf16[512,128]{1,0:T(8,128)(2,1)S(1)}, u32[]{:S(2)}, u32[]{:S(2)}) collective-permute-start(bf16[512,128]{1,0:T(8,128)(2,1)S(1)} %copy-done.14), channel_id=1, source_target_pairs={{0,3},{1,2},{2,1},{3,0},{4,7},{5,6},{6,5},{7,4},{8,11},{9,10},{10,... | collective-permute-start | bytes 393224 | tf_op jit(solution)/shard_map/ppermute | solution.py:298
  72.1 2.5 %collective-permute-done.9 = bf16[512,128]{1,0:T(8,128)(2,1)S(1)} collective-permute-done((bf16[512,128]{1,0:T(8,128)(2,1)S(1)}, bf16[512,128]{1,0:T(8,128)(2,1)S(1)}, u32[]{:S(2)}, u32[]{:S(2)}) %collective-permute-start.9) | collective-permute-done | bytes 131104 | tf_op jit(solution)/shard_map/ppermute | solution.py:298
  74.6 3.2 %collective-permute-done.10 = bf16[512,128]{1,0:T(8,128)(2,1)S(1)} collective-permute-done((bf16[512,128]{1,0:T(8,128)(2,1)S(1)}, bf16[512,128]{1,0:T(8,128)(2,1)S(1)}, u32[]{:S(2)}, u32[]{:S(2)}) %collective-permute-start.10) | collective-permute-done | bytes 131104 | tf_op jit(solution)/shard_map/ppermute | solution.py:298
  78.7 10.5 %all-to-all-start.1 = ((bf16[32,32,128]{2,1,0:T(8,128)(2,1)}), bf16[32,32,128]{2,1,0:T(8,128)(2,1)S(1)}, u32[]{:S(2)}, u32[]{:S(2)}) async-start(bf16[32,32,128]{2,1,0:T(8,128)(2,1)} %broadcast_in_dim.40), calls=%async_computation.1 | async-start | bytes 524288 | tf_op jit(solution)/shard_map/all_to_all | solution.py:280
  90.7 9.3 %collective-permute-start.11 = (bf16[512,128]{1,0:T(8,128)(2,1)S(1)}, bf16[512,128]{1,0:T(8,128)(2,1)S(1)}, u32[]{:S(2)}, u32[]{:S(2)}) collective-permute-start(bf16[512,128]{1,0:T(8,128)(2,1)S(1)} %fusion.1), channel_id=1, source_target_pairs={{0,28},{1,29},{2,30},{3,31},{4,0},{5,1},{6,2},{7,3},{8,4},{9,5},{1... | collective-permute-start | bytes 393224 | tf_op jit(solution)/shard_map/ppermute | solution.py:298
  100.0 2.0 %collective-permute-done.11.refs_5_ = bf16[512,128]{1,0:T(8,128)(2,1)S(1)} collective-permute-done((bf16[512,128]{1,0:T(8,128)(2,1)S(1)}, bf16[512,128]{1,0:T(8,128)(2,1)S(1)}, u32[]{:S(2)}, u32[]{:S(2)}) %collective-permute-start.11) | collective-permute-done | bytes 131104 | tf_op jit(solution)/shard_map/ppermute | solution.py:298
  103.3 9.5 %all-to-all-start.2 = ((bf16[16,32,128]{2,1,0:T(8,128)(2,1)}), bf16[16,32,128]{2,1,0:T(8,128)(2,1)S(1)}, u32[]{:S(2)}, u32[]{:S(2)}) async-start(bf16[16,32,128]{2,1,0:T(8,128)(2,1)} %broadcast_in_dim.43), calls=%async_computation.2 | async-start | bytes 262144 | tf_op jit(solution)/shard_map/all_to_all | solution.py:280
  112.9 2.8 %finish_keys_values.1 = (bf16[128,512]{1,0:T(8,128)(2,1)}, bf16[128,512]{1,0:T(8,128)(2,1)}) custom-call(s32[4]{0:T(128)} %flags_ref.7, s32[4]{0:T(128)} %pad_add_fusion.table_ref, f32[128,128]{1,0:T(8,128)} %get-tuple-element.38.refs_4_.refs_8_.cos_ref, f32[128,128]{1,0:T(8,128)} %get-tuple-element.39.refs_5_.refs_9_.sin_ref, ...), custom_call_target="tpu_custom_call" | custom-call | tf_op jit(solution)/shard_map/finish_keys_values/pallas_call | solution.py:263
  115.7 6.3 %all-to-all-done.2 = bf16[16,32,128]{2,1,0:T(8,128)(2,1)S(1)} async-done(((bf16[16,32,128]{2,1,0:T(8,128)(2,1)}), bf16[16,32,128]{2,1,0:T(8,128)(2,1)S(1)}, u32[]{:S(2)}, u32[]{:S(2)}) %all-to-all-start.2) | async-done | bytes 131104 | tf_op jit(solution)/shard_map/all_to_all | solution.py:280
  (61 shorter events, 7.4 us)
Async XLA Ops:
  3.1 13.6 %collective-permute-start.1 = (bf16[2,528,128]{2,1,0:T(8,128)(2,1)}, bf16[2,528,128]{2,1,0:T(8,128)(2,1)S(1)}, u32[]{:S(2)}, u32[]{:S(2)}) collective-permute-start(bf16[2,528,128]{2,1,0:T(8,128)(2,1)} %get-tuple-element.33.refs_0_), channel_id=1, source_target_pairs={{0,2},{1,3},{4,6},{5,7},{8,10},{9,11},{12,14},{13,15},{16,18},{17,... | collective-permute-start | bytes 811016 | tf_op jit(solution)/shard_map/ppermute | solution.py:298
  7.9 23.5 %collective-permute-start.3 = (bf16[2,528,128]{2,1,0:T(8,128)(2,1)}, bf16[2,528,128]{2,1,0:T(8,128)(2,1)S(1)}, u32[]{:S(2)}, u32[]{:S(2)}) collective-permute-start(bf16[2,528,128]{2,1,0:T(8,128)(2,1)} %get-tuple-element.33.refs_0_), channel_id=1, source_target_pairs={{0,1},{1,0},{2,3},{3,2},{4,5},{5,4},{6,7},{7,6},{8,9},{9,8},{10,11... | collective-permute-start | bytes 811016 | tf_op jit(solution)/shard_map/ppermute | solution.py:298
  13.2 18.2 %collective-permute-start = (bf16[528,128]{1,0:T(8,128)(2,1)}, bf16[528,128]{1,0:T(8,128)(2,1)S(1)}, u32[]{:S(2)}, u32[]{:S(2)}) collective-permute-start(bf16[528,128]{1,0:T(8,128)(2,1)} %get-tuple-element.34), channel_id=1, source_target_pairs={{0,4},{1,5},{2,6},{3,7},{4,8},{5,9},{6,10},{7,11},{8,12},{9,13},{1... | collective-permute-start | bytes 405512 | tf_op jit(solution)/shard_map/ppermute | solution.py:298
  16.6 22.6 %copy-start.6 = (bf16[2,528,128]{2,1,0:T(8,128)(2,1)}, bf16[2,528,128]{2,1,0:T(8,128)(2,1)S(1)}, u32[]{:S(2)}) copy-start(bf16[2,528,128]{2,1,0:T(8,128)(2,1)S(1)} %collective-permute-done.1.refs_1_.refs_3_) | copy-start | bytes 811012
  16.7 14.7 %collective-permute-start.2 = (bf16[2,528,128]{2,1,0:T(8,128)(2,1)S(1)}, bf16[2,528,128]{2,1,0:T(8,128)(2,1)S(1)}, u32[]{:S(2)}, u32[]{:S(2)}) collective-permute-start(bf16[2,528,128]{2,1,0:T(8,128)(2,1)S(1)} %collective-permute-done.1.refs_1_.refs_3_), channel_id=1, source_target_pairs={{0,1},{1,0},{2,3},{3,2},{4,5},{5,4},{6,7},{7,6},{8,9},{9,8},{10,11... | collective-permute-start | bytes 811016 | tf_op jit(solution)/shard_map/ppermute | solution.py:298
  31.4 13.8 %copy-start.10 = (bf16[528,128]{1,0:T(8,128)(2,1)}, bf16[528,128]{1,0:T(8,128)(2,1)S(1)}, u32[]{:S(2)}) copy-start(bf16[528,128]{1,0:T(8,128)(2,1)S(1)} %collective-permute-done) | copy-start | bytes 405508
  31.4 13.8 %collective-permute-start.6 = (bf16[528,128]{1,0:T(8,128)(2,1)S(1)}, bf16[528,128]{1,0:T(8,128)(2,1)S(1)}, u32[]{:S(2)}, u32[]{:S(2)}) collective-permute-start(bf16[528,128]{1,0:T(8,128)(2,1)S(1)} %collective-permute-done), channel_id=1, source_target_pairs={{0,3},{1,2},{2,1},{3,0},{4,7},{5,6},{6,5},{7,4},{8,11},{9,10},{10,... | collective-permute-start | bytes 405512 | tf_op jit(solution)/shard_map/ppermute | solution.py:298
  33.3 11.8 %collective-permute-start.5 = (bf16[528,128]{1,0:T(8,128)(2,1)S(1)}, bf16[528,128]{1,0:T(8,128)(2,1)S(1)}, u32[]{:S(2)}, u32[]{:S(2)}) collective-permute-start(bf16[528,128]{1,0:T(8,128)(2,1)S(1)} %collective-permute-done), channel_id=1, source_target_pairs={{0,1},{1,0},{2,3},{3,2},{4,5},{5,4},{6,7},{7,6},{8,9},{9,8},{10,11... | collective-permute-start | bytes 405512 | tf_op jit(solution)/shard_map/ppermute | solution.py:298
  35.9 9.2 %collective-permute-start.4 = (bf16[528,128]{1,0:T(8,128)(2,1)S(1)}, bf16[528,128]{1,0:T(8,128)(2,1)S(1)}, u32[]{:S(2)}, u32[]{:S(2)}) collective-permute-start(bf16[528,128]{1,0:T(8,128)(2,1)S(1)} %collective-permute-done), channel_id=1, source_target_pairs={{0,2},{1,3},{2,0},{3,1},{4,6},{5,7},{6,4},{7,5},{8,10},{9,11},{10,... | collective-permute-start | bytes 405512 | tf_op jit(solution)/shard_map/ppermute | solution.py:298
  45.9 12.9 %copy-start.9 = (bf16[2,512,128]{2,1,0:T(8,128)(2,1)S(1)}, bf16[2,512,128]{2,1,0:T(8,128)(2,1)}, u32[]{:S(2)}) copy-start(bf16[2,512,128]{2,1,0:T(8,128)(2,1)} %get-tuple-element.46) | copy-start | bytes 786436
  56.1 21.7 %collective-permute-start.8 = (bf16[3,512,128]{2,1,0:T(8,128)(2,1)}, bf16[3,512,128]{2,1,0:T(8,128)(2,1)S(1)}, u32[]{:S(2)}, u32[]{:S(2)}) collective-permute-start(bf16[3,512,128]{2,1,0:T(8,128)(2,1)} %get-tuple-element.47), channel_id=1, source_target_pairs={{0,1},{1,0},{2,3},{3,2},{4,5},{5,4},{6,7},{7,6},{8,9},{9,8},{10,11... | collective-permute-start | bytes 1179656 | tf_op jit(solution)/shard_map/ppermute | solution.py:298
  58.8 11.0 %copy-start.14 = (bf16[512,128]{1,0:T(8,128)(2,1)S(1)}, bf16[512,128]{1,0:T(8,128)(2,1)}, u32[]{:S(2)}) copy-start(bf16[512,128]{1,0:T(8,128)(2,1)} %get-tuple-element.49) | copy-start | bytes 393220
  58.9 13.2 %collective-permute-start.7 = (bf16[2,512,128]{2,1,0:T(8,128)(2,1)S(1)}, bf16[2,512,128]{2,1,0:T(8,128)(2,1)S(1)}, u32[]{:S(2)}, u32[]{:S(2)}) collective-permute-start(bf16[2,512,128]{2,1,0:T(8,128)(2,1)S(1)} %copy-done.9), channel_id=1, source_target_pairs={{0,1},{1,0},{2,3},{3,2},{4,5},{5,4},{6,7},{7,6},{8,9},{9,8},{10,11... | collective-permute-start | bytes 786440 | tf_op jit(solution)/shard_map/ppermute | solution.py:298
  60.9 28.3 %copy-start.1 = (f32[2,512,128]{2,1,0:T(8,128)S(1)}, f32[2,512,128]{2,1,0:T(8,128)}, u32[]{:S(2)}) copy-start(f32[2,512,128]{2,1,0:T(8,128)} %get-tuple-element.44.refs_0_) | copy-start | bytes 1572868
  60.9 16.9 %all-to-all-start = ((bf16[16,32,128]{2,1,0:T(8,128)(2,1)}), bf16[16,32,128]{2,1,0:T(8,128)(2,1)S(1)}, u32[]{:S(2)}, u32[]{:S(2)}) async-start(bf16[16,32,128]{2,1,0:T(8,128)(2,1)} %get-tuple-element.45), calls=%async_computation | async-start | bytes 262144 | tf_op jit(solution)/shard_map/all_to_all | solution.py:280
  66.3 22.9 %copy-start = (f32[3,512,128]{2,1,0:T(8,128)S(1)}, f32[3,512,128]{2,1,0:T(8,128)}, u32[]{:S(2)}) copy-start(f32[3,512,128]{2,1,0:T(8,128)} %get-tuple-element.51.refs_2_) | copy-start | bytes 2359300
  66.4 8.3 %collective-permute-start.9 = (bf16[512,128]{1,0:T(8,128)(2,1)S(1)}, bf16[512,128]{1,0:T(8,128)(2,1)S(1)}, u32[]{:S(2)}, u32[]{:S(2)}) collective-permute-start(bf16[512,128]{1,0:T(8,128)(2,1)S(1)} %copy-done.15), channel_id=1, source_target_pairs={{0,2},{1,3},{2,0},{3,1},{4,6},{5,7},{6,4},{7,5},{8,10},{9,11},{10,... | collective-permute-start | bytes 393224 | tf_op jit(solution)/shard_map/ppermute | solution.py:298
  69.9 8.0 %collective-permute-start.10 = (bf16[512,128]{1,0:T(8,128)(2,1)S(1)}, bf16[512,128]{1,0:T(8,128)(2,1)S(1)}, u32[]{:S(2)}, u32[]{:S(2)}) collective-permute-start(bf16[512,128]{1,0:T(8,128)(2,1)S(1)} %copy-done.14), channel_id=1, source_target_pairs={{0,3},{1,2},{2,1},{3,0},{4,7},{5,6},{6,5},{7,4},{8,11},{9,10},{10,... | collective-permute-start | bytes 393224 | tf_op jit(solution)/shard_map/ppermute | solution.py:298
  72.1 17.1 %copy-start.3 = (bf16[2,512,128]{2,1,0:T(8,128)(2,1)}, bf16[2,512,128]{2,1,0:T(8,128)(2,1)S(1)}, u32[]{:S(2)}) copy-start(bf16[2,512,128]{2,1,0:T(8,128)(2,1)S(1)} %collective-permute-done.7.refs_1_) | copy-start | bytes 786436
  77.8 12.8 %copy-start.2 = (bf16[3,512,128]{2,1,0:T(8,128)(2,1)}, bf16[3,512,128]{2,1,0:T(8,128)(2,1)S(1)}, u32[]{:S(2)}) copy-start(bf16[3,512,128]{2,1,0:T(8,128)(2,1)S(1)} %collective-permute-done.8.refs_3_) | copy-start | bytes 1179652
  78.7 23.3 %all-to-all-start.1 = ((bf16[32,32,128]{2,1,0:T(8,128)(2,1)}), bf16[32,32,128]{2,1,0:T(8,128)(2,1)S(1)}, u32[]{:S(2)}, u32[]{:S(2)}) async-start(bf16[32,32,128]{2,1,0:T(8,128)(2,1)} %broadcast_in_dim.40), calls=%async_computation.1 | async-start | bytes 524288 | tf_op jit(solution)/shard_map/all_to_all | solution.py:280
  89.4 12.7 %collective-permute-start.12 = (bf16[2,512,128]{2,1,0:T(8,128)(2,1)S(1)}, bf16[2,512,128]{2,1,0:T(8,128)(2,1)S(1)}, u32[]{:S(2)}, u32[]{:S(2)}) collective-permute-start(bf16[2,512,128]{2,1,0:T(8,128)(2,1)S(1)} %pad_maximum_fusion), channel_id=1, source_target_pairs={{2,0},{3,1},{6,4},{7,5},{10,8},{11,9},{14,12},{15,13},{18,16},{19,... | collective-permute-start | bytes 786440 | tf_op jit(solution)/shard_map/ppermute | solution.py:298
  90.7 11.3 %collective-permute-start.11 = (bf16[512,128]{1,0:T(8,128)(2,1)S(1)}, bf16[512,128]{1,0:T(8,128)(2,1)S(1)}, u32[]{:S(2)}, u32[]{:S(2)}) collective-permute-start(bf16[512,128]{1,0:T(8,128)(2,1)S(1)} %fusion.1), channel_id=1, source_target_pairs={{0,28},{1,29},{2,30},{3,31},{4,0},{5,1},{6,2},{7,3},{8,4},{9,5},{1... | collective-permute-start | bytes 393224 | tf_op jit(solution)/shard_map/ppermute | solution.py:298
  103.3 18.7 %all-to-all-start.2 = ((bf16[16,32,128]{2,1,0:T(8,128)(2,1)}), bf16[16,32,128]{2,1,0:T(8,128)(2,1)S(1)}, u32[]{:S(2)}, u32[]{:S(2)}) async-start(bf16[16,32,128]{2,1,0:T(8,128)(2,1)} %broadcast_in_dim.43), calls=%async_computation.2 | async-start | bytes 262144 | tf_op jit(solution)/shard_map/all_to_all | solution.py:280
  (8 other events, 27.3 us)

commit v4 on v3

--- a/solution.py
+++ b/solution.py
@@ -17,16 +17,14 @@
 PER_GROUP = QUERY_HEADS_HALF // KEY_VALUE_HEADS
 RANK = 8
 PACK_ROWS = 4 * TOK_DEV + 16
-PEERS = 16
-TERM_ROWS = 32
-TERM_BLOCK = PEERS // KEY_VALUE_HEADS
+TERM_ROWS = 16
 ADAPTER_SCALE = 2.0
 SCORE_SCALE = 1.0 / math.sqrt(HEAD_WIDTH)
 EXP2_SCALE = SCORE_SCALE * math.log2(math.e)
 MASKED = -1e30
 NT = (((1,), (1,)), ((), ()))
 TN = (((0,), (0,)), ((), ()))
-VMEM_LIMIT = 56 * 1024 * 1024
+VMEM_LIMIT = 20 * 1024 * 1024
 SEQ_AXES = ("yh", "zc")
 SUM_AXES = ("dp", "yh")
 
@@ -77,8 +75,7 @@
     chunks = 4 if heavy else 2
     mine, other = refs[:chunks], refs[chunks : 2 * chunks]
     cos_ref, sin_ref, low_ref = refs[2 * chunks : 2 * chunks + 3]
-    outs = refs[len(refs) - (11 if heavy else 9) : len(refs) - 5]
-    gq_ref, term_ref, keep_ref, send_ref, *swap_refs = outs
+    gq_ref, term_ref, keep_ref, send_ref = refs[len(refs) - 9 : len(refs) - 5]
     k_all, v_all, low_all, dk_ref, dv_ref = refs[len(refs) - 5 :]
     sub = pl.program_id(0)
     odd, core = table_ref[0], table_ref[1]
@@ -139,13 +136,10 @@
             )
             * ADAPTER_SCALE
         )
-        pair_rows = 2 * RANK // PER_GROUP
-        blank = jnp.zeros((2 * RANK - pair_rows, HEAD_WIDTH), jnp.float32)
-        for i in range(TERM_BLOCK):
-            block = jnp.concatenate(parts[2 * i : 2 * i + 2], axis=0)
-            term_ref[i, : 2 * RANK, :] = block.astype(jnp.bfloat16)
-            block = jnp.concatenate([value_part[i * pair_rows : (i + 1) * pair_rows], blank], axis=0)
-            term_ref[i, 2 * RANK :, :] = block.astype(jnp.bfloat16)
+        blank = jnp.zeros((TERM_ROWS - RANK - 1, HEAD_WIDTH), jnp.float32)
+        for h in range(PER_GROUP):
+            block = jnp.concatenate([parts[h], value_part[h : h + 1], blank], axis=0)
+            term_ref[h] = block.astype(jnp.bfloat16)
 
         def store(ref, j, span):
             for grad_ref, to_rows in ((dk_ref, k_rows), (dv_ref, v_rows)):
@@ -155,12 +149,9 @@
                     grad = jnp.zeros((TOK_DEV, HEAD_WIDTH), jnp.float32)
                 ref[to_rows, :] = grad.astype(ref.dtype)
 
-        kept = (0, 1, 3) if heavy else (0, 1)
-        for to, j in enumerate(kept):
-            store(keep_ref.at[to], j, 0)
-            store(send_ref.at[to], j, 1)
-        for span, ref in enumerate(swap_refs):
-            store(ref, 2, span)
+        for j in range(chunks):
+            store(keep_ref.at[j], j, 0)
+            store(send_ref.at[j], j, 1)
 
     base = 3 if heavy else 1
     for more in range(2):
@@ -172,7 +163,6 @@
     wide = PER_GROUP * HEAD_WIDTH
     chunks = len(mine)
     keys = chunks * 2 * tok
-    kept = chunks - 1 if heavy else chunks
     place = 1 if heavy else 0
 
     def whole(shape):
@@ -182,16 +172,15 @@
         return head_of(f, t[2 + place], s)
 
     columns = pl.BlockSpec((tok, wide), lambda s, f, t: (0, head(f, t, s)))
-    terms = pl.BlockSpec((TERM_BLOCK, TERM_ROWS, HEAD_WIDTH), lambda s, f, t: (head(f, t, s), 0, 0))
+    terms = pl.BlockSpec((PER_GROUP, TERM_ROWS, HEAD_WIDTH), lambda s, f, t: (head(f, t, s), 0, 0))
     table_spec = whole((tok, HEAD_WIDTH))
     in_specs = [columns, columns]
-    for array in (*mine, *other):
-        at = place if array.shape[0] == 2 else 0
+    for array, at in (*mine, *other):
         in_specs.append(
             pl.BlockSpec((1, PACK_ROWS, HEAD_WIDTH), lambda s, f, t, at=at: (at, 0, 0))
         )
     in_specs += [table_spec, table_spec, whole((RANK, tok))]
-    operands = [query, out_grad, *mine, *other, cosine, sine, low]
+    operands = [query, out_grad, *(array for array, at in (*mine, *other)), cosine, sine, low]
     aliases = {}
     if before is not None:
         for out, array in enumerate(before):
@@ -200,12 +189,10 @@
             in_specs.append(pl.BlockSpec(memory_space=pl.ANY))
     out_shape = [
         jax.ShapeDtypeStruct((tok, QUERY_HEADS_HALF * HEAD_WIDTH), jnp.bfloat16),
-        jax.ShapeDtypeStruct((PEERS, TERM_ROWS, HEAD_WIDTH), jnp.bfloat16),
-        jax.ShapeDtypeStruct((kept, 4 * tok, HEAD_WIDTH), jnp.float32),
-        jax.ShapeDtypeStruct((kept, 4 * tok, HEAD_WIDTH), jnp.bfloat16),
+        jax.ShapeDtypeStruct((QUERY_HEADS_HALF, TERM_ROWS, HEAD_WIDTH), jnp.bfloat16),
+        jax.ShapeDtypeStruct((chunks, 4 * tok, HEAD_WIDTH), jnp.float32),
+        jax.ShapeDtypeStruct((chunks, 4 * tok, HEAD_WIDTH), jnp.bfloat16),
     ]
-    if heavy:
-        out_shape += [jax.ShapeDtypeStruct((4 * tok, HEAD_WIDTH), jnp.bfloat16)] * 2
     return pl.pallas_call(
         partial(attention_kernel, heavy),
         grid_spec=pltpu.PrefetchScalarGridSpec(
@@ -236,7 +223,7 @@
 
 
 def finish_kernel(flags_ref, table_ref, cos_ref, sin_ref, *refs):
-    light_keep, light_from, heavy_keep, heavy_from, side_ref, cross_ref, gk_ref, gv_ref = refs
+    light_keep, heavy_keep, light_from, heavy_from, side_ref, cross_ref, gk_ref, gv_ref = refs
     for place, (keep_ref, from_ref) in enumerate(
         ((light_keep, light_from), (heavy_keep, heavy_from))
     ):
@@ -252,13 +239,15 @@
             gv_ref[:, columns] = dv.astype(jnp.bfloat16)
 
 
-def finish(flags, table, cosine, sine, kept, side_back, cross_back):
+def finish(flags, table, cosine, sine, light_keep, heavy_keep, pair_from, side_back, cross_back):
     tok = TOK_DEV
 
     def whole(shape):
         return pl.BlockSpec(shape, lambda i, f, t: (0,) * len(shape))
 
-    first = whole((1, 4 * tok, HEAD_WIDTH))
+    def block(at):
+        return pl.BlockSpec((1, 4 * tok, HEAD_WIDTH), lambda i, f, t: (at, 0, 0))
+
     shape = jax.ShapeDtypeStruct((tok, KEY_VALUE_HEADS * HEAD_WIDTH), jnp.bfloat16)
     return pl.pallas_call(
         finish_kernel,
@@ -266,14 +255,14 @@
             num_scalar_prefetch=2,
             grid=(1,),
             in_specs=[whole((tok, HEAD_WIDTH))] * 2
-            + [first] * 4
+            + [block(0), block(0), block(0), block(2)]
             + [whole(side_back.shape), whole(cross_back.shape)],
             out_specs=[whole(shape.shape)] * 2,
         ),
         out_shape=[shape, shape],
         compiler_params=pltpu.CompilerParams(vmem_limit_bytes=VMEM_LIMIT),
         name="finish_keys_values",
-    )(flags, table, cosine, sine, *kept, side_back, cross_back)
+    )(flags, table, cosine, sine, light_keep, heavy_keep, pair_from, pair_from, side_back, cross_back)
 
 
 def exchange(array, axes):
@@ -313,8 +302,6 @@
     both, light = pack(shift_flags, table, keys[0], values[0], value_lowrank_state[0].T)
     crossed = send(light, lambda i: i + GROUP_DEV // 2)
     sided = send(both, to_odd)
-    both_other = send(both, flip(1))
-    sided_other = send(sided, flip(1))
     half_dim = HEAD_WIDTH // 2
     positions = ctx_index * TOK_DEV + jnp.arange(TOK_DEV, dtype=jnp.int32)
     inv_freq = 10000.0 ** (-(jnp.arange(half_dim, dtype=jnp.float32) * 2.0) / HEAD_WIDTH)
@@ -323,49 +310,49 @@
     cosine = jnp.concatenate([cos_half, cos_half], axis=1)
     sine = jnp.concatenate([sin_half, -sin_half], axis=1)
     low = query_lowrank_state[0].T
-    crossed, sided_other, both_other, cosine, sine, low = lax.optimization_barrier(
-        (crossed, sided_other, both_other, cosine, sine, low)
-    )
-    crossed_other, swapped, swapped_other = (send(crossed, flip(mask)) for mask in (1, 2, 3))
+    crossed, sided, cosine, sine, low = lax.optimization_barrier(
+        (crossed, sided, cosine, sine, low)
+    )
+    crossed = crossed[None]
+    swapped = send(crossed, flip(2))
+    arrived = send(jnp.concatenate([both, sided, crossed]), flip(1))
+    swapped_other = send(crossed, flip(3))
     gq, terms, light_keep, light_send = attention(
-        False, shift_flags, table, query[0], out_grad[0], [both, sided], [both_other, sided_other],
+        False, shift_flags, table, query[0], out_grad[0],
+        [(both, 0), (sided, 0)], [(arrived, 0), (arrived, 2)],
         cosine, sine, low, None,
     )
-    gq, terms, heavy_keep, heavy_send, swap_keep, swap_send = attention(
+    gq, terms, heavy_keep, heavy_send = attention(
         True, shift_flags, table, query[0], out_grad[0],
-        [both, crossed[None], swapped[None], sided],
-        [both_other, crossed_other[None], swapped_other[None], sided_other],
+        [(both, 1), (crossed, 0), (swapped, 0), (sided, 1)],
+        [(arrived, 1), (arrived, 4), (swapped_other, 0), (arrived, 3)],
         cosine, sine, low, (gq, terms),
-    )
-
-    light_from = send(light_send, flip(1))
-    heavy_from = send(heavy_send, flip(1))
-    swap_from = send(swap_keep, flip(2))
-    swap_far = send(swap_send, flip(3))
-    terms = exchange(terms, "zc")
-    terms, light_from, heavy_from, swap_from, swap_far = lax.optimization_barrier(
-        (terms, light_from, heavy_from, swap_from, swap_far)
     )
 
     def wide(array):
         return array.astype(jnp.float32)
 
-    cross_part = heavy_keep[1] + wide(heavy_from[1]) + wide(swap_from) + wide(swap_far)
-    side_part = jnp.stack([light_keep[1] + wide(light_from[1]), heavy_keep[2] + wide(heavy_from[2])])
-    cross_back = send(cross_part.astype(jnp.bfloat16), lambda i: i - GROUP_DEV // 2)
-    side_back = send(side_part.astype(jnp.bfloat16), to_even)
+    def sent(array):
+        return array.astype(jnp.bfloat16)
+
+    terms = exchange(terms, SUM_AXES)
+    pair_from = send(jnp.concatenate([light_send, heavy_send]), flip(1))
+    swap_from = send(sent(heavy_keep[2] + wide(pair_from[4])), flip(2))
+    terms, pair_from, swap_from = lax.optimization_barrier((terms, pair_from, swap_from))
+    cross_back = send(
+        sent(heavy_keep[1] + wide(pair_from[3]) + wide(swap_from)), lambda i: i - GROUP_DEV // 2
+    )
+    side_back = send(
+        sent(jnp.stack([light_keep[1] + wide(pair_from[1]), heavy_keep[3] + wide(pair_from[5])])),
+        to_even,
+    )
+    terms = to_all(add_up(terms)[: RANK + 1], "zc")
+    gk, gv = finish(
+        shift_flags, table, cosine, sine, light_keep, heavy_keep, pair_from, side_back, cross_back
+    )
     terms = to_all(add_up(terms), SUM_AXES)
-    terms, cross_back, side_back = lax.optimization_barrier((terms, cross_back, side_back))
-    gk, gv = finish(
-        shift_flags, table, cosine, sine, [light_keep, light_from, heavy_keep, heavy_from],
-        side_back, cross_back,
-    )
-    terms = to_all(add_up(terms), "zc")
-    query_terms = terms[:, : 2 * RANK].reshape(QUERY_HEADS_HALF, RANK, HEAD_WIDTH)
-    pair_rows = 2 * RANK // PER_GROUP
-    value_terms = terms[:, 2 * RANK : 2 * RANK + pair_rows].reshape(
-        KEY_VALUE_HEADS, RANK, HEAD_WIDTH
-    )
+    query_terms = terms[:, :RANK]
+    value_terms = terms[:, RANK].reshape(KEY_VALUE_HEADS, RANK, HEAD_WIDTH)
 
     def rank_rows(heads):
         return wide(jnp.transpose(heads, (1, 0, 2)).reshape(RANK, -1))
@@ -375,7 +362,7 @@
 
 def solution(mesh):
     dp, ctx = mesh.shape["dp"], mesh.shape["ctx"]
-    split = Mesh(mesh.devices.reshape(dp, ctx // PEERS, PEERS), ("dp", "yh", "zc"))
+    split = Mesh(mesh.devices.reshape(dp, 2, ctx // 2), ("dp", "yh", "zc"))
     rows = P("dp", SEQ_AXES, None)
     return jax.shard_map(
         local,

time: 126 us -> 109 us (0.87); the launches traced: 123 us -> 109 us
  starting transfers between devices: 70 us -> 61 us
  Pallas kernels: 20.7 us -> 15.7 us
  waiting for transfers between devices: 25.5 us -> 24.2 us
    ppermute x13 -> x9, starting transfers between devices: 44.5 us -> 37.3 us  [send(): return lax.ppermute(array, SEQ_AXES, pairs)]
    ppermute x13 -> x9, waiting for transfers between devices: 19.2 us -> 12.6 us  [send(): return lax.ppermute(array, SEQ_AXES, pairs)]
    all_to_all x3, waiting for transfers between devices: 6.32 us -> 11.6 us  [exchange(): return lax.all_to_all(array, axes, 0, 0)]
    pallas_call x2, Pallas kernels: 16.1 us -> 12.5 us  [attention(): pl.pallas_call(partial(attention_kernel, heavy), grid_spec=pltpu.Prefetch...]
    all_to_all x3, starting transfers between devices: 25.5 us -> 23.8 us  [exchange(): return lax.all_to_all(array, axes, 0, 0)]
    pallas_call x1, Pallas kernels: 2.85 us -> 1.39 us  [finish(): pl.pallas_call(finish_kernel, grid_spec=pltpu.PrefetchScalarGridSpec(num_...]
  transfers between devices with their start and end apart: 16 -> 12, of which waited for: 5 -> 5; matrix products, arithmetic and copies ran while one was open for 1% -> 2% of each run, Pallas kernels for 7% -> 4%
where the time goes in v4:
time: 109 us
  starting transfers between devices  61 us (56%)
  waiting for transfers between devices  24.2 us (22%)
  Pallas kernels  15.7 us (14%)
  other arithmetic  3.55 us (3%)
  local copies, waits for them, and re-layouts  3.19 us (3%)
    ppermute x9, starting transfers between devices, send(): return lax.ppermute(array, SEQ_AXES, pairs)  37.3 us
    all_to_all x3, starting transfers between devices, exchange(): return lax.all_to_all(array, axes, 0, 0)  23.8 us
    ppermute x9, waiting for transfers between devices, send(): return lax.ppermute(array, SEQ_AXES, pairs)  12.6 us
    pallas_call x2, Pallas kernels, attention(): pl.pallas_call(partial(attention_kernel, heavy), grid_spec=pltpu.Prefetch...  12.5 us
    all_to_all x3, waiting for transfers between devices, exchange(): return lax.all_to_all(array, axes, 0, 0)  11.6 us
  transfers between devices with their start and end apart: 12, of which 5 were waited for; matrix products, arithmetic and copies ran while one was open for 2% of the time, Pallas kernels for 4%

profile of v4, /device:TPU:1, one launch (start us, length us, event | category | flops | bytes accessed | tf_op | source)
XLA Modules:
  0.0 108.6 jit_solution(3526396612679800991)
XLA Ops:
  1.3 1.8 %pack_heads.1 = (bf16[2,528,128]{2,1,0:T(8,128)(2,1)}, bf16[528,128]{1,0:T(8,128)(2,1)}) custom-call(s32[4]{0:T(128)} %flags_ref.7, s32[4]{0:T(128)} %pad_add_fusion.table_ref, bf16[128,512]{1,0:T(8,128)(2,1)} %bitcast.44, bf16[128,512]{1,0:T(8,128)(2,1)} %bitcast.45, bf16[8,128]{1,0:T(8,128)(2,1)} %bitcast.48), custom_call_target="tpu_custom_call" | custom-call | tf_op jit(solution)/shard_map/pack_heads/pallas_call | solution.py:62
  3.1 6.6 %collective-permute-start = (bf16[528,128]{1,0:T(8,128)(2,1)}, bf16[528,128]{1,0:T(8,128)(2,1)S(1)}, u32[]{:S(2)}, u32[]{:S(2)}) collective-permute-start(bf16[528,128]{1,0:T(8,128)(2,1)} %get-tuple-element.26), channel_id=1, source_target_pairs={{0,4},{1,5},{2,6},{3,7},{4,8},{5,9},{6,10},{7,11},{8,12},{9,13},{1... | collective-permute-start | bytes 405512 | tf_op jit(solution)/shard_map/ppermute | solution.py:287
  9.7 4.0 %collective-permute-start.1 = (bf16[2,528,128]{2,1,0:T(8,128)(2,1)}, bf16[2,528,128]{2,1,0:T(8,128)(2,1)S(1)}, u32[]{:S(2)}, u32[]{:S(2)}) collective-permute-start(bf16[2,528,128]{2,1,0:T(8,128)(2,1)} %get-tuple-element.25.refs_0_), channel_id=1, source_target_pairs={{0,2},{1,3},{4,6},{5,7},{8,10},{9,11},{12,14},{13,15},{16,18},{17,... | collective-permute-start | bytes 811016 | tf_op jit(solution)/shard_map/ppermute | solution.py:287
  14.2 11.6 %collective-permute-done = bf16[528,128]{1,0:T(8,128)(2,1)S(1)} collective-permute-done((bf16[528,128]{1,0:T(8,128)(2,1)}, bf16[528,128]{1,0:T(8,128)(2,1)S(1)}, u32[]{:S(2)}, u32[]{:S(2)}) %collective-permute-start) | collective-permute-done | bytes 135200 | tf_op jit(solution)/shard_map/ppermute | solution.py:287
  25.9 4.0 %collective-permute-start.3 = (bf16[5,528,128]{2,1,0:T(8,128)(2,1)S(1)}, bf16[5,528,128]{2,1,0:T(8,128)(2,1)S(1)}, u32[]{:S(2)}, u32[]{:S(2)}) collective-permute-start(bf16[5,528,128]{2,1,0:T(8,128)(2,1)S(1)} %pad_maximum_fusion.1), channel_id=1, source_target_pairs={{0,1},{1,0},{2,3},{3,2},{4,5},{5,4},{6,7},{7,6},{8,9},{9,8},{10,11... | collective-permute-start | bytes 2027528 | tf_op jit(solution)/shard_map/ppermute | solution.py:287
  29.9 2.7 %collective-permute-start.4 = (bf16[1,528,128]{2,1,0:T(8,128)(2,1)S(1)}, bf16[1,528,128]{2,1,0:T(8,128)(2,1)S(1)}, u32[]{:S(2)}, u32[]{:S(2)}) collective-permute-start(bf16[1,528,128]{2,1,0:T(8,128)(2,1)S(1)} %bitcast.35), channel_id=1, source_target_pairs={{0,3},{1,2},{2,1},{3,0},{4,7},{5,6},{6,5},{7,4},{8,11},{9,10},{10,... | collective-permute-start | bytes 405512 | tf_op jit(solution)/shard_map/ppermute | solution.py:287
  32.6 2.4 %collective-permute-start.2 = (bf16[1,528,128]{2,1,0:T(8,128)(2,1)S(1)}, bf16[1,528,128]{2,1,0:T(8,128)(2,1)S(1)}, u32[]{:S(2)}, u32[]{:S(2)}) collective-permute-start(bf16[1,528,128]{2,1,0:T(8,128)(2,1)S(1)} %bitcast.36), channel_id=1, source_target_pairs={{0,2},{1,3},{2,0},{3,1},{4,6},{5,7},{6,4},{7,5},{8,10},{9,11},{10,... | collective-permute-start | bytes 405512 | tf_op jit(solution)/shard_map/ppermute | solution.py:287
  35.7 1.2 %copy-done.4 = bf16[1,128,4096]{2,1,0:T(8,128)(2,1)S(1)} copy-done((bf16[1,128,4096]{2,1,0:T(8,128)(2,1)S(1)}, bf16[1,128,4096]{2,1,0:T(8,128)(2,1)}, u32[]{:S(2)}) %copy-start.4) | copy-done | bytes 1048600
  37.0 4.3 %attention_light.1 = (bf16[128,4096]{1,0:T(8,128)(2,1)}, bf16[32,16,128]{2,1,0:T(8,128)(2,1)}, f32[2,512,128]{2,1,0:T(8,128)S(1)}, bf16[2,512,128]{2,1,0:T(8,128)(2,1)S(1)}) custom-call(s32[4]{0:T(128)S(1)} %copy-done.2, s32[4]{0:T(128)S(1)} %copy-done.1, bf16[128,4096]{1,0:T(8,128)(2,1)S(1)} %bitcast.38, bf16[128,4096]{1,0:T(8,128)(2,1)S(1)} %bitcast.40, ...), custom_call_target="tpu_custom_call" | custom-call | flops 1342177280 | bytes 6291456 | tf_op jit(solution)/shard_map/attention_light/pallas_call | solution.py:196
  41.3 8.1 %attention_heavy.1 = (bf16[128,4096]{1,0:T(8,128)(2,1)}, bf16[32,16,128]{2,1,0:T(8,128)(2,1)}, f32[4,512,128]{2,1,0:T(8,128)S(1)}, bf16[4,512,128]{2,1,0:T(8,128)(2,1)S(1)}) custom-call(s32[4]{0:T(128)S(1)} %copy-done.2, s32[4]{0:T(128)S(1)} %copy-done.1, bf16[128,4096]{1,0:T(8,128)(2,1)S(1)} %bitcast.39, ...), custom_call_target="tpu_custom_call", output_to_operand_aliasing={{0}: (15, {}), {1}: (16, {})} | custom-call | flops 2684354560 | bytes 6291456 | tf_op jit(solution)/shard_map/attention_heavy/pallas_call | solution.py:196
  49.5 1.0 pad_maximum_fusion
  50.4 2.7 %collective-permute-start.5 = (bf16[6,512,128]{2,1,0:T(8,128)(2,1)}, bf16[6,512,128]{2,1,0:T(8,128)(2,1)S(1)}, u32[]{:S(2)}, u32[]{:S(2)}) collective-permute-start(bf16[6,512,128]{2,1,0:T(8,128)(2,1)} %pad_maximum_fusion), channel_id=1, source_target_pairs={{0,1},{1,0},{2,3},{3,2},{4,5},{5,4},{6,7},{7,6},{8,9},{9,8},{10,11... | collective-permute-start | bytes 2359304 | tf_op jit(solution)/shard_map/ppermute | solution.py:287
  53.1 6.4 %all-to-all-start = ((bf16[32,16,128]{2,1,0:T(8,128)(2,1)}), bf16[32,16,128]{2,1,0:T(8,128)(2,1)S(1)}, u32[]{:S(2)}, u32[]{:S(2)}) async-start(bf16[32,16,128]{2,1,0:T(8,128)(2,1)} %get-tuple-element.37), calls=%async_computation | async-start | bytes 262144 | tf_op jit(solution)/shard_map/all_to_all | solution.py:269
  59.6 6.8 %collective-permute-start.6 = (bf16[512,128]{1,0:T(8,128)(2,1)S(1)}, bf16[512,128]{1,0:T(8,128)(2,1)S(1)}, u32[]{:S(2)}, u32[]{:S(2)}) collective-permute-start(bf16[512,128]{1,0:T(8,128)(2,1)S(1)} %fusion.1), channel_id=1, source_target_pairs={{0,2},{1,3},{2,0},{3,1},{4,6},{5,7},{6,4},{7,5},{8,10},{9,11},{10,... | collective-permute-start | bytes 393224 | tf_op jit(solution)/shard_map/ppermute | solution.py:287
  66.4 2.6 %all-to-all-done = bf16[32,16,128]{2,1,0:T(8,128)(2,1)S(1)} async-done(((bf16[32,16,128]{2,1,0:T(8,128)(2,1)}), bf16[32,16,128]{2,1,0:T(8,128)(2,1)S(1)}, u32[]{:S(2)}, u32[]{:S(2)}) %all-to-all-start) | async-done | bytes 131104 | tf_op jit(solution)/shard_map/all_to_all | solution.py:269
  69.0 1.0 collective-permute-done.6
  70.7 11.7 %all-to-all-start.1 = ((bf16[16,9,128]{2,1,0:T(8,128)(2,1)}), bf16[16,9,128]{2,1,0:T(8,128)(2,1)S(1)}, u32[]{:S(2)}, u32[]{:S(2)}) async-start(bf16[16,9,128]{2,1,0:T(8,128)(2,1)} %broadcast_in_dim.30), calls=%async_computation.1 | async-start | bytes 131072 | tf_op jit(solution)/shard_map/all_to_all | solution.py:269
  82.4 6.7 %collective-permute-start.8 = (bf16[512,128]{1,0:T(8,128)(2,1)S(1)}, bf16[512,128]{1,0:T(8,128)(2,1)S(1)}, u32[]{:S(2)}, u32[]{:S(2)}) collective-permute-start(bf16[512,128]{1,0:T(8,128)(2,1)S(1)} %fusion), channel_id=1, source_target_pairs={{0,28},{1,29},{2,30},{3,31},{4,0},{5,1},{6,2},{7,3},{8,4},{9,5},{1... | collective-permute-start | bytes 393224 | tf_op jit(solution)/shard_map/ppermute | solution.py:287
  89.2 1.0 all-to-all-done.1
  90.2 0.7 broadcast_in_dim.31
  90.9 5.7 %all-to-all-start.2 = ((bf16[32,9,128]{2,1,0:T(8,128)(2,1)}), bf16[32,9,128]{2,1,0:T(8,128)(2,1)S(1)}, u32[]{:S(2)}, u32[]{:S(2)}) async-start(bf16[32,9,128]{2,1,0:T(8,128)(2,1)} %broadcast_in_dim.31), calls=%async_computation.2 | async-start | bytes 262144 | tf_op jit(solution)/shard_map/all_to_all | solution.py:269
  96.7 1.3 %collective-permute-start.7 = (bf16[2,512,128]{2,1,0:T(8,128)(2,1)S(1)}, bf16[2,512,128]{2,1,0:T(8,128)(2,1)S(1)}, u32[]{:S(2)}, u32[]{:S(2)}) collective-permute-start(bf16[2,512,128]{2,1,0:T(8,128)(2,1)S(1)} %pad_maximum_fusion.2), channel_id=1, source_target_pairs={{2,0},{3,1},{6,4},{7,5},{10,8},{11,9},{14,12},{15,13},{18,16},{19,... | collective-permute-start | bytes 786440 | tf_op jit(solution)/shard_map/ppermute | solution.py:287
  98.0 8.0 %all-to-all-done.2 = bf16[32,9,128]{2,1,0:T(8,128)(2,1)S(1)} async-done(((bf16[32,9,128]{2,1,0:T(8,128)(2,1)}), bf16[32,9,128]{2,1,0:T(8,128)(2,1)S(1)}, u32[]{:S(2)}, u32[]{:S(2)}) %all-to-all-start.2) | async-done | bytes 73760 | tf_op jit(solution)/shard_map/all_to_all | solution.py:269
  107.2 1.4 %finish_keys_values.1 = (bf16[128,512]{1,0:T(8,128)(2,1)}, bf16[128,512]{1,0:T(8,128)(2,1)}) custom-call(s32[4]{0:T(128)S(1)} %copy-done.2, s32[4]{0:T(128)S(1)} %copy-done.1, f32[128,128]{1,0:T(8,128)S(1)} %get-tuple-element.29.refs_4_.refs_8_.cos_ref, f32[128,128]{1,0:T(8,128)S(1)} %get-tuple-element.30.refs_5_.refs_9_.sin_ref, ...), custom_call_target="tpu_custom_call" | custom-call | tf_op jit(solution)/shard_map/finish_keys_values/pallas_call | solution.py:252
  (35 shorter events, 3.9 us)
Async XLA Ops:
  3.1 22.7 %collective-permute-start = (bf16[528,128]{1,0:T(8,128)(2,1)}, bf16[528,128]{1,0:T(8,128)(2,1)S(1)}, u32[]{:S(2)}, u32[]{:S(2)}) collective-permute-start(bf16[528,128]{1,0:T(8,128)(2,1)} %get-tuple-element.26), channel_id=1, source_target_pairs={{0,4},{1,5},{2,6},{3,7},{4,8},{5,9},{6,10},{7,11},{8,12},{9,13},{1... | collective-permute-start | bytes 405512 | tf_op jit(solution)/shard_map/ppermute | solution.py:287
  9.7 16.1 %collective-permute-start.1 = (bf16[2,528,128]{2,1,0:T(8,128)(2,1)}, bf16[2,528,128]{2,1,0:T(8,128)(2,1)S(1)}, u32[]{:S(2)}, u32[]{:S(2)}) collective-permute-start(bf16[2,528,128]{2,1,0:T(8,128)(2,1)} %get-tuple-element.25.refs_0_), channel_id=1, source_target_pairs={{0,2},{1,3},{4,6},{5,7},{8,10},{9,11},{12,14},{13,15},{16,18},{17,... | collective-permute-start | bytes 811016 | tf_op jit(solution)/shard_map/ppermute | solution.py:287
  13.7 12.0 %copy-start = (bf16[2,528,128]{2,1,0:T(8,128)(2,1)S(1)}, bf16[2,528,128]{2,1,0:T(8,128)(2,1)}, u32[]{:S(2)}) copy-start(bf16[2,528,128]{2,1,0:T(8,128)(2,1)} %get-tuple-element.25.refs_0_) | copy-start | bytes 811012
  13.8 21.3 %copy-start.3 = (bf16[1,128,4096]{2,1,0:T(8,128)(2,1)S(1)}, bf16[1,128,4096]{2,1,0:T(8,128)(2,1)}, u32[]{:S(2)}) copy-start(bf16[1,128,4096]{2,1,0:T(8,128)(2,1)} %param.7) | copy-start | bytes 3145732
  25.9 9.2 %copy-start.6 = (bf16[1,128,8]{1,2,0:T(8,128)(2,1)S(1)}, bf16[1,128,8]{1,2,0:T(8,128)(2,1)}, u32[]{:S(2)}) copy-start(bf16[1,128,8]{1,2,0:T(8,128)(2,1)} %param.11) | copy-start | bytes 6148
  25.9 9.2 %collective-permute-start.3 = (bf16[5,528,128]{2,1,0:T(8,128)(2,1)S(1)}, bf16[5,528,128]{2,1,0:T(8,128)(2,1)S(1)}, u32[]{:S(2)}, u32[]{:S(2)}) collective-permute-start(bf16[5,528,128]{2,1,0:T(8,128)(2,1)S(1)} %pad_maximum_fusion.1), channel_id=1, source_target_pairs={{0,1},{1,0},{2,3},{3,2},{4,5},{5,4},{6,7},{7,6},{8,9},{9,8},{10,11... | collective-permute-start | bytes 2027528 | tf_op jit(solution)/shard_map/ppermute | solution.py:287
  29.9 11.4 %collective-permute-start.4 = (bf16[1,528,128]{2,1,0:T(8,128)(2,1)S(1)}, bf16[1,528,128]{2,1,0:T(8,128)(2,1)S(1)}, u32[]{:S(2)}, u32[]{:S(2)}) collective-permute-start(bf16[1,528,128]{2,1,0:T(8,128)(2,1)S(1)} %bitcast.35), channel_id=1, source_target_pairs={{0,3},{1,2},{2,1},{3,0},{4,7},{5,6},{6,5},{7,4},{8,11},{9,10},{10,... | collective-permute-start | bytes 405512 | tf_op jit(solution)/shard_map/ppermute | solution.py:287
  32.6 8.7 %collective-permute-start.2 = (bf16[1,528,128]{2,1,0:T(8,128)(2,1)S(1)}, bf16[1,528,128]{2,1,0:T(8,128)(2,1)S(1)}, u32[]{:S(2)}, u32[]{:S(2)}) collective-permute-start(bf16[1,528,128]{2,1,0:T(8,128)(2,1)S(1)} %bitcast.36), channel_id=1, source_target_pairs={{0,2},{1,3},{2,0},{3,1},{4,6},{5,7},{6,4},{7,5},{8,10},{9,11},{10,... | collective-permute-start | bytes 405512 | tf_op jit(solution)/shard_map/ppermute | solution.py:287
  35.1 0.6 copy-start.1
  35.1 0.7 copy-start.2
  35.7 1.2 %copy-start.4 = (bf16[1,128,4096]{2,1,0:T(8,128)(2,1)S(1)}, bf16[1,128,4096]{2,1,0:T(8,128)(2,1)}, u32[]{:S(2)}) copy-start(bf16[1,128,4096]{2,1,0:T(8,128)(2,1)} %param.10) | copy-start | bytes 3145732
  37.0 4.4 %copy-start.5 = (bf16[1,128,4096]{2,1,0:T(8,128)(2,1)S(1)}, bf16[1,128,4096]{2,1,0:T(8,128)(2,1)}, u32[]{:S(2)}) copy-start(bf16[1,128,4096]{2,1,0:T(8,128)(2,1)} %param.10) | copy-start | bytes 3145732
  50.4 9.1 %collective-permute-start.5 = (bf16[6,512,128]{2,1,0:T(8,128)(2,1)}, bf16[6,512,128]{2,1,0:T(8,128)(2,1)S(1)}, u32[]{:S(2)}, u32[]{:S(2)}) collective-permute-start(bf16[6,512,128]{2,1,0:T(8,128)(2,1)} %pad_maximum_fusion), channel_id=1, source_target_pairs={{0,1},{1,0},{2,3},{3,2},{4,5},{5,4},{6,7},{7,6},{8,9},{9,8},{10,11... | collective-permute-start | bytes 2359304 | tf_op jit(solution)/shard_map/ppermute | solution.py:287
  53.1 15.9 %all-to-all-start = ((bf16[32,16,128]{2,1,0:T(8,128)(2,1)}), bf16[32,16,128]{2,1,0:T(8,128)(2,1)S(1)}, u32[]{:S(2)}, u32[]{:S(2)}) async-start(bf16[32,16,128]{2,1,0:T(8,128)(2,1)} %get-tuple-element.37), calls=%async_computation | async-start | bytes 262144 | tf_op jit(solution)/shard_map/all_to_all | solution.py:269
  59.6 10.5 %collective-permute-start.6 = (bf16[512,128]{1,0:T(8,128)(2,1)S(1)}, bf16[512,128]{1,0:T(8,128)(2,1)S(1)}, u32[]{:S(2)}, u32[]{:S(2)}) collective-permute-start(bf16[512,128]{1,0:T(8,128)(2,1)S(1)} %fusion.1), channel_id=1, source_target_pairs={{0,2},{1,3},{2,0},{3,1},{4,6},{5,7},{6,4},{7,5},{8,10},{9,11},{10,... | collective-permute-start | bytes 393224 | tf_op jit(solution)/shard_map/ppermute | solution.py:287
  70.7 19.5 %all-to-all-start.1 = ((bf16[16,9,128]{2,1,0:T(8,128)(2,1)}), bf16[16,9,128]{2,1,0:T(8,128)(2,1)S(1)}, u32[]{:S(2)}, u32[]{:S(2)}) async-start(bf16[16,9,128]{2,1,0:T(8,128)(2,1)} %broadcast_in_dim.30), calls=%async_computation.1 | async-start | bytes 131072 | tf_op jit(solution)/shard_map/all_to_all | solution.py:269
  82.4 24.8 %collective-permute-start.8 = (bf16[512,128]{1,0:T(8,128)(2,1)S(1)}, bf16[512,128]{1,0:T(8,128)(2,1)S(1)}, u32[]{:S(2)}, u32[]{:S(2)}) collective-permute-start(bf16[512,128]{1,0:T(8,128)(2,1)S(1)} %fusion), channel_id=1, source_target_pairs={{0,28},{1,29},{2,30},{3,31},{4,0},{5,1},{6,2},{7,3},{8,4},{9,5},{1... | collective-permute-start | bytes 393224 | tf_op jit(solution)/shard_map/ppermute | solution.py:287
  90.9 15.1 %all-to-all-start.2 = ((bf16[32,9,128]{2,1,0:T(8,128)(2,1)}), bf16[32,9,128]{2,1,0:T(8,128)(2,1)S(1)}, u32[]{:S(2)}, u32[]{:S(2)}) async-start(bf16[32,9,128]{2,1,0:T(8,128)(2,1)} %broadcast_in_dim.31), calls=%async_computation.2 | async-start | bytes 262144 | tf_op jit(solution)/shard_map/all_to_all | solution.py:269
  96.7 10.6 %collective-permute-start.7 = (bf16[2,512,128]{2,1,0:T(8,128)(2,1)S(1)}, bf16[2,512,128]{2,1,0:T(8,128)(2,1)S(1)}, u32[]{:S(2)}, u32[]{:S(2)}) collective-permute-start(bf16[2,512,128]{2,1,0:T(8,128)(2,1)S(1)} %pad_maximum_fusion.2), channel_id=1, source_target_pairs={{2,0},{3,1},{6,4},{7,5},{10,8},{11,9},{14,12},{15,13},{18,16},{19,... | collective-permute-start | bytes 786440 | tf_op jit(solution)/shard_map/ppermute | solution.py:287

commit v5 on v4

--- a/solution.py
+++ b/solution.py
@@ -71,10 +71,38 @@
     )(flags, table, keys, values, low)
 
 
+def stage_kernel(flags_ref, table_ref, query_ref, out_grad_ref, *outs):
+    for place in range(2):
+        for sub in range(HALF_KV):
+            head = head_of(flags_ref, table_ref[2 + place], sub)
+            for h in range(PER_GROUP):
+                start = (sub * PER_GROUP + h) * TOK_DEV
+                for kind, ref in enumerate((query_ref, out_grad_ref)):
+                    outs[2 * place + kind][start : start + TOK_DEV, :] = ref[
+                        :, columns_of(head * PER_GROUP + h)
+                    ]
+
+
+def stage(flags, table, query, out_grad):
+    whole = pl.BlockSpec(memory_space=pltpu.VMEM)
+    scalars = pl.BlockSpec(memory_space=pltpu.SMEM)
+    shape = jax.ShapeDtypeStruct((HALF_KV * PER_GROUP * TOK_DEV, HEAD_WIDTH), jnp.bfloat16)
+    outs = pl.pallas_call(
+        stage_kernel,
+        out_shape=[shape] * 4,
+        in_specs=[scalars, scalars, whole, whole],
+        out_specs=[whole] * 4,
+        compiler_params=pltpu.CompilerParams(vmem_limit_bytes=VMEM_LIMIT),
+        name="stage_rows",
+    )(flags, table, query, out_grad)
+    return outs[:2], outs[2:]
+
+
 def attention_kernel(heavy, flags_ref, table_ref, q_ref, d_ref, *refs):
     chunks = 4 if heavy else 2
     mine, other = refs[:chunks], refs[chunks : 2 * chunks]
     cos_ref, sin_ref, low_ref = refs[2 * chunks : 2 * chunks + 3]
+    before_ref = refs[2 * chunks + 3] if heavy else None
     gq_ref, term_ref, keep_ref, send_ref = refs[len(refs) - 9 : len(refs) - 5]
     k_all, v_all, low_all, dk_ref, dv_ref = refs[len(refs) - 5 :]
     sub = pl.program_id(0)
@@ -97,13 +125,8 @@
         limit = jnp.where(core == 1, rows, 0)
         allowed = (key <= row) | ((key >= TOK_DEV) & (key < limit))
 
-        def stacked(ref):
-            return jnp.concatenate(
-                [ref[:, h * HEAD_WIDTH : (h + 1) * HEAD_WIDTH] for h in range(PER_GROUP)], axis=0
-            )
-
-        q = stacked(q_ref)
-        d = stacked(d_ref)
+        q = q_ref[...]
+        d = d_ref[...]
         k = k_all[:width, :]
         s = lax.dot_general(k, q, NT, preferred_element_type=jnp.float32)
         near = jnp.where(allowed, s[:rows], MASKED)
@@ -149,16 +172,23 @@
                     grad = jnp.zeros((TOK_DEV, HEAD_WIDTH), jnp.float32)
                 ref[to_rows, :] = grad.astype(ref.dtype)
 
+        first = 2 if heavy else 0
         for j in range(chunks):
             store(keep_ref.at[j], j, 0)
-            store(send_ref.at[j], j, 1)
+            store(send_ref.at[first + j], j, 1)
+
+    if heavy:
+
+        @pl.when(sub == 0)
+        def _():
+            send_ref[:2] = before_ref[...]
 
     base = 3 if heavy else 1
     for more in range(2):
         pl.when(odd == more)(lambda n=base + more: branch(n))
 
 
-def attention(heavy, flags, table, query, out_grad, mine, other, cosine, sine, low, before):
+def attention(heavy, flags, table, rows, mine, other, cosine, sine, low, before):
     tok = TOK_DEV
     wide = PER_GROUP * HEAD_WIDTH
     chunks = len(mine)
@@ -174,15 +204,19 @@
     columns = pl.BlockSpec((tok, wide), lambda s, f, t: (0, head(f, t, s)))
     terms = pl.BlockSpec((PER_GROUP, TERM_ROWS, HEAD_WIDTH), lambda s, f, t: (head(f, t, s), 0, 0))
     table_spec = whole((tok, HEAD_WIDTH))
-    in_specs = [columns, columns]
+    stacked = pl.BlockSpec((wide, HEAD_WIDTH), lambda s, f, t: (s, 0))
+    in_specs = [stacked, stacked]
     for array, at in (*mine, *other):
         in_specs.append(
             pl.BlockSpec((1, PACK_ROWS, HEAD_WIDTH), lambda s, f, t, at=at: (at, 0, 0))
         )
     in_specs += [table_spec, table_spec, whole((RANK, tok))]
-    operands = [query, out_grad, *(array for array, at in (*mine, *other)), cosine, sine, low]
+    operands = [*rows, *(array for array, at in (*mine, *other)), cosine, sine, low]
     aliases = {}
-    if before is not None:
+    if heavy:
+        *before, light_send = before
+        operands.append(light_send)
+        in_specs.append(whole(light_send.shape))
         for out, array in enumerate(before):
             aliases[2 + len(operands)] = out
             operands.append(array)
@@ -191,7 +225,7 @@
         jax.ShapeDtypeStruct((tok, QUERY_HEADS_HALF * HEAD_WIDTH), jnp.bfloat16),
         jax.ShapeDtypeStruct((QUERY_HEADS_HALF, TERM_ROWS, HEAD_WIDTH), jnp.bfloat16),
         jax.ShapeDtypeStruct((chunks, 4 * tok, HEAD_WIDTH), jnp.float32),
-        jax.ShapeDtypeStruct((chunks, 4 * tok, HEAD_WIDTH), jnp.bfloat16),
+        jax.ShapeDtypeStruct((6 if heavy else 2, 4 * tok, HEAD_WIDTH), jnp.bfloat16),
     ]
     return pl.pallas_call(
         partial(attention_kernel, heavy),
@@ -310,23 +344,24 @@
     cosine = jnp.concatenate([cos_half, cos_half], axis=1)
     sine = jnp.concatenate([sin_half, -sin_half], axis=1)
     low = query_lowrank_state[0].T
-    crossed, sided, cosine, sine, low = lax.optimization_barrier(
-        (crossed, sided, cosine, sine, low)
+    light_rows, heavy_rows = stage(shift_flags, table, query[0], out_grad[0])
+    crossed, sided, cosine, sine, low, light_rows, heavy_rows = lax.optimization_barrier(
+        (crossed, sided, cosine, sine, low, light_rows, heavy_rows)
     )
     crossed = crossed[None]
     swapped = send(crossed, flip(2))
     arrived = send(jnp.concatenate([both, sided, crossed]), flip(1))
     swapped_other = send(crossed, flip(3))
     gq, terms, light_keep, light_send = attention(
-        False, shift_flags, table, query[0], out_grad[0],
+        False, shift_flags, table, light_rows,
         [(both, 0), (sided, 0)], [(arrived, 0), (arrived, 2)],
         cosine, sine, low, None,
     )
-    gq, terms, heavy_keep, heavy_send = attention(
-        True, shift_flags, table, query[0], out_grad[0],
+    gq, terms, heavy_keep, pair_send = attention(
+        True, shift_flags, table, heavy_rows,
         [(both, 1), (crossed, 0), (swapped, 0), (sided, 1)],
         [(arrived, 1), (arrived, 4), (swapped_other, 0), (arrived, 3)],
-        cosine, sine, low, (gq, terms),
+        cosine, sine, low, (gq, terms, light_send),
     )
 
     def wide(array):
@@ -336,7 +371,7 @@
         return array.astype(jnp.bfloat16)
 
     terms = exchange(terms, SUM_AXES)
-    pair_from = send(jnp.concatenate([light_send, heavy_send]), flip(1))
+    pair_from = send(pair_send, flip(1))
     swap_from = send(sent(heavy_keep[2] + wide(pair_from[4])), flip(2))
     terms, pair_from, swap_from = lax.optimization_barrier((terms, pair_from, swap_from))
     cross_back = send(

time: 109 us -> 107 us (0.982)
  waiting for transfers between devices: 24.2 us -> 20 us
  local copies, waits for them, and re-layouts: 3.19 us -> 4.43 us
  Pallas kernels: 15.7 us -> 16.9 us
    ppermute x9, waiting for transfers between devices: 12.6 us -> 7.6 us  [send(): return lax.ppermute(array, SEQ_AXES, pairs)]
    unnamed x14 -> x12, local copies, waits for them, and re-layouts: 1.88 us -> 3.11 us
    pallas_call x0 -> x1, Pallas kernels: none -> 1.09 us  [stage(): pl.pallas_call(stage_kernel, out_shape=[shape] * 4, in_specs=[scalars, sc...]
  transfers between devices with their start and end apart: 12 -> 12, of which waited for: 5 -> 5; matrix products, arithmetic and copies ran while one was open for 2% -> 2% of each run, Pallas kernels for 4% -> 5%
where the time goes in v5:
time: 107 us; the launch traced here: 106 us
  starting transfers between devices  61.1 us (57%)
  waiting for transfers between devices  20 us (19%)
  Pallas kernels  16.9 us (16%)
  local copies, waits for them, and re-layouts  4.43 us (4%)
  other arithmetic  2.59 us (2%)
    ppermute x9, starting transfers between devices, send(): return lax.ppermute(array, SEQ_AXES, pairs)  36.9 us
    all_to_all x3, starting transfers between devices, exchange(): return lax.all_to_all(array, axes, 0, 0)  24.2 us
    pallas_call x2, Pallas kernels, attention(): pl.pallas_call(partial(attention_kernel, heavy), grid_spec=pltpu.Prefetch...  12.6 us
    all_to_all x3, waiting for transfers between devices, exchange(): return lax.all_to_all(array, axes, 0, 0)  12.4 us
    ppermute x9, waiting for transfers between devices, send(): return lax.ppermute(array, SEQ_AXES, pairs)  7.6 us
    unnamed x12, local copies, waits for them, and re-layouts  3.11 us
  transfers between devices with their start and end apart: 12, of which 5 were waited for; matrix products, arithmetic and copies ran while one was open for 2% of the time, Pallas kernels for 5%

profile of v5, /device:TPU:1, one launch (start us, length us, event | category | flops | bytes accessed | tf_op | source)
XLA Modules:
  0.0 105.9 jit_solution(1716023702745548750)
XLA Ops:
  1.3 1.8 %pack_heads.1 = (bf16[2,528,128]{2,1,0:T(8,128)(2,1)}, bf16[528,128]{1,0:T(8,128)(2,1)}) custom-call(s32[4]{0:T(128)} %flags_ref.9, s32[4]{0:T(128)} %pad_add_fusion.table_ref, bf16[128,512]{1,0:T(8,128)(2,1)} %bitcast.42, bf16[128,512]{1,0:T(8,128)(2,1)} %bitcast.43, bf16[8,128]{1,0:T(8,128)(2,1)} %bitcast.46), custom_call_target="tpu_custom_call" | custom-call | tf_op jit(solution)/shard_map/pack_heads/pallas_call | solution.py:62
  3.1 6.6 %collective-permute-start = (bf16[528,128]{1,0:T(8,128)(2,1)}, bf16[528,128]{1,0:T(8,128)(2,1)S(1)}, u32[]{:S(2)}, u32[]{:S(2)}) collective-permute-start(bf16[528,128]{1,0:T(8,128)(2,1)} %get-tuple-element.33), channel_id=1, source_target_pairs={{0,4},{1,5},{2,6},{3,7},{4,8},{5,9},{6,10},{7,11},{8,12},{9,13},{1... | collective-permute-start | bytes 405512 | tf_op jit(solution)/shard_map/ppermute | solution.py:321
  9.7 4.0 %collective-permute-start.1 = (bf16[2,528,128]{2,1,0:T(8,128)(2,1)}, bf16[2,528,128]{2,1,0:T(8,128)(2,1)S(1)}, u32[]{:S(2)}, u32[]{:S(2)}) collective-permute-start(bf16[2,528,128]{2,1,0:T(8,128)(2,1)} %get-tuple-element.34.refs_0_), channel_id=1, source_target_pairs={{0,2},{1,3},{4,6},{5,7},{8,10},{9,11},{12,14},{13,15},{16,18},{17,... | collective-permute-start | bytes 811016 | tf_op jit(solution)/shard_map/ppermute | solution.py:321
  14.7 1.2 %copy-done = bf16[1,128,4096]{2,1,0:T(8,128)(2,1)S(1)} copy-done((bf16[1,128,4096]{2,1,0:T(8,128)(2,1)S(1)}, bf16[1,128,4096]{2,1,0:T(8,128)(2,1)}, u32[]{:S(2)}) %copy-start) | copy-done | bytes 1048600
  16.0 1.2 %copy-done.1 = bf16[1,128,4096]{2,1,0:T(8,128)(2,1)S(1)} copy-done((bf16[1,128,4096]{2,1,0:T(8,128)(2,1)S(1)}, bf16[1,128,4096]{2,1,0:T(8,128)(2,1)}, u32[]{:S(2)}) %copy-start.1) | copy-done | bytes 1048600
  17.2 1.1 %stage_rows.1 = (bf16[2048,128]{1,0:T(8,128)(2,1)S(1)}, bf16[2048,128]{1,0:T(8,128)(2,1)S(1)}, bf16[2048,128]{1,0:T(8,128)(2,1)S(1)}, bf16[2048,128]{1,0:T(8,128)(2,1)S(1)}) custom-call(s32[4]{0:T(128)S(1)} %copy-done.4, s32[4]{0:T(128)S(1)} %copy-done.3, bf16[128,4096]{1,0:T(8,128)(2,1)S(1)} %bitcast.34, bf16[128,4096]{1,0:T(8,128)(2,1)S(1)} %bitcast.35), custom_call_target="tpu_custom_call" | custom-call | tf_op jit(solution)/shard_map/stage_rows/pallas_call | solution.py:90
  18.4 7.4 %collective-permute-done = bf16[528,128]{1,0:T(8,128)(2,1)S(1)} collective-permute-done((bf16[528,128]{1,0:T(8,128)(2,1)}, bf16[528,128]{1,0:T(8,128)(2,1)S(1)}, u32[]{:S(2)}, u32[]{:S(2)}) %collective-permute-start) | collective-permute-done | bytes 135200 | tf_op jit(solution)/shard_map/ppermute | solution.py:321
  25.9 4.0 %collective-permute-start.3 = (bf16[5,528,128]{2,1,0:T(8,128)(2,1)S(1)}, bf16[5,528,128]{2,1,0:T(8,128)(2,1)S(1)}, u32[]{:S(2)}, u32[]{:S(2)}) collective-permute-start(bf16[5,528,128]{2,1,0:T(8,128)(2,1)S(1)} %pad_maximum_fusion), channel_id=1, source_target_pairs={{0,1},{1,0},{2,3},{3,2},{4,5},{5,4},{6,7},{7,6},{8,9},{9,8},{10,11... | collective-permute-start | bytes 2027528 | tf_op jit(solution)/shard_map/ppermute | solution.py:321
  29.9 2.7 %collective-permute-start.4 = (bf16[1,528,128]{2,1,0:T(8,128)(2,1)S(1)}, bf16[1,528,128]{2,1,0:T(8,128)(2,1)S(1)}, u32[]{:S(2)}, u32[]{:S(2)}) collective-permute-start(bf16[1,528,128]{2,1,0:T(8,128)(2,1)S(1)} %bitcast.37), channel_id=1, source_target_pairs={{0,3},{1,2},{2,1},{3,0},{4,7},{5,6},{6,5},{7,4},{8,11},{9,10},{10,... | collective-permute-start | bytes 405512 | tf_op jit(solution)/shard_map/ppermute | solution.py:321
  32.6 2.4 %collective-permute-start.2 = (bf16[1,528,128]{2,1,0:T(8,128)(2,1)S(1)}, bf16[1,528,128]{2,1,0:T(8,128)(2,1)S(1)}, u32[]{:S(2)}, u32[]{:S(2)}) collective-permute-start(bf16[1,528,128]{2,1,0:T(8,128)(2,1)S(1)} %bitcast.38), channel_id=1, source_target_pairs={{0,2},{1,3},{2,0},{3,1},{4,6},{5,7},{6,4},{7,5},{8,10},{9,11},{10,... | collective-permute-start | bytes 405512 | tf_op jit(solution)/shard_map/ppermute | solution.py:321
  35.1 4.2 %attention_light.1 = (bf16[128,4096]{1,0:T(8,128)(2,1)}, bf16[32,16,128]{2,1,0:T(8,128)(2,1)}, f32[2,512,128]{2,1,0:T(8,128)S(1)}, bf16[2,512,128]{2,1,0:T(8,128)(2,1)S(1)}) custom-call(s32[4]{0:T(128)S(1)} %copy-done.4, s32[4]{0:T(128)S(1)} %copy-done.3, bf16[2048,128]{1,0:T(8,128)(2,1)S(1)} %get-tuple-element.46.q_ref, ...), custom_call_target="tpu_custom_call" | custom-call | flops 1342177280 | bytes 6291456 | tf_op jit(solution)/shard_map/attention_light/pallas_call | solution.py:230
  39.3 8.3 %attention_heavy.1 = (bf16[128,4096]{1,0:T(8,128)(2,1)}, bf16[32,16,128]{2,1,0:T(8,128)(2,1)}, f32[4,512,128]{2,1,0:T(8,128)S(1)}, bf16[6,512,128]{2,1,0:T(8,128)(2,1)}) custom-call(s32[4]{0:T(128)S(1)} %copy-done.4, s32[4]{0:T(128)S(1)} %copy-done.3, bf16[2048,128]{1,0:T(8,128)(2,1)S(1)} %get-tuple-element.39.q_ref, ...), custom_call_target="tpu_custom_call", output_to_operand_aliasing={{0}: (16, {}), {1}: (17, {})} | custom-call | flops 2684354560 | bytes 6291456 | tf_op jit(solution)/shard_map/attention_heavy/pallas_call | solution.py:230
  47.7 3.1 %collective-permute-start.5 = (bf16[6,512,128]{2,1,0:T(8,128)(2,1)}, bf16[6,512,128]{2,1,0:T(8,128)(2,1)S(1)}, u32[]{:S(2)}, u32[]{:S(2)}) collective-permute-start(bf16[6,512,128]{2,1,0:T(8,128)(2,1)} %get-tuple-element.55), channel_id=1, source_target_pairs={{0,1},{1,0},{2,3},{3,2},{4,5},{5,4},{6,7},{7,6},{8,9},{9,8},{10,11... | collective-permute-start | bytes 2359304 | tf_op jit(solution)/shard_map/ppermute | solution.py:321
  50.8 6.9 %all-to-all-start = ((bf16[32,16,128]{2,1,0:T(8,128)(2,1)}), bf16[32,16,128]{2,1,0:T(8,128)(2,1)S(1)}, u32[]{:S(2)}, u32[]{:S(2)}) async-start(bf16[32,16,128]{2,1,0:T(8,128)(2,1)} %get-tuple-element.54), calls=%async_computation | async-start | bytes 262144 | tf_op jit(solution)/shard_map/all_to_all | solution.py:303
  57.7 6.0 %collective-permute-start.6 = (bf16[512,128]{1,0:T(8,128)(2,1)S(1)}, bf16[512,128]{1,0:T(8,128)(2,1)S(1)}, u32[]{:S(2)}, u32[]{:S(2)}) collective-permute-start(bf16[512,128]{1,0:T(8,128)(2,1)S(1)} %fusion.1), channel_id=1, source_target_pairs={{0,2},{1,3},{2,0},{3,1},{4,6},{5,7},{6,4},{7,5},{8,10},{9,11},{10,... | collective-permute-start | bytes 393224 | tf_op jit(solution)/shard_map/ppermute | solution.py:321
  63.7 3.4 %all-to-all-done = bf16[32,16,128]{2,1,0:T(8,128)(2,1)S(1)} async-done(((bf16[32,16,128]{2,1,0:T(8,128)(2,1)}), bf16[32,16,128]{2,1,0:T(8,128)(2,1)S(1)}, u32[]{:S(2)}, u32[]{:S(2)}) %all-to-all-start) | async-done | bytes 131104 | tf_op jit(solution)/shard_map/all_to_all | solution.py:303
  68.0 11.7 %all-to-all-start.1 = ((bf16[16,9,128]{2,1,0:T(8,128)(2,1)}), bf16[16,9,128]{2,1,0:T(8,128)(2,1)S(1)}, u32[]{:S(2)}, u32[]{:S(2)}) async-start(bf16[16,9,128]{2,1,0:T(8,128)(2,1)} %broadcast_in_dim.30), calls=%async_computation.1 | async-start | bytes 131072 | tf_op jit(solution)/shard_map/all_to_all | solution.py:303
  79.8 6.7 %collective-permute-start.8 = (bf16[512,128]{1,0:T(8,128)(2,1)S(1)}, bf16[512,128]{1,0:T(8,128)(2,1)S(1)}, u32[]{:S(2)}, u32[]{:S(2)}) collective-permute-start(bf16[512,128]{1,0:T(8,128)(2,1)S(1)} %fusion), channel_id=1, source_target_pairs={{0,28},{1,29},{2,30},{3,31},{4,0},{5,1},{6,2},{7,3},{8,4},{9,5},{1... | collective-permute-start | bytes 393224 | tf_op jit(solution)/shard_map/ppermute | solution.py:321
  86.5 1.0 all-to-all-done.1
  87.5 0.7 broadcast_in_dim.31
  88.2 5.7 %all-to-all-start.2 = ((bf16[32,9,128]{2,1,0:T(8,128)(2,1)}), bf16[32,9,128]{2,1,0:T(8,128)(2,1)S(1)}, u32[]{:S(2)}, u32[]{:S(2)}) async-start(bf16[32,9,128]{2,1,0:T(8,128)(2,1)} %broadcast_in_dim.31), calls=%async_computation.2 | async-start | bytes 262144 | tf_op jit(solution)/shard_map/all_to_all | solution.py:303
  94.0 1.3 %collective-permute-start.7 = (bf16[2,512,128]{2,1,0:T(8,128)(2,1)S(1)}, bf16[2,512,128]{2,1,0:T(8,128)(2,1)S(1)}, u32[]{:S(2)}, u32[]{:S(2)}) collective-permute-start(bf16[2,512,128]{2,1,0:T(8,128)(2,1)S(1)} %pad_maximum_fusion.1), channel_id=1, source_target_pairs={{2,0},{3,1},{6,4},{7,5},{10,8},{11,9},{14,12},{15,13},{18,16},{19,... | collective-permute-start | bytes 786440 | tf_op jit(solution)/shard_map/ppermute | solution.py:321
  95.3 8.0 %all-to-all-done.2 = bf16[32,9,128]{2,1,0:T(8,128)(2,1)S(1)} async-done(((bf16[32,9,128]{2,1,0:T(8,128)(2,1)}), bf16[32,9,128]{2,1,0:T(8,128)(2,1)S(1)}, u32[]{:S(2)}, u32[]{:S(2)}) %all-to-all-start.2) | async-done | bytes 73760 | tf_op jit(solution)/shard_map/all_to_all | solution.py:303
  104.6 1.4 %finish_keys_values.1 = (bf16[128,512]{1,0:T(8,128)(2,1)}, bf16[128,512]{1,0:T(8,128)(2,1)}) custom-call(s32[4]{0:T(128)S(1)} %copy-done.4, s32[4]{0:T(128)S(1)} %copy-done.3, f32[128,128]{1,0:T(8,128)S(1)} %get-tuple-element.43.refs_4_.refs_8_.cos_ref, f32[128,128]{1,0:T(8,128)S(1)} %get-tuple-element.44.refs_5_.refs_9_.sin_ref, ...), custom_call_target="tpu_custom_call" | custom-call | tf_op jit(solution)/shard_map/finish_keys_values/pallas_call | solution.py:286
  (33 shorter events, 4.1 us)
Async XLA Ops:
  3.1 22.7 %collective-permute-start = (bf16[528,128]{1,0:T(8,128)(2,1)}, bf16[528,128]{1,0:T(8,128)(2,1)S(1)}, u32[]{:S(2)}, u32[]{:S(2)}) collective-permute-start(bf16[528,128]{1,0:T(8,128)(2,1)} %get-tuple-element.33), channel_id=1, source_target_pairs={{0,4},{1,5},{2,6},{3,7},{4,8},{5,9},{6,10},{7,11},{8,12},{9,13},{1... | collective-permute-start | bytes 405512 | tf_op jit(solution)/shard_map/ppermute | solution.py:321
  9.7 16.1 %collective-permute-start.1 = (bf16[2,528,128]{2,1,0:T(8,128)(2,1)}, bf16[2,528,128]{2,1,0:T(8,128)(2,1)S(1)}, u32[]{:S(2)}, u32[]{:S(2)}) collective-permute-start(bf16[2,528,128]{2,1,0:T(8,128)(2,1)} %get-tuple-element.34.refs_0_), channel_id=1, source_target_pairs={{0,2},{1,3},{4,6},{5,7},{8,10},{9,11},{12,14},{13,15},{16,18},{17,... | collective-permute-start | bytes 811016 | tf_op jit(solution)/shard_map/ppermute | solution.py:321
  14.1 0.6 copy-start.3
  14.1 0.7 copy-start.4
  14.7 1.2 %copy-start = (bf16[1,128,4096]{2,1,0:T(8,128)(2,1)S(1)}, bf16[1,128,4096]{2,1,0:T(8,128)(2,1)}, u32[]{:S(2)}) copy-start(bf16[1,128,4096]{2,1,0:T(8,128)(2,1)} %param.7) | copy-start | bytes 3145732
  16.0 1.2 %copy-start.1 = (bf16[1,128,4096]{2,1,0:T(8,128)(2,1)S(1)}, bf16[1,128,4096]{2,1,0:T(8,128)(2,1)}, u32[]{:S(2)}) copy-start(bf16[1,128,4096]{2,1,0:T(8,128)(2,1)} %param.10) | copy-start | bytes 3145732
  18.3 7.5 %copy-start.2 = (bf16[2,528,128]{2,1,0:T(8,128)(2,1)S(1)}, bf16[2,528,128]{2,1,0:T(8,128)(2,1)}, u32[]{:S(2)}) copy-start(bf16[2,528,128]{2,1,0:T(8,128)(2,1)} %get-tuple-element.34.refs_0_) | copy-start | bytes 811012
  25.8 9.3 %copy-start.5 = (bf16[1,128,8]{1,2,0:T(8,128)(2,1)S(1)}, bf16[1,128,8]{1,2,0:T(8,128)(2,1)}, u32[]{:S(2)}) copy-start(bf16[1,128,8]{1,2,0:T(8,128)(2,1)} %param.11) | copy-start | bytes 6148
  25.9 9.2 %collective-permute-start.3 = (bf16[5,528,128]{2,1,0:T(8,128)(2,1)S(1)}, bf16[5,528,128]{2,1,0:T(8,128)(2,1)S(1)}, u32[]{:S(2)}, u32[]{:S(2)}) collective-permute-start(bf16[5,528,128]{2,1,0:T(8,128)(2,1)S(1)} %pad_maximum_fusion), channel_id=1, source_target_pairs={{0,1},{1,0},{2,3},{3,2},{4,5},{5,4},{6,7},{7,6},{8,9},{9,8},{10,11... | collective-permute-start | bytes 2027528 | tf_op jit(solution)/shard_map/ppermute | solution.py:321
  29.9 9.5 %collective-permute-start.4 = (bf16[1,528,128]{2,1,0:T(8,128)(2,1)S(1)}, bf16[1,528,128]{2,1,0:T(8,128)(2,1)S(1)}, u32[]{:S(2)}, u32[]{:S(2)}) collective-permute-start(bf16[1,528,128]{2,1,0:T(8,128)(2,1)S(1)} %bitcast.37), channel_id=1, source_target_pairs={{0,3},{1,2},{2,1},{3,0},{4,7},{5,6},{6,5},{7,4},{8,11},{9,10},{10,... | collective-permute-start | bytes 405512 | tf_op jit(solution)/shard_map/ppermute | solution.py:321
  32.6 6.7 %collective-permute-start.2 = (bf16[1,528,128]{2,1,0:T(8,128)(2,1)S(1)}, bf16[1,528,128]{2,1,0:T(8,128)(2,1)S(1)}, u32[]{:S(2)}, u32[]{:S(2)}) collective-permute-start(bf16[1,528,128]{2,1,0:T(8,128)(2,1)S(1)} %bitcast.38), channel_id=1, source_target_pairs={{0,2},{1,3},{2,0},{3,1},{4,6},{5,7},{6,4},{7,5},{8,10},{9,11},{10,... | collective-permute-start | bytes 405512 | tf_op jit(solution)/shard_map/ppermute | solution.py:321
  47.7 10.0 %collective-permute-start.5 = (bf16[6,512,128]{2,1,0:T(8,128)(2,1)}, bf16[6,512,128]{2,1,0:T(8,128)(2,1)S(1)}, u32[]{:S(2)}, u32[]{:S(2)}) collective-permute-start(bf16[6,512,128]{2,1,0:T(8,128)(2,1)} %get-tuple-element.55), channel_id=1, source_target_pairs={{0,1},{1,0},{2,3},{3,2},{4,5},{5,4},{6,7},{7,6},{8,9},{9,8},{10,11... | collective-permute-start | bytes 2359304 | tf_op jit(solution)/shard_map/ppermute | solution.py:321
  50.8 16.4 %all-to-all-start = ((bf16[32,16,128]{2,1,0:T(8,128)(2,1)}), bf16[32,16,128]{2,1,0:T(8,128)(2,1)S(1)}, u32[]{:S(2)}, u32[]{:S(2)}) async-start(bf16[32,16,128]{2,1,0:T(8,128)(2,1)} %get-tuple-element.54), calls=%async_computation | async-start | bytes 262144 | tf_op jit(solution)/shard_map/all_to_all | solution.py:303
  57.7 9.7 %collective-permute-start.6 = (bf16[512,128]{1,0:T(8,128)(2,1)S(1)}, bf16[512,128]{1,0:T(8,128)(2,1)S(1)}, u32[]{:S(2)}, u32[]{:S(2)}) collective-permute-start(bf16[512,128]{1,0:T(8,128)(2,1)S(1)} %fusion.1), channel_id=1, source_target_pairs={{0,2},{1,3},{2,0},{3,1},{4,6},{5,7},{6,4},{7,5},{8,10},{9,11},{10,... | collective-permute-start | bytes 393224 | tf_op jit(solution)/shard_map/ppermute | solution.py:321
  68.0 19.5 %all-to-all-start.1 = ((bf16[16,9,128]{2,1,0:T(8,128)(2,1)}), bf16[16,9,128]{2,1,0:T(8,128)(2,1)S(1)}, u32[]{:S(2)}, u32[]{:S(2)}) async-start(bf16[16,9,128]{2,1,0:T(8,128)(2,1)} %broadcast_in_dim.30), calls=%async_computation.1 | async-start | bytes 131072 | tf_op jit(solution)/shard_map/all_to_all | solution.py:303
  79.8 24.8 %collective-permute-start.8 = (bf16[512,128]{1,0:T(8,128)(2,1)S(1)}, bf16[512,128]{1,0:T(8,128)(2,1)S(1)}, u32[]{:S(2)}, u32[]{:S(2)}) collective-permute-start(bf16[512,128]{1,0:T(8,128)(2,1)S(1)} %fusion), channel_id=1, source_target_pairs={{0,28},{1,29},{2,30},{3,31},{4,0},{5,1},{6,2},{7,3},{8,4},{9,5},{1... | collective-permute-start | bytes 393224 | tf_op jit(solution)/shard_map/ppermute | solution.py:321
  88.2 15.1 %all-to-all-start.2 = ((bf16[32,9,128]{2,1,0:T(8,128)(2,1)}), bf16[32,9,128]{2,1,0:T(8,128)(2,1)S(1)}, u32[]{:S(2)}, u32[]{:S(2)}) async-start(bf16[32,9,128]{2,1,0:T(8,128)(2,1)} %broadcast_in_dim.31), calls=%async_computation.2 | async-start | bytes 262144 | tf_op jit(solution)/shard_map/all_to_all | solution.py:303
  94.0 10.6 %collective-permute-start.7 = (bf16[2,512,128]{2,1,0:T(8,128)(2,1)S(1)}, bf16[2,512,128]{2,1,0:T(8,128)(2,1)S(1)}, u32[]{:S(2)}, u32[]{:S(2)}) collective-permute-start(bf16[2,512,128]{2,1,0:T(8,128)(2,1)S(1)} %pad_maximum_fusion.1), channel_id=1, source_target_pairs={{2,0},{3,1},{6,4},{7,5},{10,8},{11,9},{14,12},{15,13},{18,16},{19,... | collective-permute-start | bytes 786440 | tf_op jit(solution)/shard_map/ppermute | solution.py:321

commit v6 on v5

--- a/solution.py
+++ b/solution.py
@@ -17,7 +17,10 @@
 PER_GROUP = QUERY_HEADS_HALF // KEY_VALUE_HEADS
 RANK = 8
 PACK_ROWS = 4 * TOK_DEV + 16
-TERM_ROWS = 16
+PEERS = 16
+TERM_ROWS = 32
+TERM_HEADS = QUERY_HEADS_HALF // PEERS
+TERM_USED = TERM_HEADS * (RANK + 1)
 ADAPTER_SCALE = 2.0
 SCORE_SCALE = 1.0 / math.sqrt(HEAD_WIDTH)
 EXP2_SCALE = SCORE_SCALE * math.log2(math.e)
@@ -159,10 +162,11 @@
             )
             * ADAPTER_SCALE
         )
-        blank = jnp.zeros((TERM_ROWS - RANK - 1, HEAD_WIDTH), jnp.float32)
-        for h in range(PER_GROUP):
-            block = jnp.concatenate([parts[h], value_part[h : h + 1], blank], axis=0)
-            term_ref[h] = block.astype(jnp.bfloat16)
+        blank = jnp.zeros((TERM_ROWS - TERM_USED, HEAD_WIDTH), jnp.float32)
+        for i in range(PER_GROUP // TERM_HEADS):
+            these = slice(i * TERM_HEADS, (i + 1) * TERM_HEADS)
+            block = jnp.concatenate([*parts[these], value_part[these], blank], axis=0)
+            term_ref[i] = block.astype(jnp.bfloat16)
 
         def store(ref, j, span):
             for grad_ref, to_rows in ((dk_ref, k_rows), (dv_ref, v_rows)):
@@ -202,7 +206,7 @@
         return head_of(f, t[2 + place], s)
 
     columns = pl.BlockSpec((tok, wide), lambda s, f, t: (0, head(f, t, s)))
-    terms = pl.BlockSpec((PER_GROUP, TERM_ROWS, HEAD_WIDTH), lambda s, f, t: (head(f, t, s), 0, 0))
+    terms = pl.BlockSpec((PER_GROUP // TERM_HEADS, TERM_ROWS, HEAD_WIDTH), lambda s, f, t: (head(f, t, s), 0, 0))
     table_spec = whole((tok, HEAD_WIDTH))
     stacked = pl.BlockSpec((wide, HEAD_WIDTH), lambda s, f, t: (s, 0))
     in_specs = [stacked, stacked]
@@ -223,7 +227,7 @@
             in_specs.append(pl.BlockSpec(memory_space=pl.ANY))
     out_shape = [
         jax.ShapeDtypeStruct((tok, QUERY_HEADS_HALF * HEAD_WIDTH), jnp.bfloat16),
-        jax.ShapeDtypeStruct((QUERY_HEADS_HALF, TERM_ROWS, HEAD_WIDTH), jnp.bfloat16),
+        jax.ShapeDtypeStruct((PEERS, TERM_ROWS, HEAD_WIDTH), jnp.bfloat16),
         jax.ShapeDtypeStruct((chunks, 4 * tok, HEAD_WIDTH), jnp.float32),
         jax.ShapeDtypeStruct((6 if heavy else 2, 4 * tok, HEAD_WIDTH), jnp.bfloat16),
     ]
@@ -295,6 +299,9 @@
         ),
         out_shape=[shape, shape],
         compiler_params=pltpu.CompilerParams(vmem_limit_bytes=VMEM_LIMIT),
+        cost_estimate=pl.CostEstimate(
+            flops=20_000_000_000, bytes_accessed=64 << 20, transcendentals=0
+        ),
         name="finish_keys_values",
     )(flags, table, cosine, sine, light_keep, heavy_keep, pair_from, pair_from, side_back, cross_back)
 
@@ -370,7 +377,7 @@
     def sent(array):
         return array.astype(jnp.bfloat16)
 
-    terms = exchange(terms, SUM_AXES)
+    terms = exchange(terms, "zc")
     pair_from = send(pair_send, flip(1))
     swap_from = send(sent(heavy_keep[2] + wide(pair_from[4])), flip(2))
     terms, pair_from, swap_from = lax.optimization_barrier((terms, pair_from, swap_from))
@@ -381,13 +388,13 @@
         sent(jnp.stack([light_keep[1] + wide(pair_from[1]), heavy_keep[3] + wide(pair_from[5])])),
         to_even,
     )
-    terms = to_all(add_up(terms)[: RANK + 1], "zc")
+    terms = to_all(add_up(terms)[:TERM_USED], SUM_AXES)
     gk, gv = finish(
         shift_flags, table, cosine, sine, light_keep, heavy_keep, pair_from, side_back, cross_back
     )
-    terms = to_all(add_up(terms), SUM_AXES)
-    query_terms = terms[:, :RANK]
-    value_terms = terms[:, RANK].reshape(KEY_VALUE_HEADS, RANK, HEAD_WIDTH)
+    terms = to_all(add_up(terms), "zc")
+    query_terms = terms[:, : TERM_HEADS * RANK].reshape(QUERY_HEADS_HALF, RANK, HEAD_WIDTH)
+    value_terms = terms[:, TERM_HEADS * RANK :].reshape(KEY_VALUE_HEADS, RANK, HEAD_WIDTH)
 
     def rank_rows(heads):
         return wide(jnp.transpose(heads, (1, 0, 2)).reshape(RANK, -1))
@@ -397,7 +404,7 @@
 
 def solution(mesh):
     dp, ctx = mesh.shape["dp"], mesh.shape["ctx"]
-    split = Mesh(mesh.devices.reshape(dp, 2, ctx // 2), ("dp", "yh", "zc"))
+    split = Mesh(mesh.devices.reshape(dp, ctx // PEERS, PEERS), ("dp", "yh", "zc"))
     rows = P("dp", SEQ_AXES, None)
     return jax.shard_map(
         local,

time: 107 us -> 106 us (level)
  starting transfers between devices: 61.1 us -> 59 us
  waiting for transfers between devices: 20 us -> 21.7 us
    all_to_all x3, waiting for transfers between devices: 12.4 us -> 14.3 us  [exchange(): return lax.all_to_all(array, axes, 0, 0)]
    ppermute x9, starting transfers between devices: 36.9 us -> 35.2 us  [send(): return lax.ppermute(array, SEQ_AXES, pairs)]
  transfers between devices with their start and end apart: 12 -> 12, of which waited for: 5 -> 4; matrix products, arithmetic and copies ran while one was open for 2% -> 1% of each run, Pallas kernels for 5% -> 6%
where the time goes in v6:
time: 106 us; the launch traced here: 105 us
  starting transfers between devices  59 us (56%)
  waiting for transfers between devices  21.7 us (20%)
  Pallas kernels  16.6 us (16%)
  local copies, waits for them, and re-layouts  4.48 us (4%)
  other arithmetic  2.6 us (2%)
    ppermute x9, starting transfers between devices, send(): return lax.ppermute(array, SEQ_AXES, pairs)  35.2 us
    all_to_all x3, starting transfers between devices, exchange(): return lax.all_to_all(array, axes, 0, 0)  23.9 us
    all_to_all x3, waiting for transfers between devices, exchange(): return lax.all_to_all(array, axes, 0, 0)  14.3 us
    pallas_call x2, Pallas kernels, attention(): pl.pallas_call(partial(attention_kernel, heavy), grid_spec=pltpu.Prefetch...  12.3 us
    ppermute x9, waiting for transfers between devices, send(): return lax.ppermute(array, SEQ_AXES, pairs)  7.4 us
    unnamed x12, local copies, waits for them, and re-layouts  3.11 us
  transfers between devices with their start and end apart: 12, of which 4 were waited for; matrix products, arithmetic and copies ran while one was open for 1% of the time, Pallas kernels for 6%

profile of v6, /device:TPU:1, one launch (start us, length us, event | category | flops | bytes accessed | tf_op | source)
XLA Modules:
  0.0 105.4 jit_solution(1895444072150114591)
XLA Ops:
  1.3 1.8 %pack_heads.1 = (bf16[2,528,128]{2,1,0:T(8,128)(2,1)}, bf16[528,128]{1,0:T(8,128)(2,1)}) custom-call(s32[4]{0:T(128)} %flags_ref.9, s32[4]{0:T(128)} %pad_add_fusion.table_ref, bf16[128,512]{1,0:T(8,128)(2,1)} %bitcast.47, bf16[128,512]{1,0:T(8,128)(2,1)} %bitcast.48, bf16[8,128]{1,0:T(8,128)(2,1)} %bitcast.50), custom_call_target="tpu_custom_call" | custom-call | tf_op jit(solution)/shard_map/pack_heads/pallas_call | solution.py:65
  3.1 6.6 %collective-permute-start = (bf16[528,128]{1,0:T(8,128)(2,1)}, bf16[528,128]{1,0:T(8,128)(2,1)S(1)}, u32[]{:S(2)}, u32[]{:S(2)}) collective-permute-start(bf16[528,128]{1,0:T(8,128)(2,1)} %get-tuple-element.33), channel_id=1, source_target_pairs={{0,4},{1,5},{2,6},{3,7},{4,8},{5,9},{6,10},{7,11},{8,12},{9,13},{1... | collective-permute-start | bytes 405512 | tf_op jit(solution)/shard_map/ppermute | solution.py:328
  9.7 4.0 %collective-permute-start.1 = (bf16[2,528,128]{2,1,0:T(8,128)(2,1)}, bf16[2,528,128]{2,1,0:T(8,128)(2,1)S(1)}, u32[]{:S(2)}, u32[]{:S(2)}) collective-permute-start(bf16[2,528,128]{2,1,0:T(8,128)(2,1)} %get-tuple-element.34.refs_0_), channel_id=1, source_target_pairs={{0,2},{1,3},{4,6},{5,7},{8,10},{9,11},{12,14},{13,15},{16,18},{17,... | collective-permute-start | bytes 811016 | tf_op jit(solution)/shard_map/ppermute | solution.py:328
  14.7 1.2 %copy-done = bf16[1,128,4096]{2,1,0:T(8,128)(2,1)S(1)} copy-done((bf16[1,128,4096]{2,1,0:T(8,128)(2,1)S(1)}, bf16[1,128,4096]{2,1,0:T(8,128)(2,1)}, u32[]{:S(2)}) %copy-start) | copy-done | bytes 1048600
  16.0 1.2 %copy-done.1 = bf16[1,128,4096]{2,1,0:T(8,128)(2,1)S(1)} copy-done((bf16[1,128,4096]{2,1,0:T(8,128)(2,1)S(1)}, bf16[1,128,4096]{2,1,0:T(8,128)(2,1)}, u32[]{:S(2)}) %copy-start.1) | copy-done | bytes 1048600
  17.2 1.1 %stage_rows.1 = (bf16[2048,128]{1,0:T(8,128)(2,1)S(1)}, bf16[2048,128]{1,0:T(8,128)(2,1)S(1)}, bf16[2048,128]{1,0:T(8,128)(2,1)S(1)}, bf16[2048,128]{1,0:T(8,128)(2,1)S(1)}) custom-call(s32[4]{0:T(128)S(1)} %copy-done.4, s32[4]{0:T(128)S(1)} %copy-done.3, bf16[128,4096]{1,0:T(8,128)(2,1)S(1)} %bitcast.38, bf16[128,4096]{1,0:T(8,128)(2,1)S(1)} %bitcast.39), custom_call_target="tpu_custom_call" | custom-call | tf_op jit(solution)/shard_map/stage_rows/pallas_call | solution.py:93
  18.4 7.4 %collective-permute-done = bf16[528,128]{1,0:T(8,128)(2,1)S(1)} collective-permute-done((bf16[528,128]{1,0:T(8,128)(2,1)}, bf16[528,128]{1,0:T(8,128)(2,1)S(1)}, u32[]{:S(2)}, u32[]{:S(2)}) %collective-permute-start) | collective-permute-done | bytes 135200 | tf_op jit(solution)/shard_map/ppermute | solution.py:328
  25.9 4.0 %collective-permute-start.3 = (bf16[5,528,128]{2,1,0:T(8,128)(2,1)S(1)}, bf16[5,528,128]{2,1,0:T(8,128)(2,1)S(1)}, u32[]{:S(2)}, u32[]{:S(2)}) collective-permute-start(bf16[5,528,128]{2,1,0:T(8,128)(2,1)S(1)} %pad_maximum_fusion), channel_id=1, source_target_pairs={{0,1},{1,0},{2,3},{3,2},{4,5},{5,4},{6,7},{7,6},{8,9},{9,8},{10,11... | collective-permute-start | bytes 2027528 | tf_op jit(solution)/shard_map/ppermute | solution.py:328
  29.9 2.7 %collective-permute-start.4 = (bf16[1,528,128]{2,1,0:T(8,128)(2,1)S(1)}, bf16[1,528,128]{2,1,0:T(8,128)(2,1)S(1)}, u32[]{:S(2)}, u32[]{:S(2)}) collective-permute-start(bf16[1,528,128]{2,1,0:T(8,128)(2,1)S(1)} %bitcast.41), channel_id=1, source_target_pairs={{0,3},{1,2},{2,1},{3,0},{4,7},{5,6},{6,5},{7,4},{8,11},{9,10},{10,... | collective-permute-start | bytes 405512 | tf_op jit(solution)/shard_map/ppermute | solution.py:328
  32.6 2.4 %collective-permute-start.2 = (bf16[1,528,128]{2,1,0:T(8,128)(2,1)S(1)}, bf16[1,528,128]{2,1,0:T(8,128)(2,1)S(1)}, u32[]{:S(2)}, u32[]{:S(2)}) collective-permute-start(bf16[1,528,128]{2,1,0:T(8,128)(2,1)S(1)} %bitcast.42), channel_id=1, source_target_pairs={{0,2},{1,3},{2,0},{3,1},{4,6},{5,7},{6,4},{7,5},{8,10},{9,11},{10,... | collective-permute-start | bytes 405512 | tf_op jit(solution)/shard_map/ppermute | solution.py:328
  35.1 4.2 %attention_light.1 = (bf16[128,4096]{1,0:T(8,128)(2,1)}, bf16[16,32,128]{2,1,0:T(8,128)(2,1)}, f32[2,512,128]{2,1,0:T(8,128)S(1)}, bf16[2,512,128]{2,1,0:T(8,128)(2,1)S(1)}) custom-call(s32[4]{0:T(128)S(1)} %copy-done.4, s32[4]{0:T(128)S(1)} %copy-done.3, bf16[2048,128]{1,0:T(8,128)(2,1)S(1)} %get-tuple-element.46.q_ref, ...), custom_call_target="tpu_custom_call" | custom-call | flops 1342177280 | bytes 6291456 | tf_op jit(solution)/shard_map/attention_light/pallas_call | solution.py:234
  39.3 8.1 %attention_heavy.1 = (bf16[128,4096]{1,0:T(8,128)(2,1)}, bf16[16,32,128]{2,1,0:T(8,128)(2,1)}, f32[4,512,128]{2,1,0:T(8,128)S(1)}, bf16[6,512,128]{2,1,0:T(8,128)(2,1)S(1)}) custom-call(s32[4]{0:T(128)S(1)} %copy-done.4, s32[4]{0:T(128)S(1)} %copy-done.3, ...), custom_call_target="tpu_custom_call", output_to_operand_aliasing={{0}: (16, {}), {1}: (17, {})} | custom-call | flops 2684354560 | bytes 6291456 | tf_op jit(solution)/shard_map/attention_heavy/pallas_call | solution.py:234
  47.4 3.1 %collective-permute-start.5 = (bf16[6,512,128]{2,1,0:T(8,128)(2,1)S(1)}, bf16[6,512,128]{2,1,0:T(8,128)(2,1)S(1)}, u32[]{:S(2)}, u32[]{:S(2)}) collective-permute-start(bf16[6,512,128]{2,1,0:T(8,128)(2,1)S(1)} %get-tuple-element.55), channel_id=1, source_target_pairs={{0,1},{1,0},{2,3},{3,2},{4,5},{5,4},{6,7},{7,6},{8,9},{9,8},{10,11... | collective-permute-start | bytes 2359304 | tf_op jit(solution)/shard_map/ppermute | solution.py:328
  50.5 9.2 %all-to-all-start = ((bf16[16,32,128]{2,1,0:T(8,128)(2,1)}), bf16[16,32,128]{2,1,0:T(8,128)(2,1)S(1)}, u32[]{:S(2)}, u32[]{:S(2)}) async-start(bf16[16,32,128]{2,1,0:T(8,128)(2,1)} %get-tuple-element.54), calls=%async_computation | async-start | bytes 262144 | tf_op jit(solution)/shard_map/all_to_all | solution.py:310
  59.7 3.3 %collective-permute-start.6 = (bf16[512,128]{1,0:T(8,128)(2,1)S(1)}, bf16[512,128]{1,0:T(8,128)(2,1)S(1)}, u32[]{:S(2)}, u32[]{:S(2)}) collective-permute-start(bf16[512,128]{1,0:T(8,128)(2,1)S(1)} %fusion.1), channel_id=1, source_target_pairs={{0,2},{1,3},{2,0},{3,1},{4,6},{5,7},{6,4},{7,5},{8,10},{9,11},{10,... | collective-permute-start | bytes 393224 | tf_op jit(solution)/shard_map/ppermute | solution.py:328
  63.1 5.9 %all-to-all-done = bf16[16,32,128]{2,1,0:T(8,128)(2,1)S(1)} async-done(((bf16[16,32,128]{2,1,0:T(8,128)(2,1)}), bf16[16,32,128]{2,1,0:T(8,128)(2,1)S(1)}, u32[]{:S(2)}, u32[]{:S(2)}) %all-to-all-start) | async-done | bytes 131104 | tf_op jit(solution)/shard_map/all_to_all | solution.py:310
  69.0 0.7 broadcast_in_dim.30
  69.7 7.8 %all-to-all-start.1 = ((bf16[32,18,128]{2,1,0:T(8,128)(2,1)}), bf16[32,18,128]{2,1,0:T(8,128)(2,1)S(1)}, u32[]{:S(2)}, u32[]{:S(2)}) async-start(bf16[32,18,128]{2,1,0:T(8,128)(2,1)} %broadcast_in_dim.30), calls=%async_computation.1 | async-start | bytes 393216 | tf_op jit(solution)/shard_map/all_to_all | solution.py:310
  77.6 1.3 %collective-permute-start.7 = (bf16[2,512,128]{2,1,0:T(8,128)(2,1)S(1)}, bf16[2,512,128]{2,1,0:T(8,128)(2,1)S(1)}, u32[]{:S(2)}, u32[]{:S(2)}) collective-permute-start(bf16[2,512,128]{2,1,0:T(8,128)(2,1)S(1)} %pad_maximum_fusion.1), channel_id=1, source_target_pairs={{2,0},{3,1},{6,4},{7,5},{10,8},{11,9},{14,12},{15,13},{18,16},{19,... | collective-permute-start | bytes 786440 | tf_op jit(solution)/shard_map/ppermute | solution.py:328
  79.0 7.7 %collective-permute-start.8 = (bf16[512,128]{1,0:T(8,128)(2,1)S(1)}, bf16[512,128]{1,0:T(8,128)(2,1)S(1)}, u32[]{:S(2)}, u32[]{:S(2)}) collective-permute-start(bf16[512,128]{1,0:T(8,128)(2,1)S(1)} %fusion), channel_id=1, source_target_pairs={{0,28},{1,29},{2,30},{3,31},{4,0},{5,1},{6,2},{7,3},{8,4},{9,5},{1... | collective-permute-start | bytes 393224 | tf_op jit(solution)/shard_map/ppermute | solution.py:328
  86.6 1.3 %all-to-all-done.1 = bf16[32,18,128]{2,1,0:T(8,128)(2,1)S(1)} async-done(((bf16[32,18,128]{2,1,0:T(8,128)(2,1)}), bf16[32,18,128]{2,1,0:T(8,128)(2,1)S(1)}, u32[]{:S(2)}, u32[]{:S(2)}) %all-to-all-start.1) | async-done | bytes 147488 | tf_op jit(solution)/shard_map/all_to_all | solution.py:310
  88.7 6.9 %all-to-all-start.2 = ((bf16[16,18,128]{2,1,0:T(8,128)(2,1)}), bf16[16,18,128]{2,1,0:T(8,128)(2,1)S(1)}, u32[]{:S(2)}, u32[]{:S(2)}) async-start(bf16[16,18,128]{2,1,0:T(8,128)(2,1)} %broadcast_in_dim.31), calls=%async_computation.2 | async-start | bytes 196608 | tf_op jit(solution)/shard_map/all_to_all | solution.py:310
  95.6 1.4 %finish_keys_values.1 = (bf16[128,512]{1,0:T(8,128)(2,1)}, bf16[128,512]{1,0:T(8,128)(2,1)}) custom-call(s32[4]{0:T(128)S(1)} %copy-done.4, s32[4]{0:T(128)S(1)} %copy-done.3, f32[128,128]{1,0:T(8,128)S(1)} %get-tuple-element.43.refs_4_.refs_8_.cos_ref, f32[128,128]{1,0:T(8,128)S(1)} %get-tuple-element.44.refs_5_.refs_9_.sin_ref, ...), custom_call_target="tpu_custom_call" | custom-call | flops 20000000000 | bytes 67108864 | tf_op jit(solution)/shard_map/finish_keys_values/pallas_call | solution.py:290
  97.0 7.1 %all-to-all-done.2 = bf16[16,18,128]{2,1,0:T(8,128)(2,1)S(1)} async-done(((bf16[16,18,128]{2,1,0:T(8,128)(2,1)}), bf16[16,18,128]{2,1,0:T(8,128)(2,1)S(1)}, u32[]{:S(2)}, u32[]{:S(2)}) %all-to-all-start.2) | async-done | bytes 73760 | tf_op jit(solution)/shard_map/all_to_all | solution.py:310
  (36 shorter events, 4.0 us)
Async XLA Ops:
  3.1 22.7 %collective-permute-start = (bf16[528,128]{1,0:T(8,128)(2,1)}, bf16[528,128]{1,0:T(8,128)(2,1)S(1)}, u32[]{:S(2)}, u32[]{:S(2)}) collective-permute-start(bf16[528,128]{1,0:T(8,128)(2,1)} %get-tuple-element.33), channel_id=1, source_target_pairs={{0,4},{1,5},{2,6},{3,7},{4,8},{5,9},{6,10},{7,11},{8,12},{9,13},{1... | collective-permute-start | bytes 405512 | tf_op jit(solution)/shard_map/ppermute | solution.py:328
  9.7 16.1 %collective-permute-start.1 = (bf16[2,528,128]{2,1,0:T(8,128)(2,1)}, bf16[2,528,128]{2,1,0:T(8,128)(2,1)S(1)}, u32[]{:S(2)}, u32[]{:S(2)}) collective-permute-start(bf16[2,528,128]{2,1,0:T(8,128)(2,1)} %get-tuple-element.34.refs_0_), channel_id=1, source_target_pairs={{0,2},{1,3},{4,6},{5,7},{8,10},{9,11},{12,14},{13,15},{16,18},{17,... | collective-permute-start | bytes 811016 | tf_op jit(solution)/shard_map/ppermute | solution.py:328
  14.1 0.6 copy-start.3
  14.1 0.7 copy-start.4
  14.7 1.2 %copy-start = (bf16[1,128,4096]{2,1,0:T(8,128)(2,1)S(1)}, bf16[1,128,4096]{2,1,0:T(8,128)(2,1)}, u32[]{:S(2)}) copy-start(bf16[1,128,4096]{2,1,0:T(8,128)(2,1)} %param.7) | copy-start | bytes 3145732
  16.0 1.2 %copy-start.1 = (bf16[1,128,4096]{2,1,0:T(8,128)(2,1)S(1)}, bf16[1,128,4096]{2,1,0:T(8,128)(2,1)}, u32[]{:S(2)}) copy-start(bf16[1,128,4096]{2,1,0:T(8,128)(2,1)} %param.10) | copy-start | bytes 3145732
  18.3 7.5 %copy-start.2 = (bf16[2,528,128]{2,1,0:T(8,128)(2,1)S(1)}, bf16[2,528,128]{2,1,0:T(8,128)(2,1)}, u32[]{:S(2)}) copy-start(bf16[2,528,128]{2,1,0:T(8,128)(2,1)} %get-tuple-element.34.refs_0_) | copy-start | bytes 811012
  25.8 9.3 %copy-start.5 = (bf16[1,128,8]{1,2,0:T(8,128)(2,1)S(1)}, bf16[1,128,8]{1,2,0:T(8,128)(2,1)}, u32[]{:S(2)}) copy-start(bf16[1,128,8]{1,2,0:T(8,128)(2,1)} %param.11) | copy-start | bytes 6148
  25.9 9.2 %collective-permute-start.3 = (bf16[5,528,128]{2,1,0:T(8,128)(2,1)S(1)}, bf16[5,528,128]{2,1,0:T(8,128)(2,1)S(1)}, u32[]{:S(2)}, u32[]{:S(2)}) collective-permute-start(bf16[5,528,128]{2,1,0:T(8,128)(2,1)S(1)} %pad_maximum_fusion), channel_id=1, source_target_pairs={{0,1},{1,0},{2,3},{3,2},{4,5},{5,4},{6,7},{7,6},{8,9},{9,8},{10,11... | collective-permute-start | bytes 2027528 | tf_op jit(solution)/shard_map/ppermute | solution.py:328
  29.9 9.4 %collective-permute-start.4 = (bf16[1,528,128]{2,1,0:T(8,128)(2,1)S(1)}, bf16[1,528,128]{2,1,0:T(8,128)(2,1)S(1)}, u32[]{:S(2)}, u32[]{:S(2)}) collective-permute-start(bf16[1,528,128]{2,1,0:T(8,128)(2,1)S(1)} %bitcast.41), channel_id=1, source_target_pairs={{0,3},{1,2},{2,1},{3,0},{4,7},{5,6},{6,5},{7,4},{8,11},{9,10},{10,... | collective-permute-start | bytes 405512 | tf_op jit(solution)/shard_map/ppermute | solution.py:328
  32.6 6.7 %collective-permute-start.2 = (bf16[1,528,128]{2,1,0:T(8,128)(2,1)S(1)}, bf16[1,528,128]{2,1,0:T(8,128)(2,1)S(1)}, u32[]{:S(2)}, u32[]{:S(2)}) collective-permute-start(bf16[1,528,128]{2,1,0:T(8,128)(2,1)S(1)} %bitcast.42), channel_id=1, source_target_pairs={{0,2},{1,3},{2,0},{3,1},{4,6},{5,7},{6,4},{7,5},{8,10},{9,11},{10,... | collective-permute-start | bytes 405512 | tf_op jit(solution)/shard_map/ppermute | solution.py:328
  47.4 12.3 %collective-permute-start.5 = (bf16[6,512,128]{2,1,0:T(8,128)(2,1)S(1)}, bf16[6,512,128]{2,1,0:T(8,128)(2,1)S(1)}, u32[]{:S(2)}, u32[]{:S(2)}) collective-permute-start(bf16[6,512,128]{2,1,0:T(8,128)(2,1)S(1)} %get-tuple-element.55), channel_id=1, source_target_pairs={{0,1},{1,0},{2,3},{3,2},{4,5},{5,4},{6,7},{7,6},{8,9},{9,8},{10,11... | collective-permute-start | bytes 2359304 | tf_op jit(solution)/shard_map/ppermute | solution.py:328
  50.5 18.5 %all-to-all-start = ((bf16[16,32,128]{2,1,0:T(8,128)(2,1)}), bf16[16,32,128]{2,1,0:T(8,128)(2,1)S(1)}, u32[]{:S(2)}, u32[]{:S(2)}) async-start(bf16[16,32,128]{2,1,0:T(8,128)(2,1)} %get-tuple-element.54), calls=%async_computation | async-start | bytes 262144 | tf_op jit(solution)/shard_map/all_to_all | solution.py:310
  59.7 9.2 %collective-permute-start.6 = (bf16[512,128]{1,0:T(8,128)(2,1)S(1)}, bf16[512,128]{1,0:T(8,128)(2,1)S(1)}, u32[]{:S(2)}, u32[]{:S(2)}) collective-permute-start(bf16[512,128]{1,0:T(8,128)(2,1)S(1)} %fusion.1), channel_id=1, source_target_pairs={{0,2},{1,3},{2,0},{3,1},{4,6},{5,7},{6,4},{7,5},{8,10},{9,11},{10,... | collective-permute-start | bytes 393224 | tf_op jit(solution)/shard_map/ppermute | solution.py:328
  69.7 18.2 %all-to-all-start.1 = ((bf16[32,18,128]{2,1,0:T(8,128)(2,1)}), bf16[32,18,128]{2,1,0:T(8,128)(2,1)S(1)}, u32[]{:S(2)}, u32[]{:S(2)}) async-start(bf16[32,18,128]{2,1,0:T(8,128)(2,1)} %broadcast_in_dim.30), calls=%async_computation.1 | async-start | bytes 393216 | tf_op jit(solution)/shard_map/all_to_all | solution.py:310
  77.6 18.0 %collective-permute-start.7 = (bf16[2,512,128]{2,1,0:T(8,128)(2,1)S(1)}, bf16[2,512,128]{2,1,0:T(8,128)(2,1)S(1)}, u32[]{:S(2)}, u32[]{:S(2)}) collective-permute-start(bf16[2,512,128]{2,1,0:T(8,128)(2,1)S(1)} %pad_maximum_fusion.1), channel_id=1, source_target_pairs={{2,0},{3,1},{6,4},{7,5},{10,8},{11,9},{14,12},{15,13},{18,16},{19,... | collective-permute-start | bytes 786440 | tf_op jit(solution)/shard_map/ppermute | solution.py:328
  79.0 16.6 %collective-permute-start.8 = (bf16[512,128]{1,0:T(8,128)(2,1)S(1)}, bf16[512,128]{1,0:T(8,128)(2,1)S(1)}, u32[]{:S(2)}, u32[]{:S(2)}) collective-permute-start(bf16[512,128]{1,0:T(8,128)(2,1)S(1)} %fusion), channel_id=1, source_target_pairs={{0,28},{1,29},{2,30},{3,31},{4,0},{5,1},{6,2},{7,3},{8,4},{9,5},{1... | collective-permute-start | bytes 393224 | tf_op jit(solution)/shard_map/ppermute | solution.py:328
  88.7 15.4 %all-to-all-start.2 = ((bf16[16,18,128]{2,1,0:T(8,128)(2,1)}), bf16[16,18,128]{2,1,0:T(8,128)(2,1)S(1)}, u32[]{:S(2)}, u32[]{:S(2)}) async-start(bf16[16,18,128]{2,1,0:T(8,128)(2,1)} %broadcast_in_dim.31), calls=%async_computation.2 | async-start | bytes 196608 | tf_op jit(solution)/shard_map/all_to_all | solution.py:310

commit v7 on v6

--- a/solution.py
+++ b/solution.py
@@ -43,11 +43,12 @@
     return pl.ds(pl.multiple_of(head * HEAD_WIDTH, HEAD_WIDTH), HEAD_WIDTH)
 
 
-def pack_kernel(flags_ref, table_ref, keys_ref, values_ref, low_ref, both_ref, light_ref):
+def pack_kernel(flags_ref, keys_ref, values_ref, low_ref, both_ref, light_ref):
+    light_half = lax.axis_index("zc") // 4 % 2
     low = low_ref[...].astype(jnp.float32)
     low = jnp.concatenate([low, jnp.zeros_like(low)], axis=0).astype(jnp.bfloat16)
     for place in range(2):
-        half = table_ref[2 + place]
+        half = 1 - light_half if place else light_half
         for sub in range(HALF_KV):
             columns = columns_of(head_of(flags_ref, half, sub))
             for kind, ref in enumerate((keys_ref, values_ref)):
@@ -59,7 +60,7 @@
     light_ref[4 * TOK_DEV :, :] = low
 
 
-def pack(flags, table, keys, values, low):
+def pack(flags, keys, values, low):
     whole = pl.BlockSpec(memory_space=pltpu.VMEM)
     scalars = pl.BlockSpec(memory_space=pltpu.SMEM)
     return pl.pallas_call(
@@ -68,10 +69,10 @@
             jax.ShapeDtypeStruct((2, PACK_ROWS, HEAD_WIDTH), jnp.bfloat16),
             jax.ShapeDtypeStruct((PACK_ROWS, HEAD_WIDTH), jnp.bfloat16),
         ),
-        in_specs=[scalars, scalars, whole, whole, whole],
+        in_specs=[scalars, whole, whole, whole],
         out_specs=(whole, whole),
         name="pack_heads",
-    )(flags, table, keys, values, low)
+    )(flags, keys, values, low)
 
 
 def stage_kernel(flags_ref, table_ref, query_ref, out_grad_ref, *outs):
@@ -340,7 +341,7 @@
     light_half = chip // 2 % 2
     table = jnp.stack([chip % 2, ctx_index % 2, light_half, 1 - light_half]).astype(jnp.int32)
 
-    both, light = pack(shift_flags, table, keys[0], values[0], value_lowrank_state[0].T)
+    both, light = pack(shift_flags, keys[0], values[0], value_lowrank_state[0].T)
     crossed = send(light, lambda i: i + GROUP_DEV // 2)
     sided = send(both, to_odd)
     half_dim = HEAD_WIDTH // 2

time: 106 us -> 105 us (level)
    unnamed x12 -> x10, local copies, waits for them, and re-layouts: 3.11 us -> 3.12 us
where the time goes in v7:
time: 105 us
  starting transfers between devices  59 us (56%)
  waiting for transfers between devices  21.6 us (21%)
  Pallas kernels  16.6 us (16%)
  local copies, waits for them, and re-layouts  4.49 us (4%)
  other arithmetic  2.1 us (2%)
    ppermute x9, starting transfers between devices, send(): return lax.ppermute(array, SEQ_AXES, pairs)  35.2 us
    all_to_all x3, starting transfers between devices, exchange(): return lax.all_to_all(array, axes, 0, 0)  23.9 us
    all_to_all x3, waiting for transfers between devices, exchange(): return lax.all_to_all(array, axes, 0, 0)  14.3 us
    pallas_call x2, Pallas kernels, attention(): pl.pallas_call(partial(attention_kernel, heavy), grid_spec=pltpu.Prefetch...  12.3 us
    ppermute x9, waiting for transfers between devices, send(): return lax.ppermute(array, SEQ_AXES, pairs)  7.26 us
    unnamed x10, local copies, waits for them, and re-layouts  3.12 us
  transfers between devices with their start and end apart: 12, of which 4 were waited for; matrix products, arithmetic and copies ran while one was open for 1% of the time, Pallas kernels for 6%

profile of v7, /device:TPU:1, one launch (start us, length us, event | category | flops | bytes accessed | tf_op | source)
XLA Modules:
  0.0 104.7 jit_solution(10585437050295897949)
XLA Ops:
  0.6 1.8 %pack_heads.1 = (bf16[2,528,128]{2,1,0:T(8,128)(2,1)}, bf16[528,128]{1,0:T(8,128)(2,1)}) custom-call(s32[4]{0:T(128)} %flags_ref.9, bf16[128,512]{1,0:T(8,128)(2,1)} %bitcast.47, bf16[128,512]{1,0:T(8,128)(2,1)} %bitcast.48, bf16[8,128]{1,0:T(8,128)(2,1)} %bitcast.50), custom_call_target="tpu_custom_call" | custom-call | tf_op jit(solution)/shard_map/pack_heads/pallas_call | solution.py:66
  2.4 6.6 %collective-permute-start = (bf16[528,128]{1,0:T(8,128)(2,1)}, bf16[528,128]{1,0:T(8,128)(2,1)S(1)}, u32[]{:S(2)}, u32[]{:S(2)}) collective-permute-start(bf16[528,128]{1,0:T(8,128)(2,1)} %get-tuple-element.33), channel_id=1, source_target_pairs={{0,4},{1,5},{2,6},{3,7},{4,8},{5,9},{6,10},{7,11},{8,12},{9,13},{1... | collective-permute-start | bytes 405512 | tf_op jit(solution)/shard_map/ppermute | solution.py:329
  9.1 4.0 %collective-permute-start.1 = (bf16[2,528,128]{2,1,0:T(8,128)(2,1)}, bf16[2,528,128]{2,1,0:T(8,128)(2,1)S(1)}, u32[]{:S(2)}, u32[]{:S(2)}) collective-permute-start(bf16[2,528,128]{2,1,0:T(8,128)(2,1)} %get-tuple-element.34.refs_0_), channel_id=1, source_target_pairs={{0,2},{1,3},{4,6},{5,7},{8,10},{9,11},{12,14},{13,15},{16,18},{17,... | collective-permute-start | bytes 811016 | tf_op jit(solution)/shard_map/ppermute | solution.py:329
  14.2 1.2 %copy-done = bf16[1,128,4096]{2,1,0:T(8,128)(2,1)S(1)} copy-done((bf16[1,128,4096]{2,1,0:T(8,128)(2,1)S(1)}, bf16[1,128,4096]{2,1,0:T(8,128)(2,1)}, u32[]{:S(2)}) %copy-start) | copy-done | bytes 1048600
  15.5 1.2 %copy-done.1 = bf16[1,128,4096]{2,1,0:T(8,128)(2,1)S(1)} copy-done((bf16[1,128,4096]{2,1,0:T(8,128)(2,1)S(1)}, bf16[1,128,4096]{2,1,0:T(8,128)(2,1)}, u32[]{:S(2)}) %copy-start.1) | copy-done | bytes 1048600
  16.7 1.1 %stage_rows.1 = (bf16[2048,128]{1,0:T(8,128)(2,1)S(1)}, bf16[2048,128]{1,0:T(8,128)(2,1)S(1)}, bf16[2048,128]{1,0:T(8,128)(2,1)S(1)}, bf16[2048,128]{1,0:T(8,128)(2,1)S(1)}) custom-call(s32[4]{0:T(128)S(1)} %copy-done.3, s32[4]{0:T(128)S(1)} %pad_add_fusion.table_ref, bf16[128,4096]{1,0:T(8,128)(2,1)S(1)} %bitcast.38, bf16[128,4096]{1,0:T(8,128)(2,1)S(1)} %bitcast.39), custom_call_target="tpu_custom_call" | custom-call | tf_op jit(solution)/shard_map/stage_rows/pallas_call | solution.py:94
  17.9 7.2 %collective-permute-done = bf16[528,128]{1,0:T(8,128)(2,1)S(1)} collective-permute-done((bf16[528,128]{1,0:T(8,128)(2,1)}, bf16[528,128]{1,0:T(8,128)(2,1)S(1)}, u32[]{:S(2)}, u32[]{:S(2)}) %collective-permute-start) | collective-permute-done | bytes 135200 | tf_op jit(solution)/shard_map/ppermute | solution.py:329
  25.3 4.0 %collective-permute-start.3 = (bf16[5,528,128]{2,1,0:T(8,128)(2,1)S(1)}, bf16[5,528,128]{2,1,0:T(8,128)(2,1)S(1)}, u32[]{:S(2)}, u32[]{:S(2)}) collective-permute-start(bf16[5,528,128]{2,1,0:T(8,128)(2,1)S(1)} %pad_maximum_fusion), channel_id=1, source_target_pairs={{0,1},{1,0},{2,3},{3,2},{4,5},{5,4},{6,7},{7,6},{8,9},{9,8},{10,11... | collective-permute-start | bytes 2027528 | tf_op jit(solution)/shard_map/ppermute | solution.py:329
  29.2 2.7 %collective-permute-start.4 = (bf16[1,528,128]{2,1,0:T(8,128)(2,1)S(1)}, bf16[1,528,128]{2,1,0:T(8,128)(2,1)S(1)}, u32[]{:S(2)}, u32[]{:S(2)}) collective-permute-start(bf16[1,528,128]{2,1,0:T(8,128)(2,1)S(1)} %bitcast.41), channel_id=1, source_target_pairs={{0,3},{1,2},{2,1},{3,0},{4,7},{5,6},{6,5},{7,4},{8,11},{9,10},{10,... | collective-permute-start | bytes 405512 | tf_op jit(solution)/shard_map/ppermute | solution.py:329
  32.0 2.4 %collective-permute-start.2 = (bf16[1,528,128]{2,1,0:T(8,128)(2,1)S(1)}, bf16[1,528,128]{2,1,0:T(8,128)(2,1)S(1)}, u32[]{:S(2)}, u32[]{:S(2)}) collective-permute-start(bf16[1,528,128]{2,1,0:T(8,128)(2,1)S(1)} %bitcast.42), channel_id=1, source_target_pairs={{0,2},{1,3},{2,0},{3,1},{4,6},{5,7},{6,4},{7,5},{8,10},{9,11},{10,... | collective-permute-start | bytes 405512 | tf_op jit(solution)/shard_map/ppermute | solution.py:329
  34.4 4.2 %attention_light.1 = (bf16[128,4096]{1,0:T(8,128)(2,1)}, bf16[16,32,128]{2,1,0:T(8,128)(2,1)}, f32[2,512,128]{2,1,0:T(8,128)S(1)}, bf16[2,512,128]{2,1,0:T(8,128)(2,1)S(1)}) custom-call(s32[4]{0:T(128)S(1)} %copy-done.3, s32[4]{0:T(128)S(1)} %pad_add_fusion.table_ref, bf16[2048,128]{1,0:T(8,128)(2,1)S(1)} %get-tuple-element.46.q_ref, ...), custom_call_target="tpu_custom_call" | custom-call | flops 1342177280 | bytes 6291456 | tf_op jit(solution)/shard_map/attention_light/pallas_call | solution.py:235
  38.7 8.1 %attention_heavy.1 = (bf16[128,4096]{1,0:T(8,128)(2,1)}, bf16[16,32,128]{2,1,0:T(8,128)(2,1)}, f32[4,512,128]{2,1,0:T(8,128)S(1)}, bf16[6,512,128]{2,1,0:T(8,128)(2,1)S(1)}) custom-call(s32[4]{0:T(128)S(1)} %copy-done.3, s32[4]{0:T(128)S(1)} %pad_add_fusion.table_ref, ...), custom_call_target="tpu_custom_call", output_to_operand_aliasing={{0}: (16, {}), {1}: (17, {})} | custom-call | flops 2684354560 | bytes 6291456 | tf_op jit(solution)/shard_map/attention_heavy/pallas_call | solution.py:235
  46.7 3.1 %collective-permute-start.5 = (bf16[6,512,128]{2,1,0:T(8,128)(2,1)S(1)}, bf16[6,512,128]{2,1,0:T(8,128)(2,1)S(1)}, u32[]{:S(2)}, u32[]{:S(2)}) collective-permute-start(bf16[6,512,128]{2,1,0:T(8,128)(2,1)S(1)} %get-tuple-element.55), channel_id=1, source_target_pairs={{0,1},{1,0},{2,3},{3,2},{4,5},{5,4},{6,7},{7,6},{8,9},{9,8},{10,11... | collective-permute-start | bytes 2359304 | tf_op jit(solution)/shard_map/ppermute | solution.py:329
  49.9 9.2 %all-to-all-start = ((bf16[16,32,128]{2,1,0:T(8,128)(2,1)}), bf16[16,32,128]{2,1,0:T(8,128)(2,1)S(1)}, u32[]{:S(2)}, u32[]{:S(2)}) async-start(bf16[16,32,128]{2,1,0:T(8,128)(2,1)} %get-tuple-element.54), calls=%async_computation | async-start | bytes 262144 | tf_op jit(solution)/shard_map/all_to_all | solution.py:311
  59.1 3.3 %collective-permute-start.6 = (bf16[512,128]{1,0:T(8,128)(2,1)S(1)}, bf16[512,128]{1,0:T(8,128)(2,1)S(1)}, u32[]{:S(2)}, u32[]{:S(2)}) collective-permute-start(bf16[512,128]{1,0:T(8,128)(2,1)S(1)} %fusion.1), channel_id=1, source_target_pairs={{0,2},{1,3},{2,0},{3,1},{4,6},{5,7},{6,4},{7,5},{8,10},{9,11},{10,... | collective-permute-start | bytes 393224 | tf_op jit(solution)/shard_map/ppermute | solution.py:329
  62.4 5.9 %all-to-all-done = bf16[16,32,128]{2,1,0:T(8,128)(2,1)S(1)} async-done(((bf16[16,32,128]{2,1,0:T(8,128)(2,1)}), bf16[16,32,128]{2,1,0:T(8,128)(2,1)S(1)}, u32[]{:S(2)}, u32[]{:S(2)}) %all-to-all-start) | async-done | bytes 131104 | tf_op jit(solution)/shard_map/all_to_all | solution.py:311
  68.4 0.7 broadcast_in_dim.30
  69.1 7.7 %all-to-all-start.1 = ((bf16[32,18,128]{2,1,0:T(8,128)(2,1)}), bf16[32,18,128]{2,1,0:T(8,128)(2,1)S(1)}, u32[]{:S(2)}, u32[]{:S(2)}) async-start(bf16[32,18,128]{2,1,0:T(8,128)(2,1)} %broadcast_in_dim.30), calls=%async_computation.1 | async-start | bytes 393216 | tf_op jit(solution)/shard_map/all_to_all | solution.py:311
  77.0 1.3 %collective-permute-start.7 = (bf16[2,512,128]{2,1,0:T(8,128)(2,1)S(1)}, bf16[2,512,128]{2,1,0:T(8,128)(2,1)S(1)}, u32[]{:S(2)}, u32[]{:S(2)}) collective-permute-start(bf16[2,512,128]{2,1,0:T(8,128)(2,1)S(1)} %pad_maximum_fusion.1), channel_id=1, source_target_pairs={{2,0},{3,1},{6,4},{7,5},{10,8},{11,9},{14,12},{15,13},{18,16},{19,... | collective-permute-start | bytes 786440 | tf_op jit(solution)/shard_map/ppermute | solution.py:329
  78.3 7.7 %collective-permute-start.8 = (bf16[512,128]{1,0:T(8,128)(2,1)S(1)}, bf16[512,128]{1,0:T(8,128)(2,1)S(1)}, u32[]{:S(2)}, u32[]{:S(2)}) collective-permute-start(bf16[512,128]{1,0:T(8,128)(2,1)S(1)} %fusion), channel_id=1, source_target_pairs={{0,28},{1,29},{2,30},{3,31},{4,0},{5,1},{6,2},{7,3},{8,4},{9,5},{1... | collective-permute-start | bytes 393224 | tf_op jit(solution)/shard_map/ppermute | solution.py:329
  86.0 1.3 %all-to-all-done.1 = bf16[32,18,128]{2,1,0:T(8,128)(2,1)S(1)} async-done(((bf16[32,18,128]{2,1,0:T(8,128)(2,1)}), bf16[32,18,128]{2,1,0:T(8,128)(2,1)S(1)}, u32[]{:S(2)}, u32[]{:S(2)}) %all-to-all-start.1) | async-done | bytes 147488 | tf_op jit(solution)/shard_map/all_to_all | solution.py:311
  88.0 6.9 %all-to-all-start.2 = ((bf16[16,18,128]{2,1,0:T(8,128)(2,1)}), bf16[16,18,128]{2,1,0:T(8,128)(2,1)S(1)}, u32[]{:S(2)}, u32[]{:S(2)}) async-start(bf16[16,18,128]{2,1,0:T(8,128)(2,1)} %broadcast_in_dim.31), calls=%async_computation.2 | async-start | bytes 196608 | tf_op jit(solution)/shard_map/all_to_all | solution.py:311
  95.0 1.4 %finish_keys_values.1 = (bf16[128,512]{1,0:T(8,128)(2,1)}, bf16[128,512]{1,0:T(8,128)(2,1)}) custom-call(s32[4]{0:T(128)S(1)} %copy-done.3, s32[4]{0:T(128)S(1)} %pad_add_fusion.table_ref, f32[128,128]{1,0:T(8,128)S(1)} %get-tuple-element.43.refs_4_.refs_8_.cos_ref, f32[128,128]{1,0:T(8,128)S(1)} %get-tuple-element.44.refs_5_.refs_9_.sin_ref, ...), custom_call_target="tpu_custom_call" | custom-call | flops 20000000000 | bytes 67108864 | tf_op jit(solution)/shard_map/finish_keys_values/pallas_call | solution.py:291
  96.4 7.1 %all-to-all-done.2 = bf16[16,18,128]{2,1,0:T(8,128)(2,1)S(1)} async-done(((bf16[16,18,128]{2,1,0:T(8,128)(2,1)}), bf16[16,18,128]{2,1,0:T(8,128)(2,1)S(1)}, u32[]{:S(2)}, u32[]{:S(2)}) %all-to-all-start.2) | async-done | bytes 73760 | tf_op jit(solution)/shard_map/all_to_all | solution.py:311
  (34 shorter events, 3.5 us)
Async XLA Ops:
  2.4 22.7 %collective-permute-start = (bf16[528,128]{1,0:T(8,128)(2,1)}, bf16[528,128]{1,0:T(8,128)(2,1)S(1)}, u32[]{:S(2)}, u32[]{:S(2)}) collective-permute-start(bf16[528,128]{1,0:T(8,128)(2,1)} %get-tuple-element.33), channel_id=1, source_target_pairs={{0,4},{1,5},{2,6},{3,7},{4,8},{5,9},{6,10},{7,11},{8,12},{9,13},{1... | collective-permute-start | bytes 405512 | tf_op jit(solution)/shard_map/ppermute | solution.py:329
  9.1 16.1 %collective-permute-start.1 = (bf16[2,528,128]{2,1,0:T(8,128)(2,1)}, bf16[2,528,128]{2,1,0:T(8,128)(2,1)S(1)}, u32[]{:S(2)}, u32[]{:S(2)}) collective-permute-start(bf16[2,528,128]{2,1,0:T(8,128)(2,1)} %get-tuple-element.34.refs_0_), channel_id=1, source_target_pairs={{0,2},{1,3},{4,6},{5,7},{8,10},{9,11},{12,14},{13,15},{16,18},{17,... | collective-permute-start | bytes 811016 | tf_op jit(solution)/shard_map/ppermute | solution.py:329
  13.6 0.7 copy-start.3
  14.2 1.2 %copy-start = (bf16[1,128,4096]{2,1,0:T(8,128)(2,1)S(1)}, bf16[1,128,4096]{2,1,0:T(8,128)(2,1)}, u32[]{:S(2)}) copy-start(bf16[1,128,4096]{2,1,0:T(8,128)(2,1)} %param.7) | copy-start | bytes 3145732
  15.5 1.2 %copy-start.1 = (bf16[1,128,4096]{2,1,0:T(8,128)(2,1)S(1)}, bf16[1,128,4096]{2,1,0:T(8,128)(2,1)}, u32[]{:S(2)}) copy-start(bf16[1,128,4096]{2,1,0:T(8,128)(2,1)} %param.10) | copy-start | bytes 3145732
  17.8 7.4 %copy-start.2 = (bf16[2,528,128]{2,1,0:T(8,128)(2,1)S(1)}, bf16[2,528,128]{2,1,0:T(8,128)(2,1)}, u32[]{:S(2)}) copy-start(bf16[2,528,128]{2,1,0:T(8,128)(2,1)} %get-tuple-element.34.refs_0_) | copy-start | bytes 811012
  25.2 9.3 %copy-start.4 = (bf16[1,128,8]{1,2,0:T(8,128)(2,1)S(1)}, bf16[1,128,8]{1,2,0:T(8,128)(2,1)}, u32[]{:S(2)}) copy-start(bf16[1,128,8]{1,2,0:T(8,128)(2,1)} %param.11) | copy-start | bytes 6148
  25.3 9.2 %collective-permute-start.3 = (bf16[5,528,128]{2,1,0:T(8,128)(2,1)S(1)}, bf16[5,528,128]{2,1,0:T(8,128)(2,1)S(1)}, u32[]{:S(2)}, u32[]{:S(2)}) collective-permute-start(bf16[5,528,128]{2,1,0:T(8,128)(2,1)S(1)} %pad_maximum_fusion), channel_id=1, source_target_pairs={{0,1},{1,0},{2,3},{3,2},{4,5},{5,4},{6,7},{7,6},{8,9},{9,8},{10,11... | collective-permute-start | bytes 2027528 | tf_op jit(solution)/shard_map/ppermute | solution.py:329
  29.2 9.4 %collective-permute-start.4 = (bf16[1,528,128]{2,1,0:T(8,128)(2,1)S(1)}, bf16[1,528,128]{2,1,0:T(8,128)(2,1)S(1)}, u32[]{:S(2)}, u32[]{:S(2)}) collective-permute-start(bf16[1,528,128]{2,1,0:T(8,128)(2,1)S(1)} %bitcast.41), channel_id=1, source_target_pairs={{0,3},{1,2},{2,1},{3,0},{4,7},{5,6},{6,5},{7,4},{8,11},{9,10},{10,... | collective-permute-start | bytes 405512 | tf_op jit(solution)/shard_map/ppermute | solution.py:329
  32.0 6.7 %collective-permute-start.2 = (bf16[1,528,128]{2,1,0:T(8,128)(2,1)S(1)}, bf16[1,528,128]{2,1,0:T(8,128)(2,1)S(1)}, u32[]{:S(2)}, u32[]{:S(2)}) collective-permute-start(bf16[1,528,128]{2,1,0:T(8,128)(2,1)S(1)} %bitcast.42), channel_id=1, source_target_pairs={{0,2},{1,3},{2,0},{3,1},{4,6},{5,7},{6,4},{7,5},{8,10},{9,11},{10,... | collective-permute-start | bytes 405512 | tf_op jit(solution)/shard_map/ppermute | solution.py:329
  46.7 12.3 %collective-permute-start.5 = (bf16[6,512,128]{2,1,0:T(8,128)(2,1)S(1)}, bf16[6,512,128]{2,1,0:T(8,128)(2,1)S(1)}, u32[]{:S(2)}, u32[]{:S(2)}) collective-permute-start(bf16[6,512,128]{2,1,0:T(8,128)(2,1)S(1)} %get-tuple-element.55), channel_id=1, source_target_pairs={{0,1},{1,0},{2,3},{3,2},{4,5},{5,4},{6,7},{7,6},{8,9},{9,8},{10,11... | collective-permute-start | bytes 2359304 | tf_op jit(solution)/shard_map/ppermute | solution.py:329
  49.9 18.5 %all-to-all-start = ((bf16[16,32,128]{2,1,0:T(8,128)(2,1)}), bf16[16,32,128]{2,1,0:T(8,128)(2,1)S(1)}, u32[]{:S(2)}, u32[]{:S(2)}) async-start(bf16[16,32,128]{2,1,0:T(8,128)(2,1)} %get-tuple-element.54), calls=%async_computation | async-start | bytes 262144 | tf_op jit(solution)/shard_map/all_to_all | solution.py:311
  59.1 9.2 %collective-permute-start.6 = (bf16[512,128]{1,0:T(8,128)(2,1)S(1)}, bf16[512,128]{1,0:T(8,128)(2,1)S(1)}, u32[]{:S(2)}, u32[]{:S(2)}) collective-permute-start(bf16[512,128]{1,0:T(8,128)(2,1)S(1)} %fusion.1), channel_id=1, source_target_pairs={{0,2},{1,3},{2,0},{3,1},{4,6},{5,7},{6,4},{7,5},{8,10},{9,11},{10,... | collective-permute-start | bytes 393224 | tf_op jit(solution)/shard_map/ppermute | solution.py:329
  69.1 18.2 %all-to-all-start.1 = ((bf16[32,18,128]{2,1,0:T(8,128)(2,1)}), bf16[32,18,128]{2,1,0:T(8,128)(2,1)S(1)}, u32[]{:S(2)}, u32[]{:S(2)}) async-start(bf16[32,18,128]{2,1,0:T(8,128)(2,1)} %broadcast_in_dim.30), calls=%async_computation.1 | async-start | bytes 393216 | tf_op jit(solution)/shard_map/all_to_all | solution.py:311
  77.0 18.0 %collective-permute-start.7 = (bf16[2,512,128]{2,1,0:T(8,128)(2,1)S(1)}, bf16[2,512,128]{2,1,0:T(8,128)(2,1)S(1)}, u32[]{:S(2)}, u32[]{:S(2)}) collective-permute-start(bf16[2,512,128]{2,1,0:T(8,128)(2,1)S(1)} %pad_maximum_fusion.1), channel_id=1, source_target_pairs={{2,0},{3,1},{6,4},{7,5},{10,8},{11,9},{14,12},{15,13},{18,16},{19,... | collective-permute-start | bytes 786440 | tf_op jit(solution)/shard_map/ppermute | solution.py:329
  78.3 16.6 %collective-permute-start.8 = (bf16[512,128]{1,0:T(8,128)(2,1)S(1)}, bf16[512,128]{1,0:T(8,128)(2,1)S(1)}, u32[]{:S(2)}, u32[]{:S(2)}) collective-permute-start(bf16[512,128]{1,0:T(8,128)(2,1)S(1)} %fusion), channel_id=1, source_target_pairs={{0,28},{1,29},{2,30},{3,31},{4,0},{5,1},{6,2},{7,3},{8,4},{9,5},{1... | collective-permute-start | bytes 393224 | tf_op jit(solution)/shard_map/ppermute | solution.py:329
  88.0 15.4 %all-to-all-start.2 = ((bf16[16,18,128]{2,1,0:T(8,128)(2,1)}), bf16[16,18,128]{2,1,0:T(8,128)(2,1)S(1)}, u32[]{:S(2)}, u32[]{:S(2)}) async-start(bf16[16,18,128]{2,1,0:T(8,128)(2,1)} %broadcast_in_dim.31), calls=%async_computation.2 | async-start | bytes 196608 | tf_op jit(solution)/shard_map/all_to_all | solution.py:311

commit v8 on v7

--- a/solution.py
+++ b/solution.py
@@ -112,7 +112,8 @@
     sub = pl.program_id(0)
     odd, core = table_ref[0], table_ref[1]
     rows = 2 * TOK_DEV
-    wide = PER_GROUP * TOK_DEV
+    tiles = 1 if heavy else 2
+    part = PER_GROUP * TOK_DEV // tiles
     k_rows = pl.ds(pl.multiple_of(sub * TOK_DEV, TOK_DEV), TOK_DEV)
     v_rows = pl.ds(pl.multiple_of((2 + sub) * TOK_DEV, TOK_DEV), TOK_DEV)
 
@@ -124,27 +125,44 @@
                 v_all[span, :] = side[0, v_rows, :]
                 low_all[:, span] = side[0, 4 * TOK_DEV :, :]
         width = n * rows
-        key = lax.broadcasted_iota(jnp.int32, (rows, wide), 0)
-        row = lax.broadcasted_iota(jnp.int32, (rows, wide), 1) % TOK_DEV
+        key = lax.broadcasted_iota(jnp.int32, (rows, part), 0)
+        row = lax.broadcasted_iota(jnp.int32, (rows, part), 1) % TOK_DEV
         limit = jnp.where(core == 1, rows, 0)
         allowed = (key <= row) | ((key >= TOK_DEV) & (key < limit))
 
-        q = q_ref[...]
-        d = d_ref[...]
         k = k_all[:width, :]
-        s = lax.dot_general(k, q, NT, preferred_element_type=jnp.float32)
-        near = jnp.where(allowed, s[:rows], MASKED)
-        s = near if n == 1 else jnp.concatenate([near, s[rows:]], axis=0)
-        dp = lax.dot_general(v_all[:width, :], d, NT, preferred_element_type=jnp.float32)
-        top = jnp.max(s, axis=0, keepdims=True) * EXP2_SCALE
-        p = jnp.exp2(s * EXP2_SCALE - top)
-        inverse = 1.0 / jnp.sum(p, axis=0, keepdims=True)
-        delta = jnp.sum(p * dp, axis=0, keepdims=True) * inverse
-        p = p * inverse
-        ds = (p * (dp - delta)).astype(jnp.bfloat16)
-        dv_ref[:width, :] = jnp.dot(p.astype(jnp.bfloat16), d, preferred_element_type=jnp.float32)
-        dk_ref[:width, :] = jnp.dot(ds, q, preferred_element_type=jnp.float32)
-        dq = lax.dot_general(ds, k, TN, preferred_element_type=jnp.float32) * SCORE_SCALE
+        v = v_all[:width, :]
+
+        def products(t):
+            q, d = (ref[t * part : (t + 1) * part, :] for ref in (q_ref, d_ref))
+            s = lax.dot_general(k, q, NT, preferred_element_type=jnp.float32)
+            near = jnp.where(allowed, s[:rows], MASKED)
+            s = near if n == 1 else jnp.concatenate([near, s[rows:]], axis=0)
+            dp = lax.dot_general(v, d, NT, preferred_element_type=jnp.float32)
+            top = jnp.max(s, axis=0, keepdims=True) * EXP2_SCALE
+            p = jnp.exp2(s * EXP2_SCALE - top)
+            inverse = 1.0 / jnp.sum(p, axis=0, keepdims=True)
+            delta = jnp.sum(p * dp, axis=0, keepdims=True) * inverse
+            p = p * inverse
+            ds = (p * (dp - delta)).astype(jnp.bfloat16)
+            return q, d, p.astype(jnp.bfloat16), ds
+
+        dqs = []
+        ahead = products(0)
+        for t in range(tiles):
+            q, d, p, ds = ahead
+            if t + 1 < tiles:
+                ahead = products(t + 1)
+            dv = jnp.dot(p, d, preferred_element_type=jnp.float32)
+            dk = jnp.dot(ds, q, preferred_element_type=jnp.float32)
+            if t == 0:
+                dv_ref[:width, :] = dv
+                dk_ref[:width, :] = dk
+            else:
+                dv_ref[:width, :] += dv
+                dk_ref[:width, :] += dk
+            dqs.append(lax.dot_general(ds, k, TN, preferred_element_type=jnp.float32))
+        dq = jnp.concatenate(dqs, axis=0) * SCORE_SCALE
         low_rank = low_ref[...]
         parts = []
         for h in range(PER_GROUP):

time: 105 us -> 105 us (level)
  transfers between devices with their start and end apart: 12 -> 12, of which waited for: 4 -> 5; matrix products, arithmetic and copies ran while one was open for 1% -> 1% of each run, Pallas kernels for 6% -> 6%
where the time goes in v8:
time: 105 us; the launch traced here: 104 us
  starting transfers between devices  58.7 us (56%)
  waiting for transfers between devices  21.7 us (21%)
  Pallas kernels  16.5 us (16%)
  local copies, waits for them, and re-layouts  4.49 us (4%)
  other arithmetic  2.1 us (2%)
    ppermute x9, starting transfers between devices, send(): return lax.ppermute(array, SEQ_AXES, pairs)  35.2 us
    all_to_all x3, starting transfers between devices, exchange(): return lax.all_to_all(array, axes, 0, 0)  23.4 us
    all_to_all x3, waiting for transfers between devices, exchange(): return lax.all_to_all(array, axes, 0, 0)  14.3 us
    pallas_call x2, Pallas kernels, attention(): pl.pallas_call(partial(attention_kernel, heavy), grid_spec=pltpu.Prefetch...  12.2 us
    ppermute x9, waiting for transfers between devices, send(): return lax.ppermute(array, SEQ_AXES, pairs)  7.33 us
    unnamed x10, local copies, waits for them, and re-layouts  3.12 us
  transfers between devices with their start and end apart: 12, of which 5 were waited for; matrix products, arithmetic and copies ran while one was open for 1% of the time, Pallas kernels for 6%

profile of v8, /device:TPU:1, one launch (start us, length us, event | category | flops | bytes accessed | tf_op | source)
XLA Modules:
  0.0 104.3 jit_solution(533549326740114515)
XLA Ops:
  0.6 1.8 %pack_heads.1 = (bf16[2,528,128]{2,1,0:T(8,128)(2,1)}, bf16[528,128]{1,0:T(8,128)(2,1)}) custom-call(s32[4]{0:T(128)} %flags_ref.9, bf16[128,512]{1,0:T(8,128)(2,1)} %bitcast.47, bf16[128,512]{1,0:T(8,128)(2,1)} %bitcast.48, bf16[8,128]{1,0:T(8,128)(2,1)} %bitcast.50), custom_call_target="tpu_custom_call" | custom-call | tf_op jit(solution)/shard_map/pack_heads/pallas_call | solution.py:66
  2.4 6.6 %collective-permute-start = (bf16[528,128]{1,0:T(8,128)(2,1)}, bf16[528,128]{1,0:T(8,128)(2,1)S(1)}, u32[]{:S(2)}, u32[]{:S(2)}) collective-permute-start(bf16[528,128]{1,0:T(8,128)(2,1)} %get-tuple-element.33), channel_id=1, source_target_pairs={{0,4},{1,5},{2,6},{3,7},{4,8},{5,9},{6,10},{7,11},{8,12},{9,13},{1... | collective-permute-start | bytes 405512 | tf_op jit(solution)/shard_map/ppermute | solution.py:347
  9.1 4.0 %collective-permute-start.1 = (bf16[2,528,128]{2,1,0:T(8,128)(2,1)}, bf16[2,528,128]{2,1,0:T(8,128)(2,1)S(1)}, u32[]{:S(2)}, u32[]{:S(2)}) collective-permute-start(bf16[2,528,128]{2,1,0:T(8,128)(2,1)} %get-tuple-element.34.refs_0_), channel_id=1, source_target_pairs={{0,2},{1,3},{4,6},{5,7},{8,10},{9,11},{12,14},{13,15},{16,18},{17,... | collective-permute-start | bytes 811016 | tf_op jit(solution)/shard_map/ppermute | solution.py:347
  14.2 1.2 %copy-done = bf16[1,128,4096]{2,1,0:T(8,128)(2,1)S(1)} copy-done((bf16[1,128,4096]{2,1,0:T(8,128)(2,1)S(1)}, bf16[1,128,4096]{2,1,0:T(8,128)(2,1)}, u32[]{:S(2)}) %copy-start) | copy-done | bytes 1048600
  15.5 1.2 %copy-done.1 = bf16[1,128,4096]{2,1,0:T(8,128)(2,1)S(1)} copy-done((bf16[1,128,4096]{2,1,0:T(8,128)(2,1)S(1)}, bf16[1,128,4096]{2,1,0:T(8,128)(2,1)}, u32[]{:S(2)}) %copy-start.1) | copy-done | bytes 1048600
  16.7 1.1 %stage_rows.1 = (bf16[2048,128]{1,0:T(8,128)(2,1)S(1)}, bf16[2048,128]{1,0:T(8,128)(2,1)S(1)}, bf16[2048,128]{1,0:T(8,128)(2,1)S(1)}, bf16[2048,128]{1,0:T(8,128)(2,1)S(1)}) custom-call(s32[4]{0:T(128)S(1)} %copy-done.3, s32[4]{0:T(128)S(1)} %pad_add_fusion.table_ref, bf16[128,4096]{1,0:T(8,128)(2,1)S(1)} %bitcast.38, bf16[128,4096]{1,0:T(8,128)(2,1)S(1)} %bitcast.39), custom_call_target="tpu_custom_call" | custom-call | tf_op jit(solution)/shard_map/stage_rows/pallas_call | solution.py:94
  17.9 7.2 %collective-permute-done = bf16[528,128]{1,0:T(8,128)(2,1)S(1)} collective-permute-done((bf16[528,128]{1,0:T(8,128)(2,1)}, bf16[528,128]{1,0:T(8,128)(2,1)S(1)}, u32[]{:S(2)}, u32[]{:S(2)}) %collective-permute-start) | collective-permute-done | bytes 135200 | tf_op jit(solution)/shard_map/ppermute | solution.py:347
  25.3 4.0 %collective-permute-start.3 = (bf16[5,528,128]{2,1,0:T(8,128)(2,1)S(1)}, bf16[5,528,128]{2,1,0:T(8,128)(2,1)S(1)}, u32[]{:S(2)}, u32[]{:S(2)}) collective-permute-start(bf16[5,528,128]{2,1,0:T(8,128)(2,1)S(1)} %pad_maximum_fusion), channel_id=1, source_target_pairs={{0,1},{1,0},{2,3},{3,2},{4,5},{5,4},{6,7},{7,6},{8,9},{9,8},{10,11... | collective-permute-start | bytes 2027528 | tf_op jit(solution)/shard_map/ppermute | solution.py:347
  29.2 2.7 %collective-permute-start.4 = (bf16[1,528,128]{2,1,0:T(8,128)(2,1)S(1)}, bf16[1,528,128]{2,1,0:T(8,128)(2,1)S(1)}, u32[]{:S(2)}, u32[]{:S(2)}) collective-permute-start(bf16[1,528,128]{2,1,0:T(8,128)(2,1)S(1)} %bitcast.41), channel_id=1, source_target_pairs={{0,3},{1,2},{2,1},{3,0},{4,7},{5,6},{6,5},{7,4},{8,11},{9,10},{10,... | collective-permute-start | bytes 405512 | tf_op jit(solution)/shard_map/ppermute | solution.py:347
  32.0 2.4 %collective-permute-start.2 = (bf16[1,528,128]{2,1,0:T(8,128)(2,1)S(1)}, bf16[1,528,128]{2,1,0:T(8,128)(2,1)S(1)}, u32[]{:S(2)}, u32[]{:S(2)}) collective-permute-start(bf16[1,528,128]{2,1,0:T(8,128)(2,1)S(1)} %bitcast.42), channel_id=1, source_target_pairs={{0,2},{1,3},{2,0},{3,1},{4,6},{5,7},{6,4},{7,5},{8,10},{9,11},{10,... | collective-permute-start | bytes 405512 | tf_op jit(solution)/shard_map/ppermute | solution.py:347
  34.4 4.1 %attention_light.1 = (bf16[128,4096]{1,0:T(8,128)(2,1)}, bf16[16,32,128]{2,1,0:T(8,128)(2,1)}, f32[2,512,128]{2,1,0:T(8,128)S(1)}, bf16[2,512,128]{2,1,0:T(8,128)(2,1)S(1)}) custom-call(s32[4]{0:T(128)S(1)} %copy-done.3, s32[4]{0:T(128)S(1)} %pad_add_fusion.table_ref, bf16[2048,128]{1,0:T(8,128)(2,1)S(1)} %get-tuple-element.46.q_ref, ...), custom_call_target="tpu_custom_call" | custom-call | flops 1342177280 | bytes 6291456 | tf_op jit(solution)/shard_map/attention_light/pallas_call | solution.py:253
  38.6 8.1 %attention_heavy.1 = (bf16[128,4096]{1,0:T(8,128)(2,1)}, bf16[16,32,128]{2,1,0:T(8,128)(2,1)}, f32[4,512,128]{2,1,0:T(8,128)S(1)}, bf16[6,512,128]{2,1,0:T(8,128)(2,1)S(1)}) custom-call(s32[4]{0:T(128)S(1)} %copy-done.3, s32[4]{0:T(128)S(1)} %pad_add_fusion.table_ref, ...), custom_call_target="tpu_custom_call", output_to_operand_aliasing={{0}: (16, {}), {1}: (17, {})} | custom-call | flops 2684354560 | bytes 6291456 | tf_op jit(solution)/shard_map/attention_heavy/pallas_call | solution.py:253
  46.7 3.2 %collective-permute-start.5 = (bf16[6,512,128]{2,1,0:T(8,128)(2,1)S(1)}, bf16[6,512,128]{2,1,0:T(8,128)(2,1)S(1)}, u32[]{:S(2)}, u32[]{:S(2)}) collective-permute-start(bf16[6,512,128]{2,1,0:T(8,128)(2,1)S(1)} %get-tuple-element.55), channel_id=1, source_target_pairs={{0,1},{1,0},{2,3},{3,2},{4,5},{5,4},{6,7},{7,6},{8,9},{9,8},{10,11... | collective-permute-start | bytes 2359304 | tf_op jit(solution)/shard_map/ppermute | solution.py:347
  49.9 8.8 %all-to-all-start = ((bf16[16,32,128]{2,1,0:T(8,128)(2,1)}), bf16[16,32,128]{2,1,0:T(8,128)(2,1)S(1)}, u32[]{:S(2)}, u32[]{:S(2)}) async-start(bf16[16,32,128]{2,1,0:T(8,128)(2,1)} %get-tuple-element.54), calls=%async_computation | async-start | bytes 262144 | tf_op jit(solution)/shard_map/all_to_all | solution.py:329
  58.7 3.3 %collective-permute-start.6 = (bf16[512,128]{1,0:T(8,128)(2,1)S(1)}, bf16[512,128]{1,0:T(8,128)(2,1)S(1)}, u32[]{:S(2)}, u32[]{:S(2)}) collective-permute-start(bf16[512,128]{1,0:T(8,128)(2,1)S(1)} %fusion.1), channel_id=1, source_target_pairs={{0,2},{1,3},{2,0},{3,1},{4,6},{5,7},{6,4},{7,5},{8,10},{9,11},{10,... | collective-permute-start | bytes 393224 | tf_op jit(solution)/shard_map/ppermute | solution.py:347
  62.0 5.9 %all-to-all-done = bf16[16,32,128]{2,1,0:T(8,128)(2,1)S(1)} async-done(((bf16[16,32,128]{2,1,0:T(8,128)(2,1)}), bf16[16,32,128]{2,1,0:T(8,128)(2,1)S(1)}, u32[]{:S(2)}, u32[]{:S(2)}) %all-to-all-start) | async-done | bytes 131104 | tf_op jit(solution)/shard_map/all_to_all | solution.py:329
  68.0 0.7 broadcast_in_dim.30
  68.7 7.7 %all-to-all-start.1 = ((bf16[32,18,128]{2,1,0:T(8,128)(2,1)}), bf16[32,18,128]{2,1,0:T(8,128)(2,1)S(1)}, u32[]{:S(2)}, u32[]{:S(2)}) async-start(bf16[32,18,128]{2,1,0:T(8,128)(2,1)} %broadcast_in_dim.30), calls=%async_computation.1 | async-start | bytes 393216 | tf_op jit(solution)/shard_map/all_to_all | solution.py:329
  76.6 1.3 %collective-permute-start.7 = (bf16[2,512,128]{2,1,0:T(8,128)(2,1)S(1)}, bf16[2,512,128]{2,1,0:T(8,128)(2,1)S(1)}, u32[]{:S(2)}, u32[]{:S(2)}) collective-permute-start(bf16[2,512,128]{2,1,0:T(8,128)(2,1)S(1)} %pad_maximum_fusion.1), channel_id=1, source_target_pairs={{2,0},{3,1},{6,4},{7,5},{10,8},{11,9},{14,12},{15,13},{18,16},{19,... | collective-permute-start | bytes 786440 | tf_op jit(solution)/shard_map/ppermute | solution.py:347
  77.9 7.7 %collective-permute-start.8 = (bf16[512,128]{1,0:T(8,128)(2,1)S(1)}, bf16[512,128]{1,0:T(8,128)(2,1)S(1)}, u32[]{:S(2)}, u32[]{:S(2)}) collective-permute-start(bf16[512,128]{1,0:T(8,128)(2,1)S(1)} %fusion), channel_id=1, source_target_pairs={{0,28},{1,29},{2,30},{3,31},{4,0},{5,1},{6,2},{7,3},{8,4},{9,5},{1... | collective-permute-start | bytes 393224 | tf_op jit(solution)/shard_map/ppermute | solution.py:347
  85.6 1.3 %all-to-all-done.1 = bf16[32,18,128]{2,1,0:T(8,128)(2,1)S(1)} async-done(((bf16[32,18,128]{2,1,0:T(8,128)(2,1)}), bf16[32,18,128]{2,1,0:T(8,128)(2,1)S(1)}, u32[]{:S(2)}, u32[]{:S(2)}) %all-to-all-start.1) | async-done | bytes 147488 | tf_op jit(solution)/shard_map/all_to_all | solution.py:329
  87.6 6.9 %all-to-all-start.2 = ((bf16[16,18,128]{2,1,0:T(8,128)(2,1)}), bf16[16,18,128]{2,1,0:T(8,128)(2,1)S(1)}, u32[]{:S(2)}, u32[]{:S(2)}) async-start(bf16[16,18,128]{2,1,0:T(8,128)(2,1)} %broadcast_in_dim.31), calls=%async_computation.2 | async-start | bytes 196608 | tf_op jit(solution)/shard_map/all_to_all | solution.py:329
  94.6 1.4 %finish_keys_values.1 = (bf16[128,512]{1,0:T(8,128)(2,1)}, bf16[128,512]{1,0:T(8,128)(2,1)}) custom-call(s32[4]{0:T(128)S(1)} %copy-done.3, s32[4]{0:T(128)S(1)} %pad_add_fusion.table_ref, f32[128,128]{1,0:T(8,128)S(1)} %get-tuple-element.43.refs_4_.refs_8_.cos_ref, f32[128,128]{1,0:T(8,128)S(1)} %get-tuple-element.44.refs_5_.refs_9_.sin_ref, ...), custom_call_target="tpu_custom_call" | custom-call | flops 20000000000 | bytes 67108864 | tf_op jit(solution)/shard_map/finish_keys_values/pallas_call | solution.py:309
  96.0 7.1 %all-to-all-done.2 = bf16[16,18,128]{2,1,0:T(8,128)(2,1)S(1)} async-done(((bf16[16,18,128]{2,1,0:T(8,128)(2,1)}), bf16[16,18,128]{2,1,0:T(8,128)(2,1)S(1)}, u32[]{:S(2)}, u32[]{:S(2)}) %all-to-all-start.2) | async-done | bytes 73760 | tf_op jit(solution)/shard_map/all_to_all | solution.py:329
  (34 shorter events, 3.5 us)
Async XLA Ops:
  2.4 22.7 %collective-permute-start = (bf16[528,128]{1,0:T(8,128)(2,1)}, bf16[528,128]{1,0:T(8,128)(2,1)S(1)}, u32[]{:S(2)}, u32[]{:S(2)}) collective-permute-start(bf16[528,128]{1,0:T(8,128)(2,1)} %get-tuple-element.33), channel_id=1, source_target_pairs={{0,4},{1,5},{2,6},{3,7},{4,8},{5,9},{6,10},{7,11},{8,12},{9,13},{1... | collective-permute-start | bytes 405512 | tf_op jit(solution)/shard_map/ppermute | solution.py:347
  9.1 16.1 %collective-permute-start.1 = (bf16[2,528,128]{2,1,0:T(8,128)(2,1)}, bf16[2,528,128]{2,1,0:T(8,128)(2,1)S(1)}, u32[]{:S(2)}, u32[]{:S(2)}) collective-permute-start(bf16[2,528,128]{2,1,0:T(8,128)(2,1)} %get-tuple-element.34.refs_0_), channel_id=1, source_target_pairs={{0,2},{1,3},{4,6},{5,7},{8,10},{9,11},{12,14},{13,15},{16,18},{17,... | collective-permute-start | bytes 811016 | tf_op jit(solution)/shard_map/ppermute | solution.py:347
  13.6 0.7 copy-start.3
  14.2 1.2 %copy-start = (bf16[1,128,4096]{2,1,0:T(8,128)(2,1)S(1)}, bf16[1,128,4096]{2,1,0:T(8,128)(2,1)}, u32[]{:S(2)}) copy-start(bf16[1,128,4096]{2,1,0:T(8,128)(2,1)} %param.7) | copy-start | bytes 3145732
  15.5 1.2 %copy-start.1 = (bf16[1,128,4096]{2,1,0:T(8,128)(2,1)S(1)}, bf16[1,128,4096]{2,1,0:T(8,128)(2,1)}, u32[]{:S(2)}) copy-start(bf16[1,128,4096]{2,1,0:T(8,128)(2,1)} %param.10) | copy-start | bytes 3145732
  17.8 7.4 %copy-start.2 = (bf16[2,528,128]{2,1,0:T(8,128)(2,1)S(1)}, bf16[2,528,128]{2,1,0:T(8,128)(2,1)}, u32[]{:S(2)}) copy-start(bf16[2,528,128]{2,1,0:T(8,128)(2,1)} %get-tuple-element.34.refs_0_) | copy-start | bytes 811012
  25.2 9.3 %copy-start.4 = (bf16[1,128,8]{1,2,0:T(8,128)(2,1)S(1)}, bf16[1,128,8]{1,2,0:T(8,128)(2,1)}, u32[]{:S(2)}) copy-start(bf16[1,128,8]{1,2,0:T(8,128)(2,1)} %param.11) | copy-start | bytes 6148
  25.3 9.2 %collective-permute-start.3 = (bf16[5,528,128]{2,1,0:T(8,128)(2,1)S(1)}, bf16[5,528,128]{2,1,0:T(8,128)(2,1)S(1)}, u32[]{:S(2)}, u32[]{:S(2)}) collective-permute-start(bf16[5,528,128]{2,1,0:T(8,128)(2,1)S(1)} %pad_maximum_fusion), channel_id=1, source_target_pairs={{0,1},{1,0},{2,3},{3,2},{4,5},{5,4},{6,7},{7,6},{8,9},{9,8},{10,11... | collective-permute-start | bytes 2027528 | tf_op jit(solution)/shard_map/ppermute | solution.py:347
  29.2 9.3 %collective-permute-start.4 = (bf16[1,528,128]{2,1,0:T(8,128)(2,1)S(1)}, bf16[1,528,128]{2,1,0:T(8,128)(2,1)S(1)}, u32[]{:S(2)}, u32[]{:S(2)}) collective-permute-start(bf16[1,528,128]{2,1,0:T(8,128)(2,1)S(1)} %bitcast.41), channel_id=1, source_target_pairs={{0,3},{1,2},{2,1},{3,0},{4,7},{5,6},{6,5},{7,4},{8,11},{9,10},{10,... | collective-permute-start | bytes 405512 | tf_op jit(solution)/shard_map/ppermute | solution.py:347
  32.0 6.7 %collective-permute-start.2 = (bf16[1,528,128]{2,1,0:T(8,128)(2,1)S(1)}, bf16[1,528,128]{2,1,0:T(8,128)(2,1)S(1)}, u32[]{:S(2)}, u32[]{:S(2)}) collective-permute-start(bf16[1,528,128]{2,1,0:T(8,128)(2,1)S(1)} %bitcast.42), channel_id=1, source_target_pairs={{0,2},{1,3},{2,0},{3,1},{4,6},{5,7},{6,4},{7,5},{8,10},{9,11},{10,... | collective-permute-start | bytes 405512 | tf_op jit(solution)/shard_map/ppermute | solution.py:347
  46.7 12.0 %collective-permute-start.5 = (bf16[6,512,128]{2,1,0:T(8,128)(2,1)S(1)}, bf16[6,512,128]{2,1,0:T(8,128)(2,1)S(1)}, u32[]{:S(2)}, u32[]{:S(2)}) collective-permute-start(bf16[6,512,128]{2,1,0:T(8,128)(2,1)S(1)} %get-tuple-element.55), channel_id=1, source_target_pairs={{0,1},{1,0},{2,3},{3,2},{4,5},{5,4},{6,7},{7,6},{8,9},{9,8},{10,11... | collective-permute-start | bytes 2359304 | tf_op jit(solution)/shard_map/ppermute | solution.py:347
  49.9 18.1 %all-to-all-start = ((bf16[16,32,128]{2,1,0:T(8,128)(2,1)}), bf16[16,32,128]{2,1,0:T(8,128)(2,1)S(1)}, u32[]{:S(2)}, u32[]{:S(2)}) async-start(bf16[16,32,128]{2,1,0:T(8,128)(2,1)} %get-tuple-element.54), calls=%async_computation | async-start | bytes 262144 | tf_op jit(solution)/shard_map/all_to_all | solution.py:329
  58.7 9.2 %collective-permute-start.6 = (bf16[512,128]{1,0:T(8,128)(2,1)S(1)}, bf16[512,128]{1,0:T(8,128)(2,1)S(1)}, u32[]{:S(2)}, u32[]{:S(2)}) collective-permute-start(bf16[512,128]{1,0:T(8,128)(2,1)S(1)} %fusion.1), channel_id=1, source_target_pairs={{0,2},{1,3},{2,0},{3,1},{4,6},{5,7},{6,4},{7,5},{8,10},{9,11},{10,... | collective-permute-start | bytes 393224 | tf_op jit(solution)/shard_map/ppermute | solution.py:347
  68.7 18.2 %all-to-all-start.1 = ((bf16[32,18,128]{2,1,0:T(8,128)(2,1)}), bf16[32,18,128]{2,1,0:T(8,128)(2,1)S(1)}, u32[]{:S(2)}, u32[]{:S(2)}) async-start(bf16[32,18,128]{2,1,0:T(8,128)(2,1)} %broadcast_in_dim.30), calls=%async_computation.1 | async-start | bytes 393216 | tf_op jit(solution)/shard_map/all_to_all | solution.py:329
  76.6 18.0 %collective-permute-start.7 = (bf16[2,512,128]{2,1,0:T(8,128)(2,1)S(1)}, bf16[2,512,128]{2,1,0:T(8,128)(2,1)S(1)}, u32[]{:S(2)}, u32[]{:S(2)}) collective-permute-start(bf16[2,512,128]{2,1,0:T(8,128)(2,1)S(1)} %pad_maximum_fusion.1), channel_id=1, source_target_pairs={{2,0},{3,1},{6,4},{7,5},{10,8},{11,9},{14,12},{15,13},{18,16},{19,... | collective-permute-start | bytes 786440 | tf_op jit(solution)/shard_map/ppermute | solution.py:347
  77.9 16.6 %collective-permute-start.8 = (bf16[512,128]{1,0:T(8,128)(2,1)S(1)}, bf16[512,128]{1,0:T(8,128)(2,1)S(1)}, u32[]{:S(2)}, u32[]{:S(2)}) collective-permute-start(bf16[512,128]{1,0:T(8,128)(2,1)S(1)} %fusion), channel_id=1, source_target_pairs={{0,28},{1,29},{2,30},{3,31},{4,0},{5,1},{6,2},{7,3},{8,4},{9,5},{1... | collective-permute-start | bytes 393224 | tf_op jit(solution)/shard_map/ppermute | solution.py:347
  87.6 15.4 %all-to-all-start.2 = ((bf16[16,18,128]{2,1,0:T(8,128)(2,1)}), bf16[16,18,128]{2,1,0:T(8,128)(2,1)S(1)}, u32[]{:S(2)}, u32[]{:S(2)}) async-start(bf16[16,18,128]{2,1,0:T(8,128)(2,1)} %broadcast_in_dim.31), calls=%async_computation.2 | async-start | bytes 196608 | tf_op jit(solution)/shard_map/all_to_all | solution.py:329

commit v9 on v8

--- a/solution.py
+++ b/solution.py
@@ -32,8 +32,8 @@
 SUM_AXES = ("dp", "yh")
 
 
-def head_of(flags, half, sub):
-    hit = [flags[head] == half for head in range(KEY_VALUE_HEADS)]
+def head_of(flags, half, sub, first=0):
+    hit = [flags[first + head] == half for head in range(KEY_VALUE_HEADS)]
     low = jnp.where(hit[0], 0, jnp.where(hit[1], 1, 2))
     high = jnp.where(hit[3], 3, jnp.where(hit[2], 2, 1))
     return jnp.where(sub == 0, low, high)
@@ -75,10 +75,10 @@
     )(flags, keys, values, low)
 
 
-def stage_kernel(flags_ref, table_ref, query_ref, out_grad_ref, *outs):
+def stage_kernel(table_ref, query_ref, out_grad_ref, *outs):
     for place in range(2):
         for sub in range(HALF_KV):
-            head = head_of(flags_ref, table_ref[2 + place], sub)
+            head = head_of(table_ref, table_ref[2 + place], sub, 4)
             for h in range(PER_GROUP):
                 start = (sub * PER_GROUP + h) * TOK_DEV
                 for kind, ref in enumerate((query_ref, out_grad_ref)):
@@ -87,22 +87,22 @@
                     ]
 
 
-def stage(flags, table, query, out_grad):
+def stage(table, query, out_grad):
     whole = pl.BlockSpec(memory_space=pltpu.VMEM)
     scalars = pl.BlockSpec(memory_space=pltpu.SMEM)
     shape = jax.ShapeDtypeStruct((HALF_KV * PER_GROUP * TOK_DEV, HEAD_WIDTH), jnp.bfloat16)
     outs = pl.pallas_call(
         stage_kernel,
         out_shape=[shape] * 4,
-        in_specs=[scalars, scalars, whole, whole],
+        in_specs=[scalars, whole, whole],
         out_specs=[whole] * 4,
         compiler_params=pltpu.CompilerParams(vmem_limit_bytes=VMEM_LIMIT),
         name="stage_rows",
-    )(flags, table, query, out_grad)
+    )(table, query, out_grad)
     return outs[:2], outs[2:]
 
 
-def attention_kernel(heavy, flags_ref, table_ref, q_ref, d_ref, *refs):
+def attention_kernel(heavy, table_ref, q_ref, d_ref, *refs):
     chunks = 4 if heavy else 2
     mine, other = refs[:chunks], refs[chunks : 2 * chunks]
     cos_ref, sin_ref, low_ref = refs[2 * chunks : 2 * chunks + 3]
@@ -211,7 +211,7 @@
         pl.when(odd == more)(lambda n=base + more: branch(n))
 
 
-def attention(heavy, flags, table, rows, mine, other, cosine, sine, low, before):
+def attention(heavy, table, rows, mine, other, cosine, sine, low, before):
     tok = TOK_DEV
     wide = PER_GROUP * HEAD_WIDTH
     chunks = len(mine)
@@ -219,19 +219,19 @@
     place = 1 if heavy else 0
 
     def whole(shape):
-        return pl.BlockSpec(shape, lambda s, f, t: (0,) * len(shape))
-
-    def head(f, t, s):
-        return head_of(f, t[2 + place], s)
-
-    columns = pl.BlockSpec((tok, wide), lambda s, f, t: (0, head(f, t, s)))
-    terms = pl.BlockSpec((PER_GROUP // TERM_HEADS, TERM_ROWS, HEAD_WIDTH), lambda s, f, t: (head(f, t, s), 0, 0))
+        return pl.BlockSpec(shape, lambda s, t: (0,) * len(shape))
+
+    def head(t, s):
+        return head_of(t, t[2 + place], s, 4)
+
+    columns = pl.BlockSpec((tok, wide), lambda s, t: (0, head(t, s)))
+    terms = pl.BlockSpec((PER_GROUP // TERM_HEADS, TERM_ROWS, HEAD_WIDTH), lambda s, t: (head(t, s), 0, 0))
     table_spec = whole((tok, HEAD_WIDTH))
-    stacked = pl.BlockSpec((wide, HEAD_WIDTH), lambda s, f, t: (s, 0))
+    stacked = pl.BlockSpec((wide, HEAD_WIDTH), lambda s, t: (s, 0))
     in_specs = [stacked, stacked]
     for array, at in (*mine, *other):
         in_specs.append(
-            pl.BlockSpec((1, PACK_ROWS, HEAD_WIDTH), lambda s, f, t, at=at: (at, 0, 0))
+            pl.BlockSpec((1, PACK_ROWS, HEAD_WIDTH), lambda s, t, at=at: (at, 0, 0))
         )
     in_specs += [table_spec, table_spec, whole((RANK, tok))]
     operands = [*rows, *(array for array, at in (*mine, *other)), cosine, sine, low]
@@ -241,7 +241,7 @@
         operands.append(light_send)
         in_specs.append(whole(light_send.shape))
         for out, array in enumerate(before):
-            aliases[2 + len(operands)] = out
+            aliases[1 + len(operands)] = out
             operands.append(array)
             in_specs.append(pl.BlockSpec(memory_space=pl.ANY))
     out_shape = [
@@ -253,7 +253,7 @@
     return pl.pallas_call(
         partial(attention_kernel, heavy),
         grid_spec=pltpu.PrefetchScalarGridSpec(
-            num_scalar_prefetch=2,
+            num_scalar_prefetch=1,
             grid=(HALF_KV,),
             in_specs=in_specs,
             out_specs=[columns, terms] + [whole(o.shape) for o in out_shape[2:]],
@@ -276,10 +276,10 @@
             transcendentals=HALF_KV * wide * keys,
         ),
         name="attention_heavy" if heavy else "attention_light",
-    )(flags, table, *operands)
-
-
-def finish_kernel(flags_ref, table_ref, cos_ref, sin_ref, *refs):
+    )(table, *operands)
+
+
+def finish_kernel(table_ref, cos_ref, sin_ref, *refs):
     light_keep, heavy_keep, light_from, heavy_from, side_ref, cross_ref, gk_ref, gv_ref = refs
     for place, (keep_ref, from_ref) in enumerate(
         ((light_keep, light_from), (heavy_keep, heavy_from))
@@ -288,7 +288,7 @@
         if place == 0:
             total += cross_ref[...].astype(jnp.float32)
         for sub in range(HALF_KV):
-            columns = columns_of(head_of(flags_ref, table_ref[2 + place], sub))
+            columns = columns_of(head_of(table_ref, table_ref[2 + place], sub, 4))
             dk = total[sub * TOK_DEV : (sub + 1) * TOK_DEV] * SCORE_SCALE
             turned = dk * cos_ref[...] + pltpu.roll(dk, HEAD_WIDTH // 2, 1) * sin_ref[...]
             gk_ref[:, columns] = turned.astype(jnp.bfloat16)
@@ -296,20 +296,20 @@
             gv_ref[:, columns] = dv.astype(jnp.bfloat16)
 
 
-def finish(flags, table, cosine, sine, light_keep, heavy_keep, pair_from, side_back, cross_back):
+def finish(table, cosine, sine, light_keep, heavy_keep, pair_from, side_back, cross_back):
     tok = TOK_DEV
 
     def whole(shape):
-        return pl.BlockSpec(shape, lambda i, f, t: (0,) * len(shape))
+        return pl.BlockSpec(shape, lambda i, t: (0,) * len(shape))
 
     def block(at):
-        return pl.BlockSpec((1, 4 * tok, HEAD_WIDTH), lambda i, f, t: (at, 0, 0))
+        return pl.BlockSpec((1, 4 * tok, HEAD_WIDTH), lambda i, t: (at, 0, 0))
 
     shape = jax.ShapeDtypeStruct((tok, KEY_VALUE_HEADS * HEAD_WIDTH), jnp.bfloat16)
     return pl.pallas_call(
         finish_kernel,
         grid_spec=pltpu.PrefetchScalarGridSpec(
-            num_scalar_prefetch=2,
+            num_scalar_prefetch=1,
             grid=(1,),
             in_specs=[whole((tok, HEAD_WIDTH))] * 2
             + [block(0), block(0), block(0), block(2)]
@@ -322,7 +322,7 @@
             flops=20_000_000_000, bytes_accessed=64 << 20, transcendentals=0
         ),
         name="finish_keys_values",
-    )(flags, table, cosine, sine, light_keep, heavy_keep, pair_from, pair_from, side_back, cross_back)
+    )(table, cosine, sine, light_keep, heavy_keep, pair_from, pair_from, side_back, cross_back)
 
 
 def exchange(array, axes):
@@ -358,6 +358,7 @@
     chip = ctx_index // 2
     light_half = chip // 2 % 2
     table = jnp.stack([chip % 2, ctx_index % 2, light_half, 1 - light_half]).astype(jnp.int32)
+    table = jnp.concatenate([table, shift_flags])
 
     both, light = pack(shift_flags, keys[0], values[0], value_lowrank_state[0].T)
     crossed = send(light, lambda i: i + GROUP_DEV // 2)
@@ -370,7 +371,7 @@
     cosine = jnp.concatenate([cos_half, cos_half], axis=1)
     sine = jnp.concatenate([sin_half, -sin_half], axis=1)
     low = query_lowrank_state[0].T
-    light_rows, heavy_rows = stage(shift_flags, table, query[0], out_grad[0])
+    light_rows, heavy_rows = stage(table, query[0], out_grad[0])
     crossed, sided, cosine, sine, low, light_rows, heavy_rows = lax.optimization_barrier(
         (crossed, sided, cosine, sine, low, light_rows, heavy_rows)
     )
@@ -379,12 +380,12 @@
     arrived = send(jnp.concatenate([both, sided, crossed]), flip(1))
     swapped_other = send(crossed, flip(3))
     gq, terms, light_keep, light_send = attention(
-        False, shift_flags, table, light_rows,
+        False, table, light_rows,
         [(both, 0), (sided, 0)], [(arrived, 0), (arrived, 2)],
         cosine, sine, low, None,
     )
     gq, terms, heavy_keep, pair_send = attention(
-        True, shift_flags, table, heavy_rows,
+        True, table, heavy_rows,
         [(both, 1), (crossed, 0), (swapped, 0), (sided, 1)],
         [(arrived, 1), (arrived, 4), (swapped_other, 0), (arrived, 3)],
         cosine, sine, low, (gq, terms, light_send),
@@ -409,7 +410,7 @@
     )
     terms = to_all(add_up(terms)[:TERM_USED], SUM_AXES)
     gk, gv = finish(
-        shift_flags, table, cosine, sine, light_keep, heavy_keep, pair_from, side_back, cross_back
+        table, cosine, sine, light_keep, heavy_keep, pair_from, side_back, cross_back
     )
     terms = to_all(add_up(terms), "zc")
     query_terms = terms[:, : TERM_HEADS * RANK].reshape(QUERY_HEADS_HALF, RANK, HEAD_WIDTH)

time: 105 us -> 105 us (level)
  no operation moved by 1% of the time
where the time goes in v9:
time: 105 us; the launch traced here: 104 us
  starting transfers between devices  58.7 us (56%)
  waiting for transfers between devices  21.7 us (21%)
  Pallas kernels  16.5 us (16%)
  local copies, waits for them, and re-layouts  4.57 us (4%)
  other arithmetic  2.03 us (2%)
    ppermute x9, starting transfers between devices, send(): return lax.ppermute(array, SEQ_AXES, pairs)  35.2 us
    all_to_all x3, starting transfers between devices, exchange(): return lax.all_to_all(array, axes, 0, 0)  23.5 us
    all_to_all x3, waiting for transfers between devices, exchange(): return lax.all_to_all(array, axes, 0, 0)  14.3 us
    pallas_call x2, Pallas kernels, attention(): pl.pallas_call(partial(attention_kernel, heavy), grid_spec=pltpu.Prefetch...  12.2 us
    ppermute x9, waiting for transfers between devices, send(): return lax.ppermute(array, SEQ_AXES, pairs)  7.32 us
    unnamed x10, local copies, waits for them, and re-layouts  3.11 us
  transfers between devices with their start and end apart: 12, of which 5 were waited for; matrix products, arithmetic and copies ran while one was open for 1% of the time, Pallas kernels for 6%

profile of v9, /device:TPU:1, one launch (start us, length us, event | category | flops | bytes accessed | tf_op | source)
XLA Modules:
  0.0 104.4 jit_solution(12790973955370791875)
XLA Ops:
  0.6 1.8 %pack_heads.1 = (bf16[2,528,128]{2,1,0:T(8,128)(2,1)}, bf16[528,128]{1,0:T(8,128)(2,1)}) custom-call(s32[4]{0:T(128)} %flags_ref.1, bf16[128,512]{1,0:T(8,128)(2,1)} %bitcast.47, bf16[128,512]{1,0:T(8,128)(2,1)} %bitcast.48, bf16[8,128]{1,0:T(8,128)(2,1)} %bitcast.50), custom_call_target="tpu_custom_call" | custom-call | tf_op jit(solution)/shard_map/pack_heads/pallas_call | solution.py:66
  2.4 6.6 %collective-permute-start = (bf16[528,128]{1,0:T(8,128)(2,1)}, bf16[528,128]{1,0:T(8,128)(2,1)S(1)}, u32[]{:S(2)}, u32[]{:S(2)}) collective-permute-start(bf16[528,128]{1,0:T(8,128)(2,1)} %get-tuple-element.33), channel_id=1, source_target_pairs={{0,4},{1,5},{2,6},{3,7},{4,8},{5,9},{6,10},{7,11},{8,12},{9,13},{1... | collective-permute-start | bytes 405512 | tf_op jit(solution)/shard_map/ppermute | solution.py:347
  9.1 4.0 %collective-permute-start.1 = (bf16[2,528,128]{2,1,0:T(8,128)(2,1)}, bf16[2,528,128]{2,1,0:T(8,128)(2,1)S(1)}, u32[]{:S(2)}, u32[]{:S(2)}) collective-permute-start(bf16[2,528,128]{2,1,0:T(8,128)(2,1)} %get-tuple-element.34.refs_0_), channel_id=1, source_target_pairs={{0,2},{1,3},{4,6},{5,7},{8,10},{9,11},{12,14},{13,15},{16,18},{17,... | collective-permute-start | bytes 811016 | tf_op jit(solution)/shard_map/ppermute | solution.py:347
  14.3 1.2 %copy-done = bf16[1,128,4096]{2,1,0:T(8,128)(2,1)S(1)} copy-done((bf16[1,128,4096]{2,1,0:T(8,128)(2,1)S(1)}, bf16[1,128,4096]{2,1,0:T(8,128)(2,1)}, u32[]{:S(2)}) %copy-start) | copy-done | bytes 1048600
  15.5 1.2 %copy-done.1 = bf16[1,128,4096]{2,1,0:T(8,128)(2,1)S(1)} copy-done((bf16[1,128,4096]{2,1,0:T(8,128)(2,1)S(1)}, bf16[1,128,4096]{2,1,0:T(8,128)(2,1)}, u32[]{:S(2)}) %copy-start.1) | copy-done | bytes 1048600
  16.7 1.1 %stage_rows.1 = (bf16[2048,128]{1,0:T(8,128)(2,1)S(1)}, bf16[2048,128]{1,0:T(8,128)(2,1)S(1)}, bf16[2048,128]{1,0:T(8,128)(2,1)S(1)}, bf16[2048,128]{1,0:T(8,128)(2,1)S(1)}) custom-call(s32[8]{0:T(128)S(1)} %concatenate.12.table_ref, bf16[128,4096]{1,0:T(8,128)(2,1)S(1)} %bitcast.38, bf16[128,4096]{1,0:T(8,128)(2,1)S(1)} %bitcast.39), custom_call_target="tpu_custom_call" | custom-call | tf_op jit(solution)/shard_map/stage_rows/pallas_call | solution.py:94
  17.9 7.2 %collective-permute-done = bf16[528,128]{1,0:T(8,128)(2,1)S(1)} collective-permute-done((bf16[528,128]{1,0:T(8,128)(2,1)}, bf16[528,128]{1,0:T(8,128)(2,1)S(1)}, u32[]{:S(2)}, u32[]{:S(2)}) %collective-permute-start) | collective-permute-done | bytes 135200 | tf_op jit(solution)/shard_map/ppermute | solution.py:347
  25.3 4.0 %collective-permute-start.3 = (bf16[5,528,128]{2,1,0:T(8,128)(2,1)S(1)}, bf16[5,528,128]{2,1,0:T(8,128)(2,1)S(1)}, u32[]{:S(2)}, u32[]{:S(2)}) collective-permute-start(bf16[5,528,128]{2,1,0:T(8,128)(2,1)S(1)} %pad_maximum_fusion), channel_id=1, source_target_pairs={{0,1},{1,0},{2,3},{3,2},{4,5},{5,4},{6,7},{7,6},{8,9},{9,8},{10,11... | collective-permute-start | bytes 2027528 | tf_op jit(solution)/shard_map/ppermute | solution.py:347
  29.2 2.7 %collective-permute-start.4 = (bf16[1,528,128]{2,1,0:T(8,128)(2,1)S(1)}, bf16[1,528,128]{2,1,0:T(8,128)(2,1)S(1)}, u32[]{:S(2)}, u32[]{:S(2)}) collective-permute-start(bf16[1,528,128]{2,1,0:T(8,128)(2,1)S(1)} %bitcast.41), channel_id=1, source_target_pairs={{0,3},{1,2},{2,1},{3,0},{4,7},{5,6},{6,5},{7,4},{8,11},{9,10},{10,... | collective-permute-start | bytes 405512 | tf_op jit(solution)/shard_map/ppermute | solution.py:347
  32.0 2.4 %collective-permute-start.2 = (bf16[1,528,128]{2,1,0:T(8,128)(2,1)S(1)}, bf16[1,528,128]{2,1,0:T(8,128)(2,1)S(1)}, u32[]{:S(2)}, u32[]{:S(2)}) collective-permute-start(bf16[1,528,128]{2,1,0:T(8,128)(2,1)S(1)} %bitcast.42), channel_id=1, source_target_pairs={{0,2},{1,3},{2,0},{3,1},{4,6},{5,7},{6,4},{7,5},{8,10},{9,11},{10,... | collective-permute-start | bytes 405512 | tf_op jit(solution)/shard_map/ppermute | solution.py:347
  34.4 4.1 %attention_light.1 = (bf16[128,4096]{1,0:T(8,128)(2,1)}, bf16[16,32,128]{2,1,0:T(8,128)(2,1)}, f32[2,512,128]{2,1,0:T(8,128)S(1)}, bf16[2,512,128]{2,1,0:T(8,128)(2,1)S(1)}) custom-call(s32[8]{0:T(128)S(1)} %concatenate.12.table_ref, bf16[2048,128]{1,0:T(8,128)(2,1)S(1)} %get-tuple-element.46.q_ref, bf16[2048,128]{1,0:T(8,128)(2,1)S(1)} %get-tuple-element.47.d_ref, ...), custom_call_target="tpu_custom_call" | custom-call | flops 1342177280 | bytes 6291456 | tf_op jit(solution)/shard_map/attention_light/pallas_call | solution.py:253
  38.6 8.1 %attention_heavy.1 = (bf16[128,4096]{1,0:T(8,128)(2,1)}, bf16[16,32,128]{2,1,0:T(8,128)(2,1)}, f32[4,512,128]{2,1,0:T(8,128)S(1)}, bf16[6,512,128]{2,1,0:T(8,128)(2,1)S(1)}) custom-call(s32[8]{0:T(128)S(1)} %concatenate.12.table_ref, bf16[2048,128]{1,0:T(8,128)(2,1)S(1)} %get-tuple-element.39.q_ref, ...), custom_call_target="tpu_custom_call", output_to_operand_aliasing={{0}: (15, {}), {1}: (16, {})} | custom-call | flops 2684354560 | bytes 6291456 | tf_op jit(solution)/shard_map/attention_heavy/pallas_call | solution.py:253
  46.7 3.2 %collective-permute-start.5 = (bf16[6,512,128]{2,1,0:T(8,128)(2,1)S(1)}, bf16[6,512,128]{2,1,0:T(8,128)(2,1)S(1)}, u32[]{:S(2)}, u32[]{:S(2)}) collective-permute-start(bf16[6,512,128]{2,1,0:T(8,128)(2,1)S(1)} %get-tuple-element.55), channel_id=1, source_target_pairs={{0,1},{1,0},{2,3},{3,2},{4,5},{5,4},{6,7},{7,6},{8,9},{9,8},{10,11... | collective-permute-start | bytes 2359304 | tf_op jit(solution)/shard_map/ppermute | solution.py:347
  49.9 8.8 %all-to-all-start = ((bf16[16,32,128]{2,1,0:T(8,128)(2,1)}), bf16[16,32,128]{2,1,0:T(8,128)(2,1)S(1)}, u32[]{:S(2)}, u32[]{:S(2)}) async-start(bf16[16,32,128]{2,1,0:T(8,128)(2,1)} %get-tuple-element.54), calls=%async_computation | async-start | bytes 262144 | tf_op jit(solution)/shard_map/all_to_all | solution.py:329
  58.8 3.3 %collective-permute-start.6 = (bf16[512,128]{1,0:T(8,128)(2,1)S(1)}, bf16[512,128]{1,0:T(8,128)(2,1)S(1)}, u32[]{:S(2)}, u32[]{:S(2)}) collective-permute-start(bf16[512,128]{1,0:T(8,128)(2,1)S(1)} %fusion.1), channel_id=1, source_target_pairs={{0,2},{1,3},{2,0},{3,1},{4,6},{5,7},{6,4},{7,5},{8,10},{9,11},{10,... | collective-permute-start | bytes 393224 | tf_op jit(solution)/shard_map/ppermute | solution.py:347
  62.1 5.9 %all-to-all-done = bf16[16,32,128]{2,1,0:T(8,128)(2,1)S(1)} async-done(((bf16[16,32,128]{2,1,0:T(8,128)(2,1)}), bf16[16,32,128]{2,1,0:T(8,128)(2,1)S(1)}, u32[]{:S(2)}, u32[]{:S(2)}) %all-to-all-start) | async-done | bytes 131104 | tf_op jit(solution)/shard_map/all_to_all | solution.py:329
  68.0 0.7 broadcast_in_dim.30
  68.7 7.8 %all-to-all-start.1 = ((bf16[32,18,128]{2,1,0:T(8,128)(2,1)}), bf16[32,18,128]{2,1,0:T(8,128)(2,1)S(1)}, u32[]{:S(2)}, u32[]{:S(2)}) async-start(bf16[32,18,128]{2,1,0:T(8,128)(2,1)} %broadcast_in_dim.30), calls=%async_computation.1 | async-start | bytes 393216 | tf_op jit(solution)/shard_map/all_to_all | solution.py:329
  76.6 1.3 %collective-permute-start.7 = (bf16[2,512,128]{2,1,0:T(8,128)(2,1)S(1)}, bf16[2,512,128]{2,1,0:T(8,128)(2,1)S(1)}, u32[]{:S(2)}, u32[]{:S(2)}) collective-permute-start(bf16[2,512,128]{2,1,0:T(8,128)(2,1)S(1)} %pad_maximum_fusion.1), channel_id=1, source_target_pairs={{2,0},{3,1},{6,4},{7,5},{10,8},{11,9},{14,12},{15,13},{18,16},{19,... | collective-permute-start | bytes 786440 | tf_op jit(solution)/shard_map/ppermute | solution.py:347
  78.0 7.7 %collective-permute-start.8 = (bf16[512,128]{1,0:T(8,128)(2,1)S(1)}, bf16[512,128]{1,0:T(8,128)(2,1)S(1)}, u32[]{:S(2)}, u32[]{:S(2)}) collective-permute-start(bf16[512,128]{1,0:T(8,128)(2,1)S(1)} %fusion), channel_id=1, source_target_pairs={{0,28},{1,29},{2,30},{3,31},{4,0},{5,1},{6,2},{7,3},{8,4},{9,5},{1... | collective-permute-start | bytes 393224 | tf_op jit(solution)/shard_map/ppermute | solution.py:347
  85.7 1.3 %all-to-all-done.1 = bf16[32,18,128]{2,1,0:T(8,128)(2,1)S(1)} async-done(((bf16[32,18,128]{2,1,0:T(8,128)(2,1)}), bf16[32,18,128]{2,1,0:T(8,128)(2,1)S(1)}, u32[]{:S(2)}, u32[]{:S(2)}) %all-to-all-start.1) | async-done | bytes 147488 | tf_op jit(solution)/shard_map/all_to_all | solution.py:329
  87.7 6.9 %all-to-all-start.2 = ((bf16[16,18,128]{2,1,0:T(8,128)(2,1)}), bf16[16,18,128]{2,1,0:T(8,128)(2,1)S(1)}, u32[]{:S(2)}, u32[]{:S(2)}) async-start(bf16[16,18,128]{2,1,0:T(8,128)(2,1)} %broadcast_in_dim.31), calls=%async_computation.2 | async-start | bytes 196608 | tf_op jit(solution)/shard_map/all_to_all | solution.py:329
  94.6 1.4 %finish_keys_values.1 = (bf16[128,512]{1,0:T(8,128)(2,1)}, bf16[128,512]{1,0:T(8,128)(2,1)}) custom-call(s32[8]{0:T(128)S(1)} %concatenate.12.table_ref, f32[128,128]{1,0:T(8,128)S(1)} %get-tuple-element.43.refs_4_.refs_8_.cos_ref, f32[128,128]{1,0:T(8,128)S(1)} %get-tuple-element.44.refs_5_.refs_9_.sin_ref, f32[2,512,128]{2,1,0:T(8,128)S(1)} %get-tuple-element.52.refs_0_, ...), custom_call_target="tpu_custom_call" | custom-call | flops 20000000000 | bytes 67108864 | tf_op jit(solution)/shard_map/finish_keys_values/pallas_call | solution.py:309
  96.0 7.1 %all-to-all-done.2 = bf16[16,18,128]{2,1,0:T(8,128)(2,1)S(1)} async-done(((bf16[16,18,128]{2,1,0:T(8,128)(2,1)}), bf16[16,18,128]{2,1,0:T(8,128)(2,1)S(1)}, u32[]{:S(2)}, u32[]{:S(2)}) %all-to-all-start.2) | async-done | bytes 73760 | tf_op jit(solution)/shard_map/all_to_all | solution.py:329
  (34 shorter events, 3.5 us)
Async XLA Ops:
  2.4 22.7 %collective-permute-start = (bf16[528,128]{1,0:T(8,128)(2,1)}, bf16[528,128]{1,0:T(8,128)(2,1)S(1)}, u32[]{:S(2)}, u32[]{:S(2)}) collective-permute-start(bf16[528,128]{1,0:T(8,128)(2,1)} %get-tuple-element.33), channel_id=1, source_target_pairs={{0,4},{1,5},{2,6},{3,7},{4,8},{5,9},{6,10},{7,11},{8,12},{9,13},{1... | collective-permute-start | bytes 405512 | tf_op jit(solution)/shard_map/ppermute | solution.py:347
  9.1 16.1 %collective-permute-start.1 = (bf16[2,528,128]{2,1,0:T(8,128)(2,1)}, bf16[2,528,128]{2,1,0:T(8,128)(2,1)S(1)}, u32[]{:S(2)}, u32[]{:S(2)}) collective-permute-start(bf16[2,528,128]{2,1,0:T(8,128)(2,1)} %get-tuple-element.34.refs_0_), channel_id=1, source_target_pairs={{0,2},{1,3},{4,6},{5,7},{8,10},{9,11},{12,14},{13,15},{16,18},{17,... | collective-permute-start | bytes 811016 | tf_op jit(solution)/shard_map/ppermute | solution.py:347
  13.5 0.7 copy-start.4
  14.3 1.2 %copy-start = (bf16[1,128,4096]{2,1,0:T(8,128)(2,1)S(1)}, bf16[1,128,4096]{2,1,0:T(8,128)(2,1)}, u32[]{:S(2)}) copy-start(bf16[1,128,4096]{2,1,0:T(8,128)(2,1)} %param.7) | copy-start | bytes 3145732
  15.5 1.2 %copy-start.1 = (bf16[1,128,4096]{2,1,0:T(8,128)(2,1)S(1)}, bf16[1,128,4096]{2,1,0:T(8,128)(2,1)}, u32[]{:S(2)}) copy-start(bf16[1,128,4096]{2,1,0:T(8,128)(2,1)} %param.10) | copy-start | bytes 3145732
  17.8 7.4 %copy-start.2 = (bf16[2,528,128]{2,1,0:T(8,128)(2,1)S(1)}, bf16[2,528,128]{2,1,0:T(8,128)(2,1)}, u32[]{:S(2)}) copy-start(bf16[2,528,128]{2,1,0:T(8,128)(2,1)} %get-tuple-element.34.refs_0_) | copy-start | bytes 811012
  25.2 9.3 %copy-start.3 = (bf16[1,128,8]{1,2,0:T(8,128)(2,1)S(1)}, bf16[1,128,8]{1,2,0:T(8,128)(2,1)}, u32[]{:S(2)}) copy-start(bf16[1,128,8]{1,2,0:T(8,128)(2,1)} %param.11) | copy-start | bytes 6148
  25.3 9.2 %collective-permute-start.3 = (bf16[5,528,128]{2,1,0:T(8,128)(2,1)S(1)}, bf16[5,528,128]{2,1,0:T(8,128)(2,1)S(1)}, u32[]{:S(2)}, u32[]{:S(2)}) collective-permute-start(bf16[5,528,128]{2,1,0:T(8,128)(2,1)S(1)} %pad_maximum_fusion), channel_id=1, source_target_pairs={{0,1},{1,0},{2,3},{3,2},{4,5},{5,4},{6,7},{7,6},{8,9},{9,8},{10,11... | collective-permute-start | bytes 2027528 | tf_op jit(solution)/shard_map/ppermute | solution.py:347
  29.2 9.3 %collective-permute-start.4 = (bf16[1,528,128]{2,1,0:T(8,128)(2,1)S(1)}, bf16[1,528,128]{2,1,0:T(8,128)(2,1)S(1)}, u32[]{:S(2)}, u32[]{:S(2)}) collective-permute-start(bf16[1,528,128]{2,1,0:T(8,128)(2,1)S(1)} %bitcast.41), channel_id=1, source_target_pairs={{0,3},{1,2},{2,1},{3,0},{4,7},{5,6},{6,5},{7,4},{8,11},{9,10},{10,... | collective-permute-start | bytes 405512 | tf_op jit(solution)/shard_map/ppermute | solution.py:347
  32.0 6.7 %collective-permute-start.2 = (bf16[1,528,128]{2,1,0:T(8,128)(2,1)S(1)}, bf16[1,528,128]{2,1,0:T(8,128)(2,1)S(1)}, u32[]{:S(2)}, u32[]{:S(2)}) collective-permute-start(bf16[1,528,128]{2,1,0:T(8,128)(2,1)S(1)} %bitcast.42), channel_id=1, source_target_pairs={{0,2},{1,3},{2,0},{3,1},{4,6},{5,7},{6,4},{7,5},{8,10},{9,11},{10,... | collective-permute-start | bytes 405512 | tf_op jit(solution)/shard_map/ppermute | solution.py:347
  46.7 12.0 %collective-permute-start.5 = (bf16[6,512,128]{2,1,0:T(8,128)(2,1)S(1)}, bf16[6,512,128]{2,1,0:T(8,128)(2,1)S(1)}, u32[]{:S(2)}, u32[]{:S(2)}) collective-permute-start(bf16[6,512,128]{2,1,0:T(8,128)(2,1)S(1)} %get-tuple-element.55), channel_id=1, source_target_pairs={{0,1},{1,0},{2,3},{3,2},{4,5},{5,4},{6,7},{7,6},{8,9},{9,8},{10,11... | collective-permute-start | bytes 2359304 | tf_op jit(solution)/shard_map/ppermute | solution.py:347
  49.9 18.1 %all-to-all-start = ((bf16[16,32,128]{2,1,0:T(8,128)(2,1)}), bf16[16,32,128]{2,1,0:T(8,128)(2,1)S(1)}, u32[]{:S(2)}, u32[]{:S(2)}) async-start(bf16[16,32,128]{2,1,0:T(8,128)(2,1)} %get-tuple-element.54), calls=%async_computation | async-start | bytes 262144 | tf_op jit(solution)/shard_map/all_to_all | solution.py:329
  58.8 9.2 %collective-permute-start.6 = (bf16[512,128]{1,0:T(8,128)(2,1)S(1)}, bf16[512,128]{1,0:T(8,128)(2,1)S(1)}, u32[]{:S(2)}, u32[]{:S(2)}) collective-permute-start(bf16[512,128]{1,0:T(8,128)(2,1)S(1)} %fusion.1), channel_id=1, source_target_pairs={{0,2},{1,3},{2,0},{3,1},{4,6},{5,7},{6,4},{7,5},{8,10},{9,11},{10,... | collective-permute-start | bytes 393224 | tf_op jit(solution)/shard_map/ppermute | solution.py:347
  68.7 18.2 %all-to-all-start.1 = ((bf16[32,18,128]{2,1,0:T(8,128)(2,1)}), bf16[32,18,128]{2,1,0:T(8,128)(2,1)S(1)}, u32[]{:S(2)}, u32[]{:S(2)}) async-start(bf16[32,18,128]{2,1,0:T(8,128)(2,1)} %broadcast_in_dim.30), calls=%async_computation.1 | async-start | bytes 393216 | tf_op jit(solution)/shard_map/all_to_all | solution.py:329
  76.6 18.0 %collective-permute-start.7 = (bf16[2,512,128]{2,1,0:T(8,128)(2,1)S(1)}, bf16[2,512,128]{2,1,0:T(8,128)(2,1)S(1)}, u32[]{:S(2)}, u32[]{:S(2)}) collective-permute-start(bf16[2,512,128]{2,1,0:T(8,128)(2,1)S(1)} %pad_maximum_fusion.1), channel_id=1, source_target_pairs={{2,0},{3,1},{6,4},{7,5},{10,8},{11,9},{14,12},{15,13},{18,16},{19,... | collective-permute-start | bytes 786440 | tf_op jit(solution)/shard_map/ppermute | solution.py:347
  78.0 16.6 %collective-permute-start.8 = (bf16[512,128]{1,0:T(8,128)(2,1)S(1)}, bf16[512,128]{1,0:T(8,128)(2,1)S(1)}, u32[]{:S(2)}, u32[]{:S(2)}) collective-permute-start(bf16[512,128]{1,0:T(8,128)(2,1)S(1)} %fusion), channel_id=1, source_target_pairs={{0,28},{1,29},{2,30},{3,31},{4,0},{5,1},{6,2},{7,3},{8,4},{9,5},{1... | collective-permute-start | bytes 393224 | tf_op jit(solution)/shard_map/ppermute | solution.py:347
  87.7 15.4 %all-to-all-start.2 = ((bf16[16,18,128]{2,1,0:T(8,128)(2,1)}), bf16[16,18,128]{2,1,0:T(8,128)(2,1)S(1)}, u32[]{:S(2)}, u32[]{:S(2)}) async-start(bf16[16,18,128]{2,1,0:T(8,128)(2,1)} %broadcast_in_dim.31), calls=%async_computation.2 | async-start | bytes 196608 | tf_op jit(solution)/shard_map/all_to_all | solution.py:329
